TPU v7x, 32 devices: a whole 2x2x4 slice. The times are simulated.
32 devices in a mesh: mp: 4 (over x, core), dp: 8 (over z, y).
Axes of the slice: x: 2, y: 2, z: 4, core: 2. Of those that a mesh axis runs over, the one named last changes fastest.
Arguments:
- tokens: bfloat16 [2048, 2048], P('dp'), may hold values from -7 to 7
- cotangent: bfloat16 [2048, 2048], P('dp'), may hold values from -6 to 6
- token_sequence_index: int32 [2048], P('dp'), may hold values from 0 to 1, as said below
- positions: int32 [2048], P('dp'), may hold values from 0 to 1023, as said below
- token_exit_loop: int32 [2048], P('dp'), may hold values from 0 to 2
- current_loop: int32 [1], replicated, may hold values from 0 to 2
- attention_norm_gain: float32 [2048], replicated, may hold values from 0.1 to 1.9
- feedforward_norm_gain: float32 [2048], replicated, may hold values from 0.1 to 1.9
- probe: float32 [2048], replicated, may hold values from -0.125 to 0.125
- query_matrix: bfloat16 [2048, 2048], P('dp', 'mp'), may hold values from -0.125 to 0.125
- key_value_matrix: bfloat16 [2048, 512], P('dp'), may hold values from -0.125 to 0.125
- output_matrix: bfloat16 [2048, 2048], P('dp', 'mp'), may hold values from -0.5 to 0.5
- gate_matrix: bfloat16 [2048, 16384], P('dp', 'mp'), may hold values from -0.125 to 0.125
- up_matrix: bfloat16 [2048, 16384], P('dp', 'mp'), may hold values from -0.125 to 0.125
- down_matrix: bfloat16 [2048, 16384], P('dp', 'mp'), may hold values from -0.046875 to 0.046875
- query_update_left: bfloat16 [3, 2048, 256], P(None, 'dp'), may hold values from -0.125 to 0.125
- query_update_right: bfloat16 [3, 256, 2048], P(None, None, 'mp'), may hold values from -0.375 to 0.375
- key_value_update_left: bfloat16 [3, 2048, 512], P(None, 'dp'), may hold values from -0.125 to 0.125
- key_value_update_right: bfloat16 [3, 256, 512], replicated, may hold values from -0.375 to 0.375
- output_update_left: bfloat16 [3, 2048, 256], P(None, 'dp'), may hold values from -0.5 to 0.5
- output_update_right: bfloat16 [3, 256, 2048], P(None, None, 'mp'), may hold values from -0.375 to 0.375
- gate_update_left: bfloat16 [3, 2048, 256], P(None, 'dp'), may hold values from -0.125 to 0.125
- gate_update_right: bfloat16 [3, 256, 16384], P(None, None, 'mp'), may hold values from -0.375 to 0.375
- up_update_left: bfloat16 [3, 2048, 256], P(None, 'dp'), may hold values from -0.125 to 0.125
- up_update_right: bfloat16 [3, 256, 16384], P(None, None, 'mp'), may hold values from -0.375 to 0.375
- down_update_left: bfloat16 [3, 2048, 256], P(None, 'dp'), may hold values from -0.046875 to 0.046875
- down_update_right: bfloat16 [3, 256, 16384], P(None, None, 'mp'), may hold values from -0.375 to 0.375
Outputs:
- counts: int32 [3], replicated
- confidence: float32 [1], replicated
- mixed: bfloat16 [2048, 2048], P('dp')
- tokens_grad: float32 [2048, 2048], P('dp')
- attn_gain_grad: float32 [2048], P('dp')
- mlp_gain_grad: float32 [2048], P('dp')
- q_weight_grad: float32 [2048, 2048], P('dp', 'mp')
- kv_weight_grad: float32 [2048, 512], P('dp')
- o_weight_grad: float32 [2048, 2048], P('dp', 'mp')
- gate_weight_grad: float32 [2048, 16384], P('dp', 'mp')
- up_weight_grad: float32 [2048, 16384], P('dp', 'mp')
- down_weight_grad: float32 [2048, 16384], P('dp', 'mp')
- q_lora_a_grad: float32 [3, 2048, 256], P(None, 'dp')
- q_lora_b_grad: float32 [3, 256, 2048], P(None, 'dp', 'mp')
- kv_lora_a_grad: float32 [3, 2048, 512], P(None, 'dp')
- kv_lora_b_grad: float32 [3, 256, 512], P(None, 'dp')
- o_lora_a_grad: float32 [3, 2048, 256], P(None, 'dp')
- o_lora_b_grad: float32 [3, 256, 2048], P(None, 'dp', 'mp')
- gate_lora_a_grad: float32 [3, 2048, 256], P(None, 'dp')
- gate_lora_b_grad: float32 [3, 256, 16384], P(None, 'dp', 'mp')
- up_lora_a_grad: float32 [3, 2048, 256], P(None, 'dp')
- up_lora_b_grad: float32 [3, 256, 16384], P(None, 'dp', 'mp')
- down_lora_a_grad: float32 [3, 2048, 256], P(None, 'dp')
- down_lora_b_grad: float32 [3, 256, 16384], P(None, 'dp', 'mp')
Inputs may be any that keep to these rules, and one draw needn't show every extreme that they name: `token_sequence_index`: sequence 0 has 1024 tokens, in two blocks of 64 consecutive positions in every block of 256 tokens; the other sequences have 1024 tokens each, packed in order into the remaining half of the blocks. Each pair of sequence and position occurs once; positions of a sequence run from 0 to its length less one.
All inputs are finite; a program needn't handle non-finite values.
Results may differ from a plain program's by a relative error of at most 0.015.
The roundings to bfloat16 on the way count: a program that leaves them out, or rounds other values in their place, can miss the bound.
Values may be sent and summed in bfloat16 or wider, within the bound.
No kernel may reach another device: no remote copies, remote signals or barrier semaphores. Data moves between devices by JAX's collectives and lax.ppermute only.
A program may use at most 768 MiB of HBM per device.

v0:
```python
import math

import jax
import jax.numpy as jnp
from jax import lax
from jax.sharding import PartitionSpec as P

HEAD_SIZE = 256
LOOP_COUNT = 3


EPSILON = 1e-06
MASKED_SCORE = -1e30
precise = lax.Precision.HIGHEST


def rms_norm(inputs, gain):
    return inputs * lax.rsqrt(jnp.mean(inputs * inputs, axis=-1, keepdims=True) + EPSILON) * gain


def rotate(inputs, spots, direction):
    half_width = inputs.shape[-1] // 2
    frequency = jnp.exp(
        jnp.arange(half_width, dtype=jnp.float32) * (-2.0 * math.log(10000.0) / inputs.shape[-1])
    )
    angles = spots.astype(jnp.float32)[:, None] * frequency[None, :]
    cos_part = jnp.cos(angles)
    sin_part = jnp.sin(angles) * direction
    if inputs.ndim == 3:
        cos_part = cos_part[:, None, :]
        sin_part = sin_part[:, None, :]
    first_half = inputs[..., :half_width]
    second_half = inputs[..., half_width:]
    return jnp.concatenate(
        [
            first_half * cos_part - second_half * sin_part,
            second_half * cos_part + first_half * sin_part,
        ],
        axis=-1,
    )


def update_delta(left_factor, right_factor, factor_pairs):
    if factor_pairs:
        rank_half = left_factor.shape[1] // 2
        width_half = right_factor.shape[1] // 2
        key_half = jnp.dot(
            left_factor[:, :rank_half],
            right_factor[:, :width_half],
            preferred_element_type=jnp.float32,
        )
        value_half = jnp.dot(
            left_factor[:, rank_half:],
            right_factor[:, width_half:],
            preferred_element_type=jnp.float32,
        )
        return jnp.concatenate([key_half, value_half], axis=1)
    return jnp.dot(left_factor, right_factor, preferred_element_type=jnp.float32)


def left_grad(weight_grad, right_factor, factor_pairs):
    right_wide = right_factor.astype(jnp.float32)
    if factor_pairs:
        width_half = right_factor.shape[1] // 2
        key_half = jnp.dot(
            weight_grad[:, :width_half], right_wide[:, :width_half].T, precision=precise
        )
        value_half = jnp.dot(
            weight_grad[:, width_half:], right_wide[:, width_half:].T, precision=precise
        )
        return jnp.concatenate([key_half, value_half], axis=1)
    return jnp.dot(weight_grad, right_wide.T, precision=precise)


def right_grad(left_factor, weight_grad, factor_pairs):
    left_wide = left_factor.astype(jnp.float32)
    if factor_pairs:
        rank_half = left_factor.shape[1] // 2
        width_half = weight_grad.shape[1] // 2
        key_half = jnp.dot(
            left_wide[:, :rank_half].T, weight_grad[:, :width_half], precision=precise
        )
        value_half = jnp.dot(
            left_wide[:, rank_half:].T, weight_grad[:, width_half:], precision=precise
        )
        return jnp.concatenate([key_half, value_half], axis=1)
    return jnp.dot(left_wide.T, weight_grad, precision=precise)


def attention_weights(queries, key_rows, query_seq, query_spots, key_seq, key_spots, score_scale):
    scores = (
        jnp.einsum("qhd,kd->hqk", queries, key_rows, preferred_element_type=jnp.float32)
        * score_scale
    )
    allowed = (query_seq[:, None] == key_seq[None, :]) & (
        key_spots[None, :] <= query_spots[:, None]
    )
    scores = jnp.where(allowed[None], scores, MASKED_SCORE)
    return jax.nn.softmax(scores, axis=-1)


def gated_unit(gate_act, up_act):
    return jax.nn.gelu(gate_act, approximate=True) * up_act


def outer_block(activation, gradient):
    return jnp.einsum("td,tc->dc", activation, gradient, preferred_element_type=jnp.float32)


def body(
    tokens,
    cotangent,
    token_sequence_index,
    positions,
    token_exit_loop,
    current_loop,
    attention_norm_gain,
    feedforward_norm_gain,
    probe,
    query_matrix,
    key_value_matrix,
    output_matrix,
    gate_matrix,
    up_matrix,
    down_matrix,
    query_update_left,
    query_update_right,
    key_value_update_left,
    key_value_update_right,
    output_update_left,
    output_update_right,
    gate_update_left,
    gate_update_right,
    up_update_left,
    up_update_right,
    down_update_left,
    down_update_right,
):
    loop_selection = current_loop[0]
    score_scale = HEAD_SIZE ** (-0.5)
    base_list = (query_matrix, key_value_matrix, output_matrix, gate_matrix, up_matrix, down_matrix)
    left_factor_tables = (
        query_update_left,
        key_value_update_left,
        output_update_left,
        gate_update_left,
        up_update_left,
        down_update_left,
    )
    right_factor_tables = (
        query_update_right,
        key_value_update_right,
        output_update_right,
        gate_update_right,
        up_update_right,
        down_update_right,
    )
    left_factor_list = [
        lax.dynamic_index_in_dim(update_table, loop_selection, 0, keepdims=False)
        for update_table in left_factor_tables
    ]
    right_factor_list = [
        lax.dynamic_index_in_dim(update_table, loop_selection, 0, keepdims=False)
        for update_table in right_factor_tables
    ]
    shards = [
        (
            base_list[table_index].astype(jnp.float32)
            + update_delta(
                left_factor_list[table_index], right_factor_list[table_index], table_index == 1
            )
        ).astype(jnp.bfloat16)
        for table_index in range(6)
    ]
    gathered = (
        lax.all_gather(shards[0], "dp", axis=0, tiled=True),
        lax.all_gather(shards[1], "dp", axis=0, tiled=True),
        lax.all_gather(shards[2], "dp", axis=0, tiled=True),
        lax.all_gather(shards[3], "dp", axis=0, tiled=True),
        lax.all_gather(shards[4], "dp", axis=0, tiled=True),
        lax.all_gather(shards[5], "dp", axis=0, tiled=True),
    )
    q_full, kv_full, o_full, gate_full, up_full, down_full = gathered
    row_count = tokens.shape[0]
    mp_count = lax.axis_size("mp")
    dp_count = lax.axis_size("dp")
    quarter_rows = row_count // mp_count
    head_count = q_full.shape[1] // HEAD_SIZE
    inputs_wide = tokens.astype(jnp.float32)
    normed = rms_norm(inputs_wide, attention_norm_gain)
    normed_b = normed.astype(jnp.bfloat16)
    queries = jnp.dot(normed_b, q_full, preferred_element_type=jnp.float32)
    query_b = rotate(queries.reshape(row_count, head_count, HEAD_SIZE), positions, 1.0).astype(
        jnp.bfloat16
    )
    key_value = jnp.dot(normed_b, kv_full, preferred_element_type=jnp.float32)
    key_b = rotate(key_value[:, :HEAD_SIZE], positions, 1.0).astype(jnp.bfloat16)
    value_b = key_value[:, HEAD_SIZE:].astype(jnp.bfloat16)
    outgoing = jnp.concatenate([key_b, value_b], axis=1)
    all_pairs, all_seq, all_spots = (
        lax.all_gather(outgoing, "dp", axis=0, tiled=True),
        lax.all_gather(token_sequence_index, "dp", axis=0, tiled=True),
        lax.all_gather(positions, "dp", axis=0, tiled=True),
    )

    def regroup(array):
        total_rows = array.shape[0]
        shaped = array.reshape((total_rows // row_count, mp_count, quarter_rows) + array.shape[1:])
        return jnp.swapaxes(shaped, 0, 1).reshape(array.shape)

    all_pairs = regroup(all_pairs)
    all_seq = regroup(all_seq)
    all_spots = regroup(all_spots)
    all_keys = all_pairs[:, :HEAD_SIZE]
    all_values = all_pairs[:, HEAD_SIZE:]
    weights_soft = attention_weights(
        query_b, all_keys, token_sequence_index, positions, all_seq, all_spots, score_scale
    )
    weights_low = weights_soft.astype(jnp.bfloat16)
    attended = jnp.einsum(
        "hqk,kd->qhd", weights_low, all_values, preferred_element_type=jnp.float32
    )
    attended_b = attended.reshape(row_count, head_count * HEAD_SIZE).astype(jnp.bfloat16)
    branch_part = jnp.einsum("tc,dc->td", attended_b, o_full, preferred_element_type=jnp.float32)
    branch = lax.psum(branch_part, "mp")
    middle = inputs_wide + branch
    normed2 = rms_norm(middle, feedforward_norm_gain)
    normed2_b = normed2.astype(jnp.bfloat16)
    gate_act = jnp.dot(normed2_b, gate_full, preferred_element_type=jnp.float32)
    up_act = jnp.dot(normed2_b, up_full, preferred_element_type=jnp.float32)
    hidden_b = gated_unit(gate_act, up_act).astype(jnp.bfloat16)
    output_part = jnp.einsum("tc,dc->td", hidden_b, down_full, preferred_element_type=jnp.float32)
    mlp_branch = lax.psum(output_part, "mp")
    output_rows = middle + mlp_branch
    confidence_local = jnp.sum(
        jax.nn.sigmoid(jnp.dot(output_rows, probe, precision=precise))
    ).reshape(1)
    levels = jnp.arange(LOOP_COUNT, dtype=jnp.int32)
    depth_hits = jnp.sum((token_exit_loop[:, None] == levels[None, :]).astype(jnp.float32), axis=0)
    confidence_total, depth_total = lax.psum((confidence_local, depth_hits), "dp")
    confidence = confidence_total / (row_count * dp_count)
    counts = depth_total.astype(jnp.int32)
    back_weights = (
        lax.all_gather(shards[0], "dp", axis=0, tiled=True),
        lax.all_gather(shards[1], "dp", axis=0, tiled=True),
        lax.all_gather(shards[2], "dp", axis=0, tiled=True),
        lax.all_gather(shards[3], "dp", axis=0, tiled=True),
        lax.all_gather(shards[4], "dp", axis=0, tiled=True),
        lax.all_gather(shards[5], "dp", axis=0, tiled=True),
    )
    q_back, kv_back, o_back, gate_back, up_back, down_back = back_weights
    grad_wide = cotangent.astype(jnp.float32)
    hidden_grad = jnp.dot(cotangent, down_back, preferred_element_type=jnp.float32)
    unused_value, unit_pull = jax.vjp(gated_unit, gate_act, up_act)
    gate_grad, up_grad = unit_pull(hidden_grad)
    gate_grad_b = gate_grad.astype(jnp.bfloat16)
    up_grad_b = up_grad.astype(jnp.bfloat16)
    normed2_part = jnp.einsum(
        "tc,dc->td", gate_grad_b, gate_back, preferred_element_type=jnp.float32
    ) + jnp.einsum("tc,dc->td", up_grad_b, up_back, preferred_element_type=jnp.float32)
    normed2_grad = lax.psum(normed2_part, "mp")
    unused_norm, mlp_pull = jax.vjp(rms_norm, middle, feedforward_norm_gain)
    middle_norm_grad, mlp_gain_part = mlp_pull(normed2_grad)
    middle_grad = grad_wide + middle_norm_grad
    middle_grad_b = middle_grad.astype(jnp.bfloat16)
    attended_grad_b = (
        jnp.dot(middle_grad_b, o_back, preferred_element_type=jnp.float32)
        .astype(jnp.bfloat16)
        .reshape(row_count, head_count, HEAD_SIZE)
    )
    weights_soft = attention_weights(
        query_b, all_keys, token_sequence_index, positions, all_seq, all_spots, score_scale
    )
    weights_low = weights_soft.astype(jnp.bfloat16)
    prob_grad = jnp.einsum(
        "qhd,kd->hqk", attended_grad_b, all_values, preferred_element_type=jnp.float32
    )
    score_grad_b = (
        weights_soft * (prob_grad - jnp.sum(prob_grad * weights_soft, axis=-1, keepdims=True))
    ).astype(jnp.bfloat16)
    query_grad = (
        jnp.einsum("hqk,kd->qhd", score_grad_b, all_keys, preferred_element_type=jnp.float32)
        * score_scale
    )
    keys_grad = (
        jnp.einsum("hqk,qhd->kd", score_grad_b, query_b, preferred_element_type=jnp.float32)
        * score_scale
    )
    values_grad = jnp.einsum(
        "hqk,qhd->kd", weights_low, attended_grad_b, preferred_element_type=jnp.float32
    )
    pair_grad = jnp.concatenate([keys_grad, values_grad], axis=1)
    quarter_grad = lax.psum_scatter(pair_grad, ("mp", "dp"), scatter_dimension=0, tiled=True)
    start_row = lax.axis_index("mp") * quarter_rows
    quarter_spots = lax.dynamic_slice_in_dim(positions, start_row, quarter_rows, 0)
    quarter_pair_b = jnp.concatenate(
        [rotate(quarter_grad[:, :HEAD_SIZE], quarter_spots, -1.0), quarter_grad[:, HEAD_SIZE:]],
        axis=1,
    ).astype(jnp.bfloat16)
    query_grad_b = (
        rotate(query_grad, positions, -1.0)
        .reshape(row_count, head_count * HEAD_SIZE)
        .astype(jnp.bfloat16)
    )
    local_part = jnp.einsum("tc,dc->td", query_grad_b, q_back, preferred_element_type=jnp.float32)
    pair_rows = jnp.einsum("tc,dc->td", quarter_pair_b, kv_back, preferred_element_type=jnp.float32)
    current_rows = lax.dynamic_slice_in_dim(local_part, start_row, quarter_rows, 0)
    normed_part = lax.dynamic_update_slice_in_dim(
        local_part, current_rows + pair_rows, start_row, 0
    )
    normed_grad = lax.psum(normed_part, "mp")
    unused_first, attn_pull = jax.vjp(rms_norm, inputs_wide, attention_norm_gain)
    inputs_norm_grad, attn_gain_part = attn_pull(normed_grad)
    tokens_grad = middle_grad + inputs_norm_grad
    quarter_normed_b = lax.dynamic_slice_in_dim(normed_b, start_row, quarter_rows, 0)
    widths = [
        q_full.shape[1],
        kv_full.shape[1],
        o_full.shape[1],
        gate_full.shape[1],
        up_full.shape[1],
        down_full.shape[1],
    ]
    stacked = lax.psum_scatter(
        jnp.concatenate(
            [
                outer_block(normed_b, query_grad_b),
                outer_block(quarter_normed_b, quarter_pair_b),
                outer_block(middle_grad_b, attended_b),
                outer_block(normed2_b, gate_grad_b),
                outer_block(normed2_b, up_grad_b),
                outer_block(cotangent, hidden_b),
            ],
            axis=1,
        ),
        "dp",
        scatter_dimension=0,
        tiled=True,
    )
    weight_grads = []
    offset = 0
    for width_item in widths:
        weight_grads.append(stacked[:, offset : offset + width_item])
        offset = offset + width_item
    left_parts = [
        left_grad(weight_grads[table_index], right_factor_list[table_index], table_index == 1)
        for table_index in range(6)
    ]
    summed = lax.psum(
        (
            left_parts[0],
            left_parts[1],
            left_parts[2],
            left_parts[3],
            left_parts[4],
            left_parts[5],
            weight_grads[1],
        ),
        "mp",
    )
    weight_grads[1] = summed[6]
    right_parts = [
        right_grad(left_factor_list[table_index], weight_grads[table_index], table_index == 1)
        for table_index in range(6)
    ]
    reduced = (
        lax.psum_scatter(right_parts[0], "dp", scatter_dimension=0, tiled=True),
        lax.psum_scatter(right_parts[1], "dp", scatter_dimension=0, tiled=True),
        lax.psum_scatter(right_parts[2], "dp", scatter_dimension=0, tiled=True),
        lax.psum_scatter(right_parts[3], "dp", scatter_dimension=0, tiled=True),
        lax.psum_scatter(right_parts[4], "dp", scatter_dimension=0, tiled=True),
        lax.psum_scatter(right_parts[5], "dp", scatter_dimension=0, tiled=True),
        lax.psum_scatter(attn_gain_part, "dp", scatter_dimension=0, tiled=True),
        lax.psum_scatter(mlp_gain_part, "dp", scatter_dimension=0, tiled=True),
    )

    def place_loop(grad_item):
        empty = jnp.zeros((LOOP_COUNT,) + grad_item.shape, jnp.float32)
        return lax.dynamic_update_index_in_dim(empty, grad_item, loop_selection, 0)

    return (
        counts,
        confidence,
        output_rows.astype(jnp.bfloat16),
        tokens_grad,
        reduced[6],
        reduced[7],
        weight_grads[0],
        weight_grads[1],
        weight_grads[2],
        weight_grads[3],
        weight_grads[4],
        weight_grads[5],
        place_loop(summed[0]),
        place_loop(reduced[0]),
        place_loop(summed[1]),
        place_loop(reduced[1]),
        place_loop(summed[2]),
        place_loop(reduced[2]),
        place_loop(summed[3]),
        place_loop(reduced[3]),
        place_loop(summed[4]),
        place_loop(reduced[4]),
        place_loop(summed[5]),
        place_loop(reduced[5]),
    )


def solution(mesh):
    return jax.shard_map(
        body,
        mesh=mesh,
        in_specs=(
            P("dp", None),
            P("dp", None),
            P("dp"),
            P("dp"),
            P("dp"),
            P(),
            P(),
            P(),
            P(),
            P("dp", "mp"),
            P("dp", None),
            P("dp", "mp"),
            P("dp", "mp"),
            P("dp", "mp"),
            P("dp", "mp"),
            P(None, "dp", None),
            P(None, None, "mp"),
            P(None, "dp", None),
            P(),
            P(None, "dp", None),
            P(None, None, "mp"),
            P(None, "dp", None),
            P(None, None, "mp"),
            P(None, "dp", None),
            P(None, None, "mp"),
            P(None, "dp", None),
            P(None, None, "mp"),
        ),
        out_specs=(
            P(),
            P(),
            P("dp", None),
            P("dp", None),
            P("dp"),
            P("dp"),
            P("dp", "mp"),
            P("dp", None),
            P("dp", "mp"),
            P("dp", "mp"),
            P("dp", "mp"),
            P("dp", "mp"),
            P(None, "dp", None),
            P(None, "dp", "mp"),
            P(None, "dp", None),
            P(None, "dp", None),
            P(None, "dp", None),
            P(None, "dp", "mp"),
            P(None, "dp", None),
            P(None, "dp", "mp"),
            P(None, "dp", None),
            P(None, "dp", "mp"),
            P(None, "dp", None),
            P(None, "dp", "mp"),
        ),
        check_vma=False,
    )
```

profile of v0, /device:TPU:0, one launch (start us, length us, event | category | flops | bytes accessed | tf_op | source)
XLA Modules:
  0.0 5234.7 jit_solution(11021996251609456132)
XLA Ops:
  10.6 2.0 fusion.44
  13.9 50.6 all-gather.10.cloned.1.call-done
  64.5 2.3 fusion.163
  69.0 2.0 fusion.45
  71.0 17.7 all-gather.1
  88.9 17.0 all-gather
  107.5 7.2 all-gather.14.cloned.1.call-done
  114.7 2.3 fusion.164
  119.2 46.0 all-gather.12.cloned.1.call-done
  167.1 4.7 fusion.162
  171.8 3.4 convolution_convert_fusion.1
  175.2 40.6 all-gather.16.cloned.1.call-done
  215.8 3.7 fusion.165
  221.1 3.7 fusion.1
  226.4 3.7 fusion.2
  231.7 3.8 fusion.3
  235.8 33.8 all-reduce.10.cloned.1.call-done
  269.5 2.2 multiply_reduce_fusion.2
  273.0 227.1 %all-gather.18.cloned.1.call-done = bf16[2048,4096]{1,0:T(8,128)(2,1)} async-done(((bf16[256,4096]{1,0:T(8,128)(2,1)}), bf16[2048,4096]{1,0:T(8,128)(2,1)}) %all-gather.18.cloned.1.call-update) | async-done | bytes 16777232 | tf_op jit(solution)/shard_map/all_gather | solution.py:179
  500.0 12.6 fusion.166
  512.6 216.1 %all-gather.20.cloned.1.call-done = bf16[2048,4096]{1,0:T(8,128)(2,1)} async-done(((bf16[256,4096]{1,0:T(8,128)(2,1)}), bf16[2048,4096]{1,0:T(8,128)(2,1)}) %all-gather.20.cloned.1.call-update) | async-done | bytes 16777232 | tf_op jit(solution)/shard_map/all_gather | solution.py:180
  728.8 12.7 fusion.167
  741.5 215.5 %all-gather.22.cloned.1.call-done = bf16[2048,4096]{1,0:T(8,128)(2,1)} async-done(((bf16[256,4096]{1,0:T(8,128)(2,1)}), bf16[2048,4096]{1,0:T(8,128)(2,1)}) %all-gather.22.cloned.1.call-update) | async-done | bytes 16777232 | tf_op jit(solution)/shard_map/all_gather | solution.py:181
  957.0 15.0 multiply_convert_fusion
  971.9 12.2 fusion.169
  984.2 12.8 convolution_add_fusion.3
  997.2 49.5 all-reduce.12.cloned.1.call-done
  1046.7 2.8 multiply_reduce_fusion
  1054.8 4.6 convolution_bitcast_fusion.1
  1059.4 3.4 fusion.11
  1066.3 2.4 pad_maximum_fusion
  1068.7 5.3 copy.209
  1074.2 2.9 fusion.43
  1079.0 4.0 convolution_dynamic-update-slice_fusion.4
  1083.0 135.2 %reduce-scatter.22.cloned.1.call-done = f32[64,512]{1,0:T(8,128)} async-done(((f32[2048,512]{1,0:T(8,128)}), f32[64,512]{1,0:T(8,128)}) %reduce-scatter.22.cloned.1.call-update) | async-done | bytes 131088 | tf_op jit(solution)/shard_map/reduce_scatter | solution.py:293
  1220.4 3.9 convolution_dynamic-update-slice_fusion.2
  1224.3 2.8 convolution_dynamic-update-slice_fusion.3
  1227.1 13.3 convolution_dynamic-update-slice_fusion.1
  1240.5 13.4 convolution_dynamic-update-slice_fusion
  1253.8 13.2 bitcast_dynamic-update-slice_fusion
  1269.0 13.6 fusion.168
  1282.5 3.8 fusion.170
  1286.3 2.4 fusion.18
  1288.7 3303.0 %all-reduce.14.cloned.1.call-done = f32[2048,13824]{1,0:T(8,128)} async-done(((f32[2048,13824]{1,0:T(8,128)}), f32[2048,13824]{1,0:T(8,128)}) %all-reduce.14.cloned.1.call-update) | async-done | bytes 113246224
  4591.7 2.6 fusion.160
  4596.2 2.1 convolution_bitcast_fusion.3
  4598.3 12.7 fusion.159
  4610.9 5.8 fusion.46
  4616.7 4.7 fusion.49
  4621.4 4.4 fusion.52
  4629.6 2.4 fusion.100
  4632.1 2.2 fusion.97
  4634.3 120.0 %all-reduce.16.cloned.1.call-done = (f32[256,2048]{1,0:T(8,128)}, f32[256,2048]{1,0:T(8,128)}, f32[256,512]{1,0:T(8,128)}, f32[1,256,256]{2,1,0:T(8,128)}, f32[1...) async-done(((f32[256,2048]{1,0:T(8,128)}, f32[256,2048]{1,0:T(8,128)}, ...) | async-done | bytes 6553616 | tf_op jit(solution)/shard_map/psum | solution.py:233
  4758.3 6.6 fusion.94
  4764.9 6.7 fusion.91
  4771.9 6.7 fusion.88
  4779.3 41.4 reduce-scatter.12.cloned.1.call-done
  4822.9 62.5 %reduce-scatter.14.cloned.1.call-done = f32[32,512]{1,0:T(8,128)} async-done(((f32[256,512]{1,0:T(8,128)}), f32[32,512]{1,0:T(8,128)}) %reduce-scatter.14.cloned.1.call-update) | async-done | bytes 65552 | tf_op jit(solution)/shard_map/reduce_scatter | solution.py:369
  4887.0 3.5 fusion.57
  4891.9 36.4 all-reduce.3
  4942.1 8.4 reduce-scatter.24.cloned.1.call-done
  4951.7 89.5 %reduce-scatter.16.cloned.1.call-done = f32[32,4096]{1,0:T(8,128)} async-done(((f32[256,4096]{1,0:T(8,128)}), f32[32,4096]{1,0:T(8,128)}) %reduce-scatter.16.cloned.1.call-update) | async-done | bytes 524304 | tf_op jit(solution)/shard_map/reduce_scatter | solution.py:370
  5042.4 90.4 %reduce-scatter.18.cloned.1.call-done = f32[32,4096]{1,0:T(8,128)} async-done(((f32[256,4096]{1,0:T(8,128)}), f32[32,4096]{1,0:T(8,128)}) %reduce-scatter.18.cloned.1.call-update) | async-done | bytes 524304 | tf_op jit(solution)/shard_map/reduce_scatter | solution.py:371
  5136.0 87.9 %reduce-scatter.20.cloned.1.call-done = f32[32,4096]{1,0:T(8,128)} async-done(((f32[256,4096]{1,0:T(8,128)}), f32[32,4096]{1,0:T(8,128)}) %reduce-scatter.20.cloned.1.call-update) | async-done | bytes 524304 | tf_op jit(solution)/shard_map/reduce_scatter | solution.py:372
  (263 shorter events, 69.1 us)
Async XLA Ops:
  7.2 3.4 copy-start
  7.2 2.4 copy-start.50
  7.2 57.3 %all-gather.10.cloned.1.call-start = ((), (), s32[]{:S(2)}) async-start(), calls=%async_computation.7 | async-start | bytes 2359296 | tf_op jit(solution)/shard_map/all_gather | solution.py:177
  9.1 3.9 copy-start.23
  9.1 3.9 copy-start.24
  9.1 3.5 copy-start.60
  9.1 3.5 copy-start.6
  9.6 4.0 copy-start.55
  10.5 104.2 %all-gather.14.cloned.1.call-start = ((), (), s32[]{:S(2)}) async-start(), calls=%async_computation.9 | async-start | bytes 2359296 | tf_op jit(solution)/shard_map/all_gather | solution.py:176
  12.6 152.7 %all-gather.12.cloned.1.call-start = ((), (), s32[]{:S(2)}) async-start(), calls=%async_computation.8 | async-start | bytes 2359296 | tf_op jit(solution)/shard_map/all_gather | solution.py:201
  12.7 54.2 %copy-start.65 = (f32[128]{0:T(128)}, f32[128]{0:T(128)S(1)}, u32[]{:S(2)}) copy-start(f32[128]{0:T(128)S(1)} %multiply_exponential_fusion) | copy-start | bytes 1540
  13.0 53.8 %copy-start.61 = (f32[256]{0:T(256)}, f32[256]{0:T(256)S(1)}, u32[]{:S(2)}) copy-start(f32[256]{0:T(256)S(1)} %fusion.23) | copy-start | bytes 3076
  13.9 100.8 %copy-start.10 = (bf16[256,2048]{1,0:T(8,128)(2,1)}, bf16[256,2048]{1,0:T(8,128)(2,1)S(1)}, u32[]{:S(2)}) copy-start(bf16[256,2048]{1,0:T(8,128)(2,1)S(1)} %fusion.19) | copy-start | bytes 3145732
  13.9 55.0 %copy-start.51 = (bf16[256,512]{1,0:T(8,128)(2,1)S(1)}, bf16[256,512]{1,0:T(8,128)(2,1)}, u32[]{:S(2)}) copy-start(bf16[256,512]{1,0:T(8,128)(2,1)} %param.38) | copy-start | bytes 786436
  66.8 22.1 copy-start.64
  68.9 146.9 %all-gather.16.cloned.1.call-start = ((), (), s32[]{:S(2)}) async-start(), calls=%async_computation.10 | async-start | bytes 2359296 | tf_op jit(solution)/shard_map/all_gather | solution.py:178
  70.9 198.6 %all-reduce.10.cloned.1.call-start = ((), (), s32[]{:S(2)}) async-start(), calls=%async_computation.11 | async-start | bytes 4194304 | tf_op jit(solution)/shard_map/psum | solution.py:225
  107.5 59.6 %copy-start.42 = (pred[256,2048]{0,1:T(8,128)(4,1)}, pred[256,2048]{0,1:T(8,128)(4,1)S(1)}, u32[]{:S(2)}) copy-start(pred[256,2048]{0,1:T(8,128)(4,1)S(1)} %compare_and_fusion) | copy-start | bytes 1572868
  167.1 4.7 copy-start.32
  219.5 280.5 %all-gather.18.cloned.1.call-start = ((), (), s32[]{:S(2)}) async-start(), calls=%async_computation.12 | async-start | bytes 18874368 | tf_op jit(solution)/shard_map/all_gather | solution.py:179
  224.8 504.0 %all-gather.20.cloned.1.call-start = ((), (), s32[]{:S(2)}) async-start(), calls=%async_computation.13 | async-start | bytes 18874368 | tf_op jit(solution)/shard_map/all_gather | solution.py:180
  230.1 726.8 %all-gather.22.cloned.1.call-start = ((), (), s32[]{:S(2)}) async-start(), calls=%async_computation.14 | async-start | bytes 18874368 | tf_op jit(solution)/shard_map/all_gather | solution.py:181
  235.5 36.3 copy-start.54
  235.5 811.2 %all-reduce.12.cloned.1.call-start = ((), (), s32[]{:S(2)}) async-start(), calls=%async_computation.15 | async-start | bytes 4194304 | tf_op jit(solution)/shard_map/psum | solution.py:261
  997.0 221.2 %reduce-scatter.22.cloned.1.call-start = ((), (), s32[]{:S(2)}) async-start(), calls=%async_computation.21 | async-start | bytes 4325376 | tf_op jit(solution)/shard_map/reduce_scatter | solution.py:293
  1046.7 2.9 copy-start.15
  1046.7 2.9 copy-start.20
  1051.5 3.2 copy-start.43
  1051.5 3.2 copy-start.44
  1059.4 3.8 copy-start.19
  1064.0 2.4 copy-start.34
  1074.1 3517.6 %all-reduce.14.cloned.1.call-start = ((), (), s32[]{:S(2)}) async-start(), calls=%async_computation.23 | async-start | bytes 226492416
  1074.2 2.9 copy-start.45
  1079.0 140.2 %copy-start.66 = (f32[128]{0:T(128)S(1)}, f32[128]{0:T(128)}, u32[]{:S(2)}) copy-start(f32[128]{0:T(128)} %copy-done.65) | copy-start | bytes 1540
  1220.4 3.9 copy-start.4
  1224.3 2.8 copy-start.9
  1224.3 2.8 copy-start.27
  1227.1 13.3 copy-start.26
  1240.5 13.4 copy-start.21
  1240.5 13.4 copy-start.22
  1267.1 3487.2 %all-reduce.16.cloned.1.call-start = ((), (), s32[]{:S(2)}) async-start(), calls=%async_computation.24 | async-start | bytes 13107200 | tf_op jit(solution)/shard_map/psum | solution.py:233
  1282.5 3.8 copy-start.31
  4594.3 37.8 copy-start.17
  4610.9 5.8 copy-start.2
  4616.7 4.7 copy-start.1
  4621.4 4.5 copy-start.25
  4629.6 191.2 %reduce-scatter.12.cloned.1.call-start = ((), (), s32[]{:S(2)}) async-start(), calls=%async_computation.16 | async-start | bytes 589824 | tf_op jit(solution)/shard_map/reduce_scatter | solution.py:367
  4632.0 253.4 %reduce-scatter.14.cloned.1.call-start = ((), (), s32[]{:S(2)}) async-start(), calls=%async_computation.17 | async-start | bytes 589824 | tf_op jit(solution)/shard_map/reduce_scatter | solution.py:369
  4634.3 316.3 %reduce-scatter.24.cloned.1.call-start = ((), (), s32[]{:S(2)}) async-start(), calls=%async_computation.22 | async-start | bytes 589824
  4758.2 282.9 %reduce-scatter.16.cloned.1.call-start = ((), (), s32[]{:S(2)}) async-start(), calls=%async_computation.18 | async-start | bytes 4718592 | tf_op jit(solution)/shard_map/reduce_scatter | solution.py:370
  4764.9 367.9 %reduce-scatter.18.cloned.1.call-start = ((), (), s32[]{:S(2)}) async-start(), calls=%async_computation.19 | async-start | bytes 4718592 | tf_op jit(solution)/shard_map/reduce_scatter | solution.py:371
  4771.6 452.3 %reduce-scatter.20.cloned.1.call-start = ((), (), s32[]{:S(2)}) async-start(), calls=%async_computation.20 | async-start | bytes 4718592 | tf_op jit(solution)/shard_map/reduce_scatter | solution.py:372
  4778.5 108.5 %copy-start.63 = (f32[2048]{0:T(1024)S(1)}, f32[2048]{0:T(1024)}, u32[]{:S(2)}) copy-start(f32[2048]{0:T(1024)} %param.35) | copy-start | bytes 24580
  4887.0 4.1 copy-start.7
  4887.0 4.1 copy-start.11
  4887.0 4.1 copy-start.56
  4887.0 4.1 copy-start.59
  4933.5 3.7 copy-start.62
  4933.5 3.7 copy-start.14
  4937.3 2.3 copy-start.8
  4937.3 2.9 copy-start.12
  4951.6 182.4 %copy-start.53 = (f32[3,32,512]{2,1,0:T(8,128)}, f32[3,32,512]{2,1,0:T(8,128)S(1)}, u32[]{:S(2)}) copy-start(f32[3,32,512]{2,1,0:T(8,128)S(1)} %constant_dynamic-update-slice_fusion.4) | copy-start | bytes 589828
  5042.3 90.4 %copy-start.37 = (f32[3,32,4096]{2,1,0:T(8,128)}, f32[3,32,4096]{2,1,0:T(8,128)S(1)}, u32[]{:S(2)}) copy-start(f32[3,32,4096]{2,1,0:T(8,128)S(1)} %bitcast_dynamic-update-slice_fusion.3) | copy-start | bytes 4718596
  5134.0 91.1 %copy-start.33 = (f32[256,512]{1,0:T(8,128)S(1)}, f32[256,512]{1,0:T(8,128)}, u32[]{:S(2)}) copy-start(f32[256,512]{1,0:T(8,128)} %get-tuple-element.80) | copy-start | bytes 1572868
  (23 other events, 31.4 us)
Sparse Core Ops, SparseCore 0:
  10.7 53.7 all-gather.9
  67.2 47.5 all-gather.13
  117.4 47.7 all-gather.11
  167.8 47.9 all-gather.15
  219.6 49.8 all-reduce.9
  272.3 227.6 all-gather.17
  503.0 225.7 all-gather.19
  731.1 225.7 all-gather.21
  997.1 49.5 all-reduce.11
  1074.2 143.9 reduce-scatter.21
  1267.2 3324.4 all-reduce.13
  4629.7 124.5 all-reduce.15
  4758.6 62.0 reduce-scatter.11
  4824.5 60.8 reduce-scatter.13
  4889.6 60.8 reduce-scatter.23
  4954.0 87.0 reduce-scatter.15
  5045.0 87.6 reduce-scatter.17
  5136.2 87.6 reduce-scatter.19
where the time goes:
time: 5240 us; the launch traced here: 5230 us
  waiting for transfers between devices  4820 us (92%)
  matrix products  232 us (4%)
  blocking collectives  71.1 us (1%)
  local copies, waits for them, and re-layouts  61.2 us (1%)
    unnamed x20, waiting for transfers between devices  3310 us
    all_gather x1, waiting for transfers between devices, body(): lax.all_gather(shards[3], 'dp', axis=0, tiled=True)  227 us
    all_gather x1, waiting for transfers between devices, body(): lax.all_gather(shards[4], 'dp', axis=0, tiled=True)  216 us
    all_gather x1, waiting for transfers between devices, body(): lax.all_gather(shards[5], 'dp', axis=0, tiled=True)  215 us
    reduce_scatter x1, waiting for transfers between devices, body(): lax.psum_scatter(pair_grad, ('mp', 'dp'), scatter_dimension=0, tiled=True)  135 us
    psum x1, waiting for transfers between devices, body(): mlp_branch = lax.psum(output_part, 'mp')  120 us
  transfers between devices with their start and end apart: 18, of which 18 were waited for; matrix products, arithmetic and copies ran while one was open for 3% of the time, Pallas kernels for 0%

commit v1 on v0

v1 whole, which is shorter than its diff:
```python
import math

import jax
import jax.numpy as jnp
from jax import lax
from jax.sharding import PartitionSpec as P

HEAD_SIZE = 256
LOOP_COUNT = 3


EPSILON = 1e-06
MASKED_SCORE = -1e30
precise = lax.Precision.HIGHEST
f32 = jnp.float32
bf16 = jnp.bfloat16


def rms_norm(inputs, gain):
    return inputs * lax.rsqrt(jnp.mean(inputs * inputs, axis=-1, keepdims=True) + EPSILON) * gain


def rotate(inputs, spots, direction):
    half_width = inputs.shape[-1] // 2
    frequency = jnp.exp(
        jnp.arange(half_width, dtype=jnp.float32) * (-2.0 * math.log(10000.0) / inputs.shape[-1])
    )
    angles = spots.astype(jnp.float32)[:, None] * frequency[None, :]
    cos_part = jnp.cos(angles)
    sin_part = jnp.sin(angles) * direction
    if inputs.ndim == 3:
        cos_part = cos_part[:, None, :]
        sin_part = sin_part[:, None, :]
    first_half = inputs[..., :half_width]
    second_half = inputs[..., half_width:]
    return jnp.concatenate(
        [
            first_half * cos_part - second_half * sin_part,
            second_half * cos_part + first_half * sin_part,
        ],
        axis=-1,
    )


def update_delta(left_factor, right_factor, factor_pairs):
    if factor_pairs:
        rank_half = left_factor.shape[1] // 2
        width_half = right_factor.shape[1] // 2
        key_half = jnp.dot(
            left_factor[:, :rank_half],
            right_factor[:, :width_half],
            preferred_element_type=jnp.float32,
        )
        value_half = jnp.dot(
            left_factor[:, rank_half:],
            right_factor[:, width_half:],
            preferred_element_type=jnp.float32,
        )
        return jnp.concatenate([key_half, value_half], axis=1)
    return jnp.dot(left_factor, right_factor, preferred_element_type=jnp.float32)


def attention_weights(queries, key_rows, query_seq, query_spots, key_seq, key_spots, score_scale):
    scores = (
        jnp.einsum("qhd,kd->hqk", queries, key_rows, preferred_element_type=jnp.float32)
        * score_scale
    )
    allowed = (query_seq[:, None] == key_seq[None, :]) & (
        key_spots[None, :] <= query_spots[:, None]
    )
    scores = jnp.where(allowed[None], scores, MASKED_SCORE)
    return jax.nn.softmax(scores, axis=-1)


def gated_unit(gate_act, up_act):
    return jax.nn.gelu(gate_act, approximate=True) * up_act


def dot(left, right):
    return jnp.dot(left, right, preferred_element_type=f32)


def dot_rows(left, right):
    return lax.dot_general(left, right, (((0,), (0,)), ((), ())), preferred_element_type=f32)


def dot_cols(left, right):
    return lax.dot_general(left, right, (((1,), (1,)), ((), ())), preferred_element_type=f32)


def swap(value, axis, bit):
    count = lax.axis_size(axis)
    return lax.ppermute(value, axis, [(place, place ^ bit) for place in range(count)])


def far_bits():
    bit = lax.axis_size("dp") // 2
    bits = []
    while bit > 1:
        bits.append(bit)
        bit = bit // 2
    return bits


def grow(value, axis, bit):
    return jnp.concatenate([value, swap(value, axis, bit)], axis=0)


def fold(value, axis, bit):
    half = value.shape[0] // 2
    arrived = swap(value[half:].astype(bf16), axis, bit)
    return value[:half] + arrived.astype(f32)


def gather_mp(value):
    return grow(grow(value, "mp", 2), "mp", 1)


def scatter_mp(value):
    return fold(fold(value, "mp", 1), "mp", 2)


def gather_all(value):
    for bit in far_bits():
        value = grow(value, "dp", bit)
    half = value.shape[0] // 2
    front = grow(grow(value[:half], "dp", 1), "mp", 2)
    rear = grow(grow(value[half:], "mp", 2), "dp", 1)
    return grow(jnp.concatenate([front, rear], axis=0), "mp", 1)


def scatter_all(value):
    value = fold(value, "mp", 1)
    half = value.shape[0] // 2
    front = fold(fold(value[:half], "mp", 2), "dp", 1)
    rear = fold(fold(value[half:], "dp", 1), "mp", 2)
    value = jnp.concatenate([front, rear], axis=0)
    for bit in reversed(far_bits()):
        value = fold(value, "dp", bit)
    return value


def sum_all(value):
    for axis in ("mp", "dp"):
        bit = 1
        while bit < lax.axis_size(axis):
            value = value + swap(value, axis, bit)
            bit = bit * 2
    return value


def sum_mp(value):
    value = value + swap(value, "mp", 1)
    low = value.astype(bf16)
    return low.astype(f32) + swap(low, "mp", 2).astype(f32)


def exchange_dp(block_for):
    count = lax.axis_size("dp")
    me = lax.axis_index("dp")
    own = block_for(me)
    result = jnp.zeros((count,) + own.shape, own.dtype)
    result = lax.dynamic_update_index_in_dim(result, own, me, 0)
    for step in range(count - 1, 0, -1):
        place = jnp.bitwise_xor(me, step)
        arrived = swap(block_for(place), "dp", step)
        result = lax.dynamic_update_index_in_dim(result, arrived, place, 0)
    return result


def relative_rows(value):
    me = lax.axis_index("mp")
    rows = value.shape[0] // 4
    return jnp.concatenate(
        [
            lax.dynamic_slice_in_dim(value, jnp.bitwise_xor(me, step) * rows, rows, 0)
            for step in (0, 2, 1, 3)
        ],
        axis=0,
    )


def natural_rows(value):
    me = lax.axis_index("mp")
    rows = value.shape[0] // 4
    blocks = []
    for place in range(4):
        step = jnp.bitwise_xor(me, place)
        slot = (step & 1) * 2 + (step >> 1)
        blocks.append(lax.dynamic_slice_in_dim(value, slot * rows, rows, 0))
    return jnp.concatenate(blocks, axis=0)


def body(
    tokens,
    cotangent,
    token_sequence_index,
    positions,
    token_exit_loop,
    current_loop,
    attention_norm_gain,
    feedforward_norm_gain,
    probe,
    query_matrix,
    key_value_matrix,
    output_matrix,
    gate_matrix,
    up_matrix,
    down_matrix,
    query_update_left,
    query_update_right,
    key_value_update_left,
    key_value_update_right,
    output_update_left,
    output_update_right,
    gate_update_left,
    gate_update_right,
    up_update_left,
    up_update_right,
    down_update_left,
    down_update_right,
):
    loop_selection = current_loop[0]
    score_scale = HEAD_SIZE ** (-0.5)
    mp_count = lax.axis_size("mp")
    dp_count = lax.axis_size("dp")
    mp_place = lax.axis_index("mp")
    dp_place = lax.axis_index("dp")
    row_count, model_width = tokens.shape
    own_rows = row_count // mp_count
    head_count = query_matrix.shape[1] // HEAD_SIZE
    hidden_own = gate_matrix.shape[1] // dp_count
    query_cols = query_matrix.shape[1]
    block_width = query_matrix.shape[0]

    def pick(table):
        return lax.dynamic_index_in_dim(table, loop_selection, 0, keepdims=False)

    q_left, kv_left, o_left = map(
        pick, (query_update_left, key_value_update_left, output_update_left)
    )
    gate_left, up_left, down_left = map(pick, (gate_update_left, up_update_left, down_update_left))
    q_right, kv_right, o_right = map(
        pick, (query_update_right, key_value_update_right, output_update_right)
    )
    gate_right, up_right, down_right = map(
        pick, (gate_update_right, up_update_right, down_update_right)
    )

    def merge(base, left, right, pairs=False):
        return (base.astype(f32) + update_delta(left, right, pairs)).astype(bf16)

    def own_slice(value):
        return lax.dynamic_slice_in_dim(value, mp_place * own_rows, own_rows, 0)

    block_rows = block_width // mp_count
    kv_base_own = lax.dynamic_slice_in_dim(key_value_matrix, mp_place * block_rows, block_rows, 0)
    kv_left_own = lax.dynamic_slice_in_dim(kv_left, mp_place * block_rows, block_rows, 0)
    kv_full = lax.all_gather(
        merge(kv_base_own, kv_left_own, kv_right, True), ("dp", "mp"), axis=0, tiled=True
    )
    q_full = lax.all_gather(merge(query_matrix, q_left, q_right), "dp", axis=0, tiled=True)
    o_full = lax.all_gather(merge(output_matrix, o_left, o_right), "dp", axis=0, tiled=True)

    def spread(shard):
        shape = (dp_count * shard.shape[0], hidden_own)
        return exchange_dp(
            lambda place: lax.dynamic_slice_in_dim(shard, place * hidden_own, hidden_own, 1)
        ).reshape(shape)

    gate_own = spread(merge(gate_matrix, gate_left, gate_right))
    up_own = spread(merge(up_matrix, up_left, up_right))
    down_own = spread(merge(down_matrix, down_left, down_right))
    gate_up_own = jnp.concatenate([gate_own, up_own], axis=1)
    left_block = jnp.concatenate([gate_left, up_left, down_left], axis=1)
    left_all = lax.all_gather(
        lax.dynamic_slice_in_dim(left_block, mp_place * block_rows, block_rows, 0),
        ("dp", "mp"),
        axis=0,
        tiled=True,
    )
    cotangent_own = own_slice(cotangent)
    cotangent_all = gather_all(cotangent_own)

    tokens_wide = relative_rows(tokens).astype(f32)
    query_seq = relative_rows(token_sequence_index)
    query_spots = relative_rows(positions)
    normed_b = rms_norm(tokens_wide, attention_norm_gain).astype(bf16)
    pair_own = dot(normed_b[:own_rows], kv_full)
    spots_own = query_spots[:own_rows]
    outgoing = jnp.concatenate(
        [rotate(pair_own[:, :HEAD_SIZE], spots_own, 1.0), pair_own[:, HEAD_SIZE:]], axis=1
    ).astype(bf16)
    all_pairs = gather_all(outgoing)
    all_places = gather_all(jnp.stack([query_seq[:own_rows], spots_own], axis=1))
    all_seq = all_places[:, 0]
    all_spots = all_places[:, 1]
    all_keys = all_pairs[:, :HEAD_SIZE]
    all_values = all_pairs[:, HEAD_SIZE:]
    queries = dot(normed_b, q_full)
    query_b = rotate(queries.reshape(row_count, head_count, HEAD_SIZE), query_spots, 1.0).astype(
        bf16
    )
    weights_soft = attention_weights(
        query_b, all_keys, query_seq, query_spots, all_seq, all_spots, score_scale
    )
    weights_low = weights_soft.astype(bf16)
    attended = jnp.einsum("hqk,kd->qhd", weights_low, all_values, preferred_element_type=f32)
    attended_b = attended.reshape(row_count, query_cols).astype(bf16)
    branch_own = scatter_mp(dot_cols(attended_b, o_full))
    middle = tokens_wide[:own_rows] + branch_own
    normed2_b = rms_norm(middle, feedforward_norm_gain).astype(bf16)

    normed2_all = gather_all(normed2_b)
    gate_up = dot(normed2_all, gate_up_own)
    gate_act = gate_up[:, :hidden_own]
    up_act = gate_up[:, hidden_own:]
    hidden_grad = dot(cotangent_all, down_own)
    hidden_value, unit_pull = jax.vjp(gated_unit, gate_act, up_act)
    hidden_b = hidden_value.astype(bf16)
    gate_grad, up_grad = unit_pull(hidden_grad)
    unit_grad_b = jnp.concatenate([gate_grad.astype(bf16), up_grad.astype(bf16)], axis=1)
    normed2_grad = scatter_all(dot_cols(unit_grad_b, gate_up_own))
    mlp_branch = scatter_all(dot_cols(hidden_b, down_own))

    output_rows = middle + mlp_branch
    mixed = natural_rows(gather_mp(output_rows.astype(bf16)))
    confidence_own = jnp.sum(jax.nn.sigmoid(jnp.dot(output_rows, probe, precision=precise)))
    levels = jnp.arange(LOOP_COUNT, dtype=jnp.int32)
    exit_own = own_slice(token_exit_loop)
    depth_own = jnp.sum((exit_own[:, None] == levels[None, :]).astype(f32), axis=0)

    gate_up_grad = dot_rows(normed2_all, unit_grad_b)
    down_grad = dot_rows(cotangent_all, hidden_b)
    rank = gate_left.shape[1]
    rank_own = rank // dp_count

    def collect(grad_cols, left_cols):
        grad_b = grad_cols.astype(bf16)
        right_part = dot_rows(left_cols, grad_b).astype(bf16)
        blocks = jnp.concatenate(
            [
                grad_b.reshape(dp_count, block_width, hidden_own),
                right_part.reshape(dp_count, rank_own, hidden_own),
            ],
            axis=1,
        )
        arrived = exchange_dp(
            lambda place: lax.dynamic_index_in_dim(blocks, place, 0, keepdims=False)
        )
        rows = jnp.swapaxes(arrived, 0, 1).reshape(block_width + rank_own, dp_count * hidden_own)
        return rows[:block_width], rows[block_width:].astype(f32)

    down_weight_b, down_lora_b = collect(down_grad, left_all[:, 2 * rank :])
    gate_weight_b, gate_lora_b = collect(gate_up_grad[:, :hidden_own], left_all[:, :rank])
    up_weight_b, up_lora_b = collect(gate_up_grad[:, hidden_own:], left_all[:, rank : 2 * rank])
    mlp_lora_a = sum_mp(
        jnp.concatenate(
            [
                dot_cols(gate_weight_b, gate_right),
                dot_cols(up_weight_b, up_right),
                dot_cols(down_weight_b, down_right),
            ],
            axis=1,
        )
    )

    unused_norm, mlp_pull = jax.vjp(rms_norm, middle, feedforward_norm_gain)
    middle_norm_grad, mlp_gain_part = mlp_pull(normed2_grad)
    middle_grad = cotangent_own.astype(f32) + middle_norm_grad
    branch_grad_own = middle_grad.astype(bf16)
    branch_grad = gather_mp(branch_grad_own)
    attended_grad_b = (
        dot(branch_grad, o_full).astype(bf16).reshape(row_count, head_count, HEAD_SIZE)
    )
    prob_grad = jnp.einsum("qhd,kd->hqk", attended_grad_b, all_values, preferred_element_type=f32)
    score_grad_b = (
        weights_soft * (prob_grad - jnp.sum(prob_grad * weights_soft, axis=-1, keepdims=True))
    ).astype(bf16)
    keys_grad = (
        jnp.einsum("hqk,qhd->kd", score_grad_b, query_b, preferred_element_type=f32) * score_scale
    )
    values_grad = jnp.einsum(
        "hqk,qhd->kd", weights_low, attended_grad_b, preferred_element_type=f32
    )
    pair_grad_own = scatter_all(jnp.concatenate([keys_grad, values_grad], axis=1))
    pair_grad_b = jnp.concatenate(
        [rotate(pair_grad_own[:, :HEAD_SIZE], spots_own, -1.0), pair_grad_own[:, HEAD_SIZE:]],
        axis=1,
    ).astype(bf16)
    query_grad = (
        jnp.einsum("hqk,kd->qhd", score_grad_b, all_keys, preferred_element_type=f32) * score_scale
    )
    query_grad_b = (
        rotate(query_grad, query_spots, -1.0).reshape(row_count, query_cols).astype(bf16)
    )
    normed_grad = scatter_mp(dot_cols(query_grad_b, q_full)) + dot_cols(pair_grad_b, kv_full)
    unused_first, attn_pull = jax.vjp(rms_norm, tokens_wide[:own_rows], attention_norm_gain)
    inputs_norm_grad, attn_gain_part = attn_pull(normed_grad)
    tokens_grad = natural_rows(gather_mp(middle_grad + inputs_norm_grad))

    def all_token_cols(rows_own):
        arrived = exchange_dp(
            lambda place: lax.dynamic_slice_in_dim(rows_own, place * block_width, block_width, 1)
        )
        arrived = gather_mp(arrived.reshape(dp_count * own_rows, block_width))
        arrived = arrived.reshape(mp_count, dp_count, own_rows, block_width)
        return jnp.swapaxes(arrived, 0, 1).reshape(dp_count * row_count, block_width)

    normed_cols = all_token_cols(normed_b[:own_rows])
    branch_cols = all_token_cols(branch_grad_own)
    attended_all = lax.all_gather(attended_b, "dp", axis=0, tiled=True)
    query_grad_all = lax.all_gather(query_grad_b, "dp", axis=0, tiled=True)
    pair_grad_all = lax.all_gather(pair_grad_b, "dp", axis=0, tiled=True)
    pair_grad_all = gather_mp(pair_grad_all).reshape(mp_count, dp_count, own_rows, -1)
    pair_grad_all = jnp.swapaxes(pair_grad_all, 0, 1).reshape(dp_count * row_count, -1)
    q_weight_grad = dot_rows(normed_cols, query_grad_all)
    kv_weight_grad = dot_rows(normed_cols, pair_grad_all)
    o_weight_grad = dot_rows(branch_cols, attended_all)
    q_weight_b = q_weight_grad.astype(bf16)
    kv_weight_b = kv_weight_grad.astype(bf16)
    o_weight_b = o_weight_grad.astype(bf16)
    qo_lora_a = sum_mp(
        jnp.concatenate([dot_cols(q_weight_b, q_right), dot_cols(o_weight_b, o_right)], axis=1)
    )
    kv_lora_a = jnp.concatenate(
        [
            dot_cols(kv_weight_b[:, :HEAD_SIZE], kv_right[:, :HEAD_SIZE]),
            dot_cols(kv_weight_b[:, HEAD_SIZE:], kv_right[:, HEAD_SIZE:]),
        ],
        axis=1,
    )
    right_parts = jnp.concatenate(
        [
            dot_rows(q_left, q_weight_b),
            dot_rows(o_left, o_weight_b),
            dot_rows(kv_left[:, :rank], kv_weight_b[:, :HEAD_SIZE]),
            dot_rows(kv_left[:, rank:], kv_weight_b[:, HEAD_SIZE:]),
        ],
        axis=1,
    ).astype(bf16)
    right_grads = jnp.sum(
        exchange_dp(
            lambda place: lax.dynamic_slice_in_dim(right_parts, place * rank_own, rank_own, 0)
        ).astype(f32),
        axis=0,
    )

    small = sum_all(
        jnp.concatenate([attn_gain_part, mlp_gain_part, depth_own, confidence_own.reshape(1)])
    )
    gain_width = model_width // dp_count
    attn_gain_grad = lax.dynamic_slice_in_dim(small, dp_place * gain_width, gain_width, 0)
    mlp_gain_grad = lax.dynamic_slice_in_dim(
        small, model_width + dp_place * gain_width, gain_width, 0
    )
    counts = small[2 * model_width : 2 * model_width + LOOP_COUNT].astype(jnp.int32)
    confidence = small[2 * model_width + LOOP_COUNT :] / (row_count * dp_count)

    def place_loop(grad_item):
        empty = jnp.zeros((LOOP_COUNT,) + grad_item.shape, f32)
        return lax.dynamic_update_index_in_dim(empty, grad_item, loop_selection, 0)

    return (
        counts,
        confidence,
        mixed,
        tokens_grad,
        attn_gain_grad,
        mlp_gain_grad,
        q_weight_grad,
        kv_weight_grad,
        o_weight_grad,
        gate_weight_b.astype(f32),
        up_weight_b.astype(f32),
        down_weight_b.astype(f32),
        place_loop(qo_lora_a[:, :rank]),
        place_loop(right_grads[:, :query_cols]),
        place_loop(kv_lora_a),
        place_loop(right_grads[:, 2 * query_cols :]),
        place_loop(qo_lora_a[:, rank:]),
        place_loop(right_grads[:, query_cols : 2 * query_cols]),
        place_loop(mlp_lora_a[:, :rank]),
        place_loop(gate_lora_b),
        place_loop(mlp_lora_a[:, rank : 2 * rank]),
        place_loop(up_lora_b),
        place_loop(mlp_lora_a[:, 2 * rank :]),
        place_loop(down_lora_b),
    )


def solution(mesh):
    return jax.shard_map(
        body,
        mesh=mesh,
        in_specs=(
            P("dp", None),
            P("dp", None),
            P("dp"),
            P("dp"),
            P("dp"),
            P(),
            P(),
            P(),
            P(),
            P("dp", "mp"),
            P("dp", None),
            P("dp", "mp"),
            P("dp", "mp"),
            P("dp", "mp"),
            P("dp", "mp"),
            P(None, "dp", None),
            P(None, None, "mp"),
            P(None, "dp", None),
            P(),
            P(None, "dp", None),
            P(None, None, "mp"),
            P(None, "dp", None),
            P(None, None, "mp"),
            P(None, "dp", None),
            P(None, None, "mp"),
            P(None, "dp", None),
            P(None, None, "mp"),
        ),
        out_specs=(
            P(),
            P(),
            P("dp", None),
            P("dp", None),
            P("dp"),
            P("dp"),
            P("dp", "mp"),
            P("dp", None),
            P("dp", "mp"),
            P("dp", "mp"),
            P("dp", "mp"),
            P("dp", "mp"),
            P(None, "dp", None),
            P(None, "dp", "mp"),
            P(None, "dp", None),
            P(None, "dp", None),
            P(None, "dp", None),
            P(None, "dp", "mp"),
            P(None, "dp", None),
            P(None, "dp", "mp"),
            P(None, "dp", None),
            P(None, "dp", "mp"),
            P(None, "dp", None),
            P(None, "dp", "mp"),
        ),
        check_vma=False,
    )
```

time: 5240 us -> 1120 us (0.21)
  waiting for transfers between devices: 4820 us -> 400 us
  starting transfers between devices: 1.76 us -> 228 us
  local copies, waits for them, and re-layouts: 61.2 us -> 217 us
  matrix products: 232 us -> 136 us
  other arithmetic: 24.5 us -> 79.5 us
    unnamed x20 -> x6, waiting for transfers between devices: 3310 us -> 0.1 us
    all_gather x7 -> x6, waiting for transfers between devices: 803 us -> 18.3 us  [the longest x1 18.3 us: body(): lax.all_gather(merge(output_matrix, o_left, o_right), 'dp', axis=0, tiled...]
    reduce_scatter x6 -> x0, waiting for transfers between devices: 507 us -> none  [the longest x1 135 us: body(): lax.psum_scatter(pair_grad, ('mp', 'dp'), scatter_dimension=0, tiled=True)]
    ppermute x0 -> x137, waiting for transfers between devices: none -> 381 us  [swap(): lax.ppermute(value, axis, [(place, place ^ bit) for place in range(count)])]
    ppermute x0 -> x137, starting transfers between devices: none -> 227 us  [swap(): lax.ppermute(value, axis, [(place, place ^ bit) for place in range(count)])]
    psum x3 -> x0, waiting for transfers between devices: 203 us -> none  [the longest x1 120 us: body(): mlp_branch = lax.psum(output_part, 'mp')]
    dynamic_update_slice x0 -> x70, local copies, waits for them, and re-layouts: none -> 107 us  [the longest x63 102 us: exchange_dp(): result = lax.dynamic_update_index_in_dim(result, arrived, place, 0)]
    dot_general x33 -> x30, matrix products: 194 us -> 104 us  [the longest x12 38.8 us: dot_cols(): lax.dot_general(left, right, (((1,), (1,)), ((), ())), preferred_element_...]
  transfers between devices with their start and end apart: 18 -> 143, of which waited for: 18 -> 71; matrix products, arithmetic and copies ran while one was open for 3% -> 36% of each run, Pallas kernels for 0% -> 0%
where the time goes in v1:
time: 1120 us; the launch traced here: 1110 us
  waiting for transfers between devices  400 us (36%)
  starting transfers between devices  228 us (20%)
  local copies, waits for them, and re-layouts  217 us (19%)
  matrix products  136 us (12%)
  other arithmetic  79.5 us (7%)
  blocking collectives  32.3 us (3%)
  between operations  20.7 us (2%)
    ppermute x137, waiting for transfers between devices, swap(): lax.ppermute(value, axis, [(place, place ^ bit) for place in range(count)])  381 us
    ppermute x137, starting transfers between devices, swap(): lax.ppermute(value, axis, [(place, place ^ bit) for place in range(count)])  227 us
    dynamic_update_slice x63, local copies, waits for them, and re-layouts, exchange_dp(): result = lax.dynamic_update_index_in_dim(result, arrived, place, 0)  102 us
    unnamed x273, local copies, waits for them, and re-layouts  40.1 us
    dot_general x12, matrix products, dot_cols(): lax.dot_general(left, right, (((1,), (1,)), ((), ())), preferred_element_...  38.8 us
    dot_general x12, matrix products, dot_rows(): lax.dot_general(left, right, (((0,), (0,)), ((), ())), preferred_element_...  32.7 us
    all_gather x1, blocking collectives, body(): pair_grad_all = lax.all_gather(pair_grad_b, 'dp', axis=0, tiled=True)  32.3 us
    dot_general x5, matrix products, dot(): return jnp.dot(left, right, preferred_element_type=f32)  32.1 us
  transfers between devices with their start and end apart: 143, of which 71 were waited for; matrix products, arithmetic and copies ran while one was open for 36% of the time, Pallas kernels for 0%

profile of v1, /device:TPU:0, one launch (start us, length us, event | category | flops | bytes accessed | tf_op | source)
XLA Modules:
  0.0 1113.1 jit_solution(17381532164922736431)
XLA Ops:
  17.7 4.0 collective-permute-start.14
  26.9 4.8 collective-permute-start.37
  85.2 9.5 collective-permute-start.87
  96.5 3.9 collective-permute-start.88
  116.5 5.1 collective-permute-start.40
  129.9 13.2 %collective-permute-done = bf16[64,512]{1,0:T(8,128)(2,1)S(1)} collective-permute-done((bf16[64,512]{1,0:T(8,128)(2,1)S(1)}, bf16[64,512]{1,0:T(8,128)(2,1)S(1)}, u32[]{:S(2)}, u32[]{:S(2)}) %collective-permute-start) | collective-permute-done | bytes 65568 | tf_op jit(solution)/shard_map/ppermute | solution.py:93
  152.2 4.4 collective-permute-done.4
  158.9 7.0 collective-permute-done.5
  180.8 4.6 fusion.237
  189.2 18.3 %all-gather.11.cloned.1.call-done = bf16[2048,512]{1,0:T(8,128)(2,1)} async-done(((bf16[256,512]{1,0:T(8,128)(2,1)}), bf16[2048,512]{1,0:T(8,128)(2,1)}) %all-gather.11.cloned.1.call-update) | async-done | bytes 2097168 | tf_op jit(solution)/shard_map/all_gather | solution.py:263
  221.8 9.1 collective-permute-done.15
  242.1 34.1 %collective-permute-done.18 = bf16[128,2048]{1,0:T(8,128)(2,1)S(1)} collective-permute-done((bf16[128,2048]{1,0:T(8,128)(2,1)S(1)}, bf16[128,2048]{1,0:T(8,128)(2,1)S(1)}, u32[]{:S(2)}, u32[]{:S(2)}) %collective-permute-start.18) | collective-permute-done | bytes 524320 | tf_op jit(solution)/shard_map/ppermute | solution.py:93
  282.3 6.7 collective-permute-done.33
  292.2 24.6 %collective-permute-done.31 = bf16[128,2048]{1,0:T(8,128)(2,1)S(1)} collective-permute-done((bf16[128,2048]{1,0:T(8,128)(2,1)S(1)}, bf16[128,2048]{1,0:T(8,128)(2,1)S(1)}, u32[]{:S(2)}, u32[]{:S(2)}) %collective-permute-start.31) | collective-permute-done | bytes 524320 | tf_op jit(solution)/shard_map/ppermute | solution.py:93
  320.7 11.0 collective-permute-done.34
  334.0 16.7 %collective-permute-done.32 = bf16[256,2048]{1,0:T(8,128)(2,1)S(1)} collective-permute-done((bf16[256,2048]{1,0:T(8,128)(2,1)S(1)}, bf16[256,2048]{1,0:T(8,128)(2,1)S(1)}, u32[]{:S(2)}, u32[]{:S(2)}) %collective-permute-start.32) | collective-permute-done | bytes 1048608 | tf_op jit(solution)/shard_map/ppermute | solution.py:93
  363.3 4.3 collective-permute-done.48
  370.6 8.3 collective-permute-done.49
  380.9 17.3 %collective-permute-start.24 = (bf16[256,512]{1,0:T(8,128)(2,1)S(1)}, bf16[256,512]{1,0:T(8,128)(2,1)S(1)}, u32[]{:S(2)}, u32[]{:S(2)}) collective-permute-start(bf16[256,512]{1,0:T(8,128)(2,1)S(1)} %copy-done.71), channel_id=1, source_target_pairs={{0,4},{1,5},{2,6},{3,7},{4,0},{5,1},{6,2},{7,3},{8,12},{9,13},{10,... | collective-permute-start | bytes 786440 | tf_op jit(solution)/shard_map/ppermute | solution.py:93
  398.2 8.8 collective-permute-start.25
  407.0 5.1 collective-permute-done.23
  414.5 4.0 collective-permute-done.92
  429.2 5.1 constant_dynamic-update-slice_fusion.22
  441.3 14.9 %fusion.17 = f32[2048,1024]{0,1:T(8,128)} fusion(bf16[2048,2048]{1,0:T(8,128)(2,1)} %copy-done.94, bf16[2048,512]{1,0:T(8,128)(2,1)} %bitcast.50, bf16[2048,512]{1,0:T(8,128)(2,1)} %bitcast.39), kind=kOutput, calls=%fused_computation.65 | convolution fusion | flops 8598323200 | bytes 20971520 | tf_op jit(solution)/shard_map/dot_general | solution.py:80
  456.2 11.4 %fusion.10 = (bf16[2048,512]{0,1:T(8,128)(2,1)}, bf16[2048,512]{0,1:T(8,128)(2,1)}, bf16[2048,512]{0,1:T(8,128)(2,1)S(1)}) fusion(f32[2048,1024]{0,1:T(8,128)} %fusion.17, bf16[2048,2048]{1,0:T(8,128)(2,1)S(1)} %bitcast.476, bf16[2048,512]{1,0:T(8,128)(2,1)S(1)} %bitcast.444), kind=kOutput, calls=%fused_computation.43 | convolution fusion | flops 4322230272 | bytes 25165824 | tf_op jit(solution)/shard_map/dot_general | solution.py:80
  467.6 5.4 convolution_convert_fusion.1
  473.0 8.5 fusion.242
  481.5 12.7 %convolution_convert_fusion = bf16[2048,1024]{1,0:T(8,128)(2,1)} fusion(bf16[2048,2048]{1,0:T(8,128)(2,1)} %copy-done.94, bf16[2048,512]{0,1:T(8,128)(2,1)S(1)} %copy-done.123, bf16[2048,512]{0,1:T(8,128)(2,1)S(1)} %copy-done.122), kind=kOutput, calls=%fused_computation.58 | convolution fusion | flops 8600420352 | bytes 16777216 | tf_op jit(solution)/shard_map/dot_general | solution.py:84
  494.2 14.7 %fusion.16 = f32[2048,2048]{1,0:T(8,128)} fusion(bf16[2048,512]{0,1:T(8,128)(2,1)S(1)} %copy-done.123, bf16[2048,512]{0,1:T(8,128)(2,1)S(1)} %copy-done.122, bf16[2048,512]{1,0:T(8,128)(2,1)} %bitcast.50, bf16[2048,512]{1,0:T(8,128)(2,1)} %bitcast.39), kind=kOutput, calls=%fused_computation.64 | convolution fusion | flops 8606711808 | bytes 25165824 | tf_op jit(solution)/shard_map/dot_general | solution.py:88
  524.5 6.1 slice.705
  530.6 6.0 slice.706
  536.7 11.0 collective-permute-start.124
  548.4 11.5 %collective-permute-done.121 = bf16[288,512]{1,0:T(8,128)(2,1)S(1)} collective-permute-done((bf16[288,512]{1,0:T(8,128)(2,1)S(1)}, bf16[288,512]{1,0:T(8,128)(2,1)S(1)}, u32[]{:S(2)}, u32[]{:S(2)}) %collective-permute-start.121) | collective-permute-done | bytes 294944 | tf_op jit(solution)/shard_map/ppermute | solution.py:93
  575.8 23.0 %collective-permute-start.117 = (bf16[288,512]{1,0:T(8,128)(2,1)S(1)}, bf16[288,512]{1,0:T(8,128)(2,1)S(1)}, u32[]{:S(2)}, u32[]{:S(2)}) collective-permute-start(bf16[288,512]{1,0:T(8,128)(2,1)S(1)} %get-tuple-element.73), channel_id=1, source_target_pairs={{0,2},{1,3},{2,0},{3,1},{4,6},{5,7},{6,4},{7,5},{8,10},{9,11},{10,... | collective-permute-start | bytes 884744 | tf_op jit(solution)/shard_map/ppermute | solution.py:93
  599.2 11.8 %collective-permute-done.114 = bf16[288,512]{1,0:T(8,128)(2,1)S(1)} collective-permute-done((bf16[288,512]{1,0:T(8,128)(2,1)S(1)}, bf16[288,512]{1,0:T(8,128)(2,1)S(1)}, u32[]{:S(2)}, u32[]{:S(2)}) %collective-permute-start.114) | collective-permute-done | bytes 294944 | tf_op jit(solution)/shard_map/ppermute | solution.py:93
  620.0 14.4 %collective-permute-done.109 = bf16[288,512]{1,0:T(8,128)(2,1)S(1)} collective-permute-done((bf16[288,512]{1,0:T(8,128)(2,1)S(1)}, bf16[288,512]{1,0:T(8,128)(2,1)S(1)}, u32[]{:S(2)}, u32[]{:S(2)}) %collective-permute-start.109) | collective-permute-done | bytes 294944 | tf_op jit(solution)/shard_map/ppermute | solution.py:93
  634.5 15.6 %collective-permute-start.110 = (bf16[288,512]{1,0:T(8,128)(2,1)S(1)}, bf16[288,512]{1,0:T(8,128)(2,1)S(1)}, u32[]{:S(2)}, u32[]{:S(2)}) collective-permute-start(bf16[288,512]{1,0:T(8,128)(2,1)S(1)} %get-tuple-element.81), channel_id=1, source_target_pairs={{0,2},{1,3},{2,0},{3,1},{4,6},{5,7},{6,4},{7,5},{8,10},{9,11},{10,... | collective-permute-start | bytes 884744 | tf_op jit(solution)/shard_map/ppermute | solution.py:93
  655.4 6.8 collective-permute-done.107
  669.5 12.1 %dynamic_update_slice.301 = bf16[8,288,512]{2,0,1:T(8,128)(2,1)} dynamic-update-slice(bf16[8,288,512]{2,0,1:T(8,128)(2,1)} %copy.170, bf16[1,288,512]{2,0,1:T(2,128)(2,1)} %copy.171, s32[]{:T(128)S(6)} %select_n.312, s32[]{:T(128)} %constant.341.clone.1, s32[]{:T(128)} %constant.341.clone.1) | dynamic-update-slice | bytes 589828 | tf_op jit(solution)/shard_map/jit(dynamic_update_index_in_dim)/dynamic_update_slice | solution.py:167
  681.6 12.1 %dynamic_update_slice.302 = bf16[8,288,512]{2,0,1:T(8,128)(2,1)} dynamic-update-slice(bf16[8,288,512]{2,0,1:T(8,128)(2,1)} %dynamic_update_slice.301, bf16[1,288,512]{2,0,1:T(2,128)(2,1)} %copy.172, s32[]{:T(128)S(6)} %select_n.314, s32[]{:T(128)} %constant.341.clone.1, s32[]{:T(128)} %constant.341.clone.1) | dynamic-update-slice | bytes 589828 | tf_op jit(solution)/shard_map/jit(dynamic_update_index_in_dim)/dynamic_update_slice | solution.py:167
  693.8 12.1 %dynamic_update_slice.303 = bf16[8,288,512]{2,0,1:T(8,128)(2,1)} dynamic-update-slice(bf16[8,288,512]{2,0,1:T(8,128)(2,1)} %dynamic_update_slice.302, bf16[1,288,512]{2,0,1:T(2,128)(2,1)} %copy.173, s32[]{:T(128)S(6)} %select_n.316, s32[]{:T(128)} %constant.341.clone.1, s32[]{:T(128)} %constant.341.clone.1) | dynamic-update-slice | bytes 589828 | tf_op jit(solution)/shard_map/jit(dynamic_update_index_in_dim)/dynamic_update_slice | solution.py:167
  705.9 12.1 %dynamic_update_slice.304 = bf16[8,288,512]{2,0,1:T(8,128)(2,1)} dynamic-update-slice(bf16[8,288,512]{2,0,1:T(8,128)(2,1)} %dynamic_update_slice.303, bf16[1,288,512]{2,0,1:T(2,128)(2,1)} %copy.174, s32[]{:T(128)S(6)} %select_n.318, s32[]{:T(128)} %constant.341.clone.1, s32[]{:T(128)} %constant.341.clone.1) | dynamic-update-slice | bytes 589828 | tf_op jit(solution)/shard_map/jit(dynamic_update_index_in_dim)/dynamic_update_slice | solution.py:167
  718.0 12.1 %dynamic_update_slice.305 = bf16[8,288,512]{2,0,1:T(8,128)(2,1)} dynamic-update-slice(bf16[8,288,512]{2,0,1:T(8,128)(2,1)} %dynamic_update_slice.304, bf16[1,288,512]{2,0,1:T(2,128)(2,1)S(1)} %copy.175, s32[]{:T(128)S(6)} %select_n.320, s32[]{:T(128)} %constant.341.clone.1, s32[]{:T(128)} %constant.341.clone.1) | dynamic-update-slice | bytes 589828 | tf_op jit(solution)/shard_map/jit(dynamic_update_index_in_dim)/dynamic_update_slice | solution.py:167
  730.1 12.1 %dynamic_update_slice.306 = bf16[8,288,512]{2,0,1:T(8,128)(2,1)} dynamic-update-slice(bf16[8,288,512]{2,0,1:T(8,128)(2,1)} %dynamic_update_slice.305, bf16[1,288,512]{2,0,1:T(2,128)(2,1)} %copy.176, s32[]{:T(128)S(6)} %select_n.322, s32[]{:T(128)} %constant.341.clone.1, s32[]{:T(128)} %constant.341.clone.1) | dynamic-update-slice | bytes 589828 | tf_op jit(solution)/shard_map/jit(dynamic_update_index_in_dim)/dynamic_update_slice | solution.py:167
  742.3 12.3 %dynamic_update_slice.307 = bf16[8,288,512]{2,0,1:T(8,128)(2,1)} dynamic-update-slice(bf16[8,288,512]{2,0,1:T(8,128)(2,1)} %dynamic_update_slice.306, bf16[1,288,512]{2,0,1:T(2,128)(2,1)} %copy.177, s32[]{:T(128)S(6)} %select_n.324, s32[]{:T(128)} %constant.341.clone.1, s32[]{:T(128)} %constant.341.clone.1) | dynamic-update-slice | bytes 589828 | tf_op jit(solution)/shard_map/jit(dynamic_update_index_in_dim)/dynamic_update_slice | solution.py:167
  786.0 9.6 collective-permute-done.136
  795.8 10.2 fusion.225
  810.0 10.2 fusion.220
  823.8 9.9 collective-permute-done.52
  839.4 16.9 %collective-permute-done.70 = bf16[256,2048]{1,0:T(8,128)(2,1)} collective-permute-done((bf16[256,2048]{1,0:T(8,128)(2,1)}, bf16[256,2048]{1,0:T(8,128)(2,1)}, u32[]{:S(2)}, u32[]{:S(2)}) %collective-permute-start.70) | collective-permute-done | bytes 1048608 | tf_op jit(solution)/shard_map/ppermute | solution.py:93
  862.5 4.9 collective-permute-done.55
  869.9 7.5 collective-permute-done.73
  884.0 11.9 %collective-permute-done.74 = bf16[128,2048]{1,0:T(8,128)(2,1)S(1)} collective-permute-done((bf16[128,2048]{1,0:T(8,128)(2,1)S(1)}, bf16[128,2048]{1,0:T(8,128)(2,1)S(1)}, u32[]{:S(2)}, u32[]{:S(2)}) %collective-permute-start.74) | collective-permute-done | bytes 524320 | tf_op jit(solution)/shard_map/ppermute | solution.py:93
  896.5 12.4 %collective-permute-done.75 = bf16[64,2048]{1,0:T(8,128)(2,1)S(1)} collective-permute-done((bf16[64,2048]{1,0:T(8,128)(2,1)S(1)}, bf16[64,2048]{1,0:T(8,128)(2,1)S(1)}, u32[]{:S(2)}, u32[]{:S(2)}) %collective-permute-start.75) | collective-permute-done | bytes 262176 | tf_op jit(solution)/shard_map/ppermute | solution.py:93
  927.5 5.2 collective-permute-done.81
  941.8 5.3 convolution_bitcast_fusion
  962.5 6.2 collective-permute-done.63
  985.3 7.4 collective-permute-done.68
  993.1 32.3 %all_gather.25 = bf16[512,512]{1,0:T(8,128)(2,1)S(1)} all-gather(bf16[64,512]{1,0:T(8,128)(2,1)S(1)} %pad_maximum_fusion.41), channel_id=1, replica_groups=mesh['mp'=4,'dp'=8] {'dp'}, dimensions={0}, use_global_device_ids=true | all-gather | bytes 589824 | tf_op jit(solution)/shard_map/all_gather | solution.py:414
  1036.5 3.8 collective-permute-done.78
  1044.4 4.4 collective-permute-done.80
  1051.2 4.9 collective-permute-done.83
  1080.1 8.9 collective-permute-start.133
  1095.5 7.6 collective-permute-done.127
  (827 shorter events, 424.3 us)
Async XLA Ops:
  7.2 118.0 %all-gather.7.cloned.1.call-start = ((), (), s32[]{:S(2)}) async-start(), calls=%async_computation | async-start | bytes 2162688 | tf_op jit(solution)/shard_map/all_gather | solution.py:259
  11.9 158.5 %all-gather.9.cloned.1.call-start = ((), (), s32[]{:S(2)}) async-start(), calls=%async_computation.1 | async-start | bytes 2359296 | tf_op jit(solution)/shard_map/all_gather | solution.py:262
  14.0 193.5 %all-gather.11.cloned.1.call-start = ((), (), s32[]{:S(2)}) async-start(), calls=%async_computation.2 | async-start | bytes 2359296 | tf_op jit(solution)/shard_map/all_gather | solution.py:263
  15.9 493.0 %all-gather.17.cloned.1.call-start = ((), (), s32[]{:S(2)}) async-start(), calls=%async_computation.5 | async-start | bytes 3244032 | tf_op jit(solution)/shard_map/all_gather | solution.py:276
  17.7 103.9 %collective-permute-start.14 = (bf16[64,2048]{1,0:T(8,128)(2,1)S(1)}, bf16[64,2048]{1,0:T(8,128)(2,1)}, u32[]{:S(2)}, u32[]{:S(2)}) collective-permute-start(bf16[64,2048]{1,0:T(8,128)(2,1)S(1)} %get-tuple-element.39), channel_id=1, source_target_pairs={{0,4},{1,5},{2,6},{3,7},{4,0},{5,1},{6,2},{7,3},{8,12},{9,13},{10,... | collective-permute-start | bytes 786440 | tf_op jit(solution)/shard_map/ppermute | solution.py:93
  22.4 36.8 %collective-permute-start.7 = (s32[64,2]{0,1:T(2,128)S(1)}, s32[64,2]{0,1:T(2,128)S(1)}, u32[]{:S(2)}, u32[]{:S(2)}) collective-permute-start(s32[64,2]{0,1:T(2,128)S(1)} %pad_add_fusion.3), channel_id=1, source_target_pairs={{0,4},{1,5},{2,6},{3,7},{4,0},{5,1},{6,2},{7,3},{8,12},{9,13},{10,... | collective-permute-start | bytes 1544 | tf_op jit(solution)/shard_map/ppermute | solution.py:93
  26.9 101.3 %collective-permute-start.37 = (bf16[256,512]{1,0:T(8,128)(2,1)}, bf16[256,512]{1,0:T(8,128)(2,1)}, u32[]{:S(2)}, u32[]{:S(2)}) collective-permute-start(bf16[256,512]{1,0:T(8,128)(2,1)} %get-tuple-element.96), channel_id=1, source_target_pairs={{0,7},{1,6},{2,5},{3,4},{4,3},{5,2},{6,1},{7,0},{8,15},{9,14},{10,... | collective-permute-start | bytes 786440 | tf_op jit(solution)/shard_map/ppermute | solution.py:93
  31.7 112.0 %collective-permute-start.38 = (bf16[256,512]{1,0:T(8,128)(2,1)}, bf16[256,512]{1,0:T(8,128)(2,1)}, u32[]{:S(2)}, u32[]{:S(2)}) collective-permute-start(bf16[256,512]{1,0:T(8,128)(2,1)} %get-tuple-element.95), channel_id=1, source_target_pairs={{0,6},{1,7},{2,4},{3,5},{4,2},{5,3},{6,0},{7,1},{8,14},{9,15},{10,... | collective-permute-start | bytes 786440 | tf_op jit(solution)/shard_map/ppermute | solution.py:93
  34.5 995.4 %all-gather.15.cloned.1.call-start = ((), (), s32[]{:S(2)}) async-start(), calls=%async_computation.4 | async-start | bytes 2359296 | tf_op jit(solution)/shard_map/all_gather | solution.py:412
  68.0 100.4 %collective-permute-start.39 = (bf16[256,512]{1,0:T(8,128)(2,1)}, bf16[256,512]{1,0:T(8,128)(2,1)S(1)}, u32[]{:S(2)}, u32[]{:S(2)}) collective-permute-start(bf16[256,512]{1,0:T(8,128)(2,1)} %get-tuple-element.94), channel_id=1, source_target_pairs={{0,5},{1,4},{2,7},{3,6},{4,1},{5,0},{6,3},{7,2},{8,13},{9,12},{10,... | collective-permute-start | bytes 786440 | tf_op jit(solution)/shard_map/ppermute | solution.py:93
  116.5 93.5 %collective-permute-start.40 = (bf16[256,512]{1,0:T(8,128)(2,1)}, bf16[256,512]{1,0:T(8,128)(2,1)}, u32[]{:S(2)}, u32[]{:S(2)}) collective-permute-start(bf16[256,512]{1,0:T(8,128)(2,1)} %get-tuple-element.93), channel_id=1, source_target_pairs={{0,4},{1,5},{2,6},{3,7},{4,0},{5,1},{6,2},{7,3},{8,12},{9,13},{10,... | collective-permute-start | bytes 786440 | tf_op jit(solution)/shard_map/ppermute | solution.py:93
  121.6 90.3 %collective-permute-start.41 = (bf16[256,512]{1,0:T(8,128)(2,1)}, bf16[256,512]{1,0:T(8,128)(2,1)}, u32[]{:S(2)}, u32[]{:S(2)}) collective-permute-start(bf16[256,512]{1,0:T(8,128)(2,1)} %get-tuple-element.92), channel_id=1, source_target_pairs={{0,3},{1,2},{2,1},{3,0},{4,7},{5,6},{6,5},{7,4},{8,11},{9,10},{10,... | collective-permute-start | bytes 786440 | tf_op jit(solution)/shard_map/ppermute | solution.py:93
  156.5 59.7 %collective-permute-start.42 = (bf16[256,512]{1,0:T(8,128)(2,1)}, bf16[256,512]{1,0:T(8,128)(2,1)}, u32[]{:S(2)}, u32[]{:S(2)}) collective-permute-start(bf16[256,512]{1,0:T(8,128)(2,1)} %get-tuple-element.91), channel_id=1, source_target_pairs={{0,2},{1,3},{2,0},{3,1},{4,6},{5,7},{6,4},{7,5},{8,10},{9,11},{10,... | collective-permute-start | bytes 786440 | tf_op jit(solution)/shard_map/ppermute | solution.py:93
  165.9 52.7 %collective-permute-start.43 = (bf16[256,512]{1,0:T(8,128)(2,1)}, bf16[256,512]{1,0:T(8,128)(2,1)}, u32[]{:S(2)}, u32[]{:S(2)}) collective-permute-start(bf16[256,512]{1,0:T(8,128)(2,1)} %get-tuple-element.90), channel_id=1, source_target_pairs={{0,1},{1,0},{2,3},{3,2},{4,5},{5,4},{6,7},{7,6},{8,9},{9,8},{10,11... | collective-permute-start | bytes 786440 | tf_op jit(solution)/shard_map/ppermute | solution.py:93
  175.2 179.7 %collective-permute-start.44 = (bf16[256,512]{1,0:T(8,128)(2,1)S(1)}, bf16[256,512]{1,0:T(8,128)(2,1)S(1)}, u32[]{:S(2)}, u32[]{:S(2)}) collective-permute-start(bf16[256,512]{1,0:T(8,128)(2,1)S(1)} %copy-done.81), channel_id=1, source_target_pairs={{0,7},{1,6},{2,5},{3,4},{4,3},{5,2},{6,1},{7,0},{8,15},{9,14},{10,... | collective-permute-start | bytes 786440 | tf_op jit(solution)/shard_map/ppermute | solution.py:93
  211.8 144.3 %collective-permute-start.45 = (bf16[256,512]{1,0:T(8,128)(2,1)S(1)}, bf16[256,512]{1,0:T(8,128)(2,1)S(1)}, u32[]{:S(2)}, u32[]{:S(2)}) collective-permute-start(bf16[256,512]{1,0:T(8,128)(2,1)S(1)} %copy-done.80), channel_id=1, source_target_pairs={{0,6},{1,7},{2,4},{3,5},{4,2},{5,3},{6,0},{7,1},{8,14},{9,15},{10,... | collective-permute-start | bytes 786440 | tf_op jit(solution)/shard_map/ppermute | solution.py:93
  218.6 18.5 %collective-permute-start.29 = (bf16[64,2048]{1,0:T(8,128)(2,1)S(1)}, bf16[64,2048]{1,0:T(8,128)(2,1)S(1)}, u32[]{:S(2)}, u32[]{:S(2)}) collective-permute-start(bf16[64,2048]{1,0:T(8,128)(2,1)S(1)} %slice.716), channel_id=1, source_target_pairs={{0,16},{8,24},{16,0},{24,8},{1,17},{9,25},{17,1},{25,9},{2,18},{10... | collective-permute-start | bytes 786440 | tf_op jit(solution)/shard_map/ppermute | solution.py:93
  231.9 45.1 %collective-permute-start.16 = (bf16[256,2048]{1,0:T(8,128)(2,1)S(1)}, bf16[256,2048]{1,0:T(8,128)(2,1)S(1)}, u32[]{:S(2)}, u32[]{:S(2)}) collective-permute-start(bf16[256,2048]{1,0:T(8,128)(2,1)S(1)} %pad_maximum_fusion.10), channel_id=1, source_target_pairs={{0,16},{8,24},{16,0},{24,8},{1,17},{9,25},{17,1},{25,9},{2,18},{10... | collective-permute-start | bytes 3145736 | tf_op jit(solution)/shard_map/ppermute | solution.py:93
  235.7 40.4 %collective-permute-start.18 = (bf16[128,2048]{1,0:T(8,128)(2,1)S(1)}, bf16[128,2048]{1,0:T(8,128)(2,1)S(1)}, u32[]{:S(2)}, u32[]{:S(2)}) collective-permute-start(bf16[128,2048]{1,0:T(8,128)(2,1)S(1)} %collective-permute-done.17), channel_id=1, source_target_pairs={{0,16},{8,24},{16,0},{24,8},{1,17},{9,25},{17,1},{25,9},{2,18},{10... | collective-permute-start | bytes 1572872 | tf_op jit(solution)/shard_map/ppermute | solution.py:93
  240.0 36.9 %collective-permute-start.30 = (bf16[64,2048]{1,0:T(8,128)(2,1)S(1)}, bf16[64,2048]{1,0:T(8,128)(2,1)S(1)}, u32[]{:S(2)}, u32[]{:S(2)}) collective-permute-start(bf16[64,2048]{1,0:T(8,128)(2,1)S(1)} %get-tuple-element.37), channel_id=1, source_target_pairs={{0,4},{1,5},{2,6},{3,7},{4,0},{5,1},{6,2},{7,3},{8,12},{9,13},{10,... | collective-permute-start | bytes 786440 | tf_op jit(solution)/shard_map/ppermute | solution.py:93
  276.3 42.2 %collective-permute-start.19 = (bf16[256,2048]{1,0:T(8,128)(2,1)S(1)}, bf16[256,2048]{1,0:T(8,128)(2,1)S(1)}, u32[]{:S(2)}, u32[]{:S(2)}) collective-permute-start(bf16[256,2048]{1,0:T(8,128)(2,1)S(1)} %pad_maximum_fusion.11), channel_id=1, source_target_pairs={{0,1},{1,0},{2,3},{3,2},{4,5},{5,4},{6,7},{7,6},{8,9},{9,8},{10,11... | collective-permute-start | bytes 3145736 | tf_op jit(solution)/shard_map/ppermute | solution.py:93
  277.0 39.7 %collective-permute-start.31 = (bf16[128,2048]{1,0:T(8,128)(2,1)S(1)}, bf16[128,2048]{1,0:T(8,128)(2,1)S(1)}, u32[]{:S(2)}, u32[]{:S(2)}) collective-permute-start(bf16[128,2048]{1,0:T(8,128)(2,1)S(1)} %pad_maximum_fusion.23), channel_id=1, source_target_pairs={{0,1},{1,0},{2,3},{3,2},{4,5},{5,4},{6,7},{7,6},{8,9},{9,8},{10,11... | collective-permute-start | bytes 1572872 | tf_op jit(solution)/shard_map/ppermute | solution.py:93
  289.1 70.7 %collective-permute-start.46 = (bf16[256,512]{1,0:T(8,128)(2,1)S(1)}, bf16[256,512]{1,0:T(8,128)(2,1)S(1)}, u32[]{:S(2)}, u32[]{:S(2)}) collective-permute-start(bf16[256,512]{1,0:T(8,128)(2,1)S(1)} %copy-done.79), channel_id=1, source_target_pairs={{0,5},{1,4},{2,7},{3,6},{4,1},{5,0},{6,3},{7,2},{8,13},{9,12},{10,... | collective-permute-start | bytes 786440 | tf_op jit(solution)/shard_map/ppermute | solution.py:93
  318.5 32.2 %collective-permute-start.32 = (bf16[256,2048]{1,0:T(8,128)(2,1)S(1)}, bf16[256,2048]{1,0:T(8,128)(2,1)S(1)}, u32[]{:S(2)}, u32[]{:S(2)}) collective-permute-start(bf16[256,2048]{1,0:T(8,128)(2,1)S(1)} %pad_maximum_fusion.12), channel_id=1, source_target_pairs={{0,16},{8,24},{16,0},{24,8},{1,17},{9,25},{17,1},{25,9},{2,18},{10... | collective-permute-start | bytes 3145736 | tf_op jit(solution)/shard_map/ppermute | solution.py:93
  331.8 21.9 %collective-permute-start.35 = (bf16[256,2048]{1,0:T(8,128)(2,1)S(1)}, bf16[256,2048]{1,0:T(8,128)(2,1)S(1)}, u32[]{:S(2)}, u32[]{:S(2)}) collective-permute-start(bf16[256,2048]{1,0:T(8,128)(2,1)S(1)} %pad_maximum_fusion.13), channel_id=1, source_target_pairs={{0,1},{1,0},{2,3},{3,2},{4,5},{5,4},{6,7},{7,6},{8,9},{9,8},{10,11... | collective-permute-start | bytes 3145736 | tf_op jit(solution)/shard_map/ppermute | solution.py:93
  353.6 75.5 %collective-permute-start.20 = (bf16[1024,2048]{1,0:T(8,128)(2,1)}, bf16[1024,2048]{1,0:T(8,128)(2,1)}, u32[]{:S(2)}, u32[]{:S(2)}) collective-permute-start(bf16[1024,2048]{1,0:T(8,128)(2,1)} %get-tuple-element.121), channel_id=1, source_target_pairs={{0,8},{8,0},{16,24},{24,16},{1,9},{9,1},{17,25},{25,17},{2,10},{10... | collective-permute-start | bytes 12582920 | tf_op jit(solution)/shard_map/ppermute | solution.py:93
  354.9 79.4 %collective-permute-start.36 = (bf16[1024,2048]{1,0:T(8,128)(2,1)}, bf16[1024,2048]{1,0:T(8,128)(2,1)}, u32[]{:S(2)}, u32[]{:S(2)}) collective-permute-start(bf16[1024,2048]{1,0:T(8,128)(2,1)} %get-tuple-element.117), channel_id=1, source_target_pairs={{0,8},{8,0},{16,24},{24,16},{1,9},{9,1},{17,25},{25,17},{2,10},{10... | collective-permute-start | bytes 12582920 | tf_op jit(solution)/shard_map/ppermute | solution.py:93
  359.8 19.1 %collective-permute-start.49 = (bf16[256,512]{1,0:T(8,128)(2,1)S(1)}, bf16[256,512]{1,0:T(8,128)(2,1)S(1)}, u32[]{:S(2)}, u32[]{:S(2)}) collective-permute-start(bf16[256,512]{1,0:T(8,128)(2,1)S(1)} %copy-done.76), channel_id=1, source_target_pairs={{0,2},{1,3},{2,0},{3,1},{4,6},{5,7},{6,4},{7,5},{8,10},{9,11},{10,... | collective-permute-start | bytes 786440 | tf_op jit(solution)/shard_map/ppermute | solution.py:93
  378.9 19.3 %collective-permute-start.22 = (bf16[256,512]{1,0:T(8,128)(2,1)S(1)}, bf16[256,512]{1,0:T(8,128)(2,1)S(1)}, u32[]{:S(2)}, u32[]{:S(2)}) collective-permute-start(bf16[256,512]{1,0:T(8,128)(2,1)S(1)} %copy-done.73), channel_id=1, source_target_pairs={{0,6},{1,7},{2,4},{3,5},{4,2},{5,3},{6,0},{7,1},{8,14},{9,15},{10,... | collective-permute-start | bytes 786440 | tf_op jit(solution)/shard_map/ppermute | solution.py:93
  380.1 32.1 %collective-permute-start.23 = (bf16[256,512]{1,0:T(8,128)(2,1)S(1)}, bf16[256,512]{1,0:T(8,128)(2,1)S(1)}, u32[]{:S(2)}, u32[]{:S(2)}) collective-permute-start(bf16[256,512]{1,0:T(8,128)(2,1)S(1)} %copy-done.72), channel_id=1, source_target_pairs={{0,5},{1,4},{2,7},{3,6},{4,1},{5,0},{6,3},{7,2},{8,13},{9,12},{10,... | collective-permute-start | bytes 786440 | tf_op jit(solution)/shard_map/ppermute | solution.py:93
  380.9 33.6 %collective-permute-start.24 = (bf16[256,512]{1,0:T(8,128)(2,1)S(1)}, bf16[256,512]{1,0:T(8,128)(2,1)S(1)}, u32[]{:S(2)}, u32[]{:S(2)}) collective-permute-start(bf16[256,512]{1,0:T(8,128)(2,1)S(1)} %copy-done.71), channel_id=1, source_target_pairs={{0,4},{1,5},{2,6},{3,7},{4,0},{5,1},{6,2},{7,3},{8,12},{9,13},{10,... | collective-permute-start | bytes 786440 | tf_op jit(solution)/shard_map/ppermute | solution.py:93
  398.2 22.3 %collective-permute-start.25 = (bf16[256,512]{1,0:T(8,128)(2,1)S(1)}, bf16[256,512]{1,0:T(8,128)(2,1)S(1)}, u32[]{:S(2)}, u32[]{:S(2)}) collective-permute-start(bf16[256,512]{1,0:T(8,128)(2,1)S(1)} %copy-done.70), channel_id=1, source_target_pairs={{0,3},{1,2},{2,1},{3,0},{4,7},{5,6},{6,5},{7,4},{8,11},{9,10},{10,... | collective-permute-start | bytes 786440 | tf_op jit(solution)/shard_map/ppermute | solution.py:93
  428.6 637.9 %all-gather.13.cloned.1.call-start = ((), (), s32[]{:S(2)}) async-start(), calls=%async_computation.3 | async-start | bytes 2359296 | tf_op jit(solution)/shard_map/all_gather | solution.py:413
  511.0 54.5 %collective-permute-start.123 = (bf16[288,512]{1,0:T(8,128)(2,1)S(1)}, bf16[288,512]{1,0:T(8,128)(2,1)S(1)}, u32[]{:S(2)}, u32[]{:S(2)}) collective-permute-start(bf16[288,512]{1,0:T(8,128)(2,1)S(1)} %get-tuple-element.66), channel_id=1, source_target_pairs={{0,3},{1,2},{2,1},{3,0},{4,7},{5,6},{6,5},{7,4},{8,11},{9,10},{10,... | collective-permute-start | bytes 884744 | tf_op jit(solution)/shard_map/ppermute | solution.py:93
  511.4 25.2 %collective-permute-start.119 = (bf16[288,512]{1,0:T(8,128)(2,1)S(1)}, bf16[288,512]{1,0:T(8,128)(2,1)S(1)}, u32[]{:S(2)}, u32[]{:S(2)}) collective-permute-start(bf16[288,512]{1,0:T(8,128)(2,1)S(1)} %get-tuple-element.61), channel_id=1, source_target_pairs={{0,7},{1,6},{2,5},{3,4},{4,3},{5,2},{6,1},{7,0},{8,15},{9,14},{10,... | collective-permute-start | bytes 884744 | tf_op jit(solution)/shard_map/ppermute | solution.py:93
  511.9 35.8 %collective-permute-start.120 = (bf16[288,512]{1,0:T(8,128)(2,1)S(1)}, bf16[288,512]{1,0:T(8,128)(2,1)S(1)}, u32[]{:S(2)}, u32[]{:S(2)}) collective-permute-start(bf16[288,512]{1,0:T(8,128)(2,1)S(1)} %get-tuple-element.62), channel_id=1, source_target_pairs={{0,6},{1,7},{2,4},{3,5},{4,2},{5,3},{6,0},{7,1},{8,14},{9,15},{10,... | collective-permute-start | bytes 884744 | tf_op jit(solution)/shard_map/ppermute | solution.py:93
  515.1 44.8 %collective-permute-start.121 = (bf16[288,512]{1,0:T(8,128)(2,1)S(1)}, bf16[288,512]{1,0:T(8,128)(2,1)S(1)}, u32[]{:S(2)}, u32[]{:S(2)}) collective-permute-start(bf16[288,512]{1,0:T(8,128)(2,1)S(1)} %get-tuple-element.63), channel_id=1, source_target_pairs={{0,5},{1,4},{2,7},{3,6},{4,1},{5,0},{6,3},{7,2},{8,13},{9,12},{10,... | collective-permute-start | bytes 884744 | tf_op jit(solution)/shard_map/ppermute | solution.py:93
  515.9 47.1 %collective-permute-start.122 = (bf16[288,512]{1,0:T(8,128)(2,1)S(1)}, bf16[288,512]{1,0:T(8,128)(2,1)S(1)}, u32[]{:S(2)}, u32[]{:S(2)}) collective-permute-start(bf16[288,512]{1,0:T(8,128)(2,1)S(1)} %get-tuple-element.64), channel_id=1, source_target_pairs={{0,4},{1,5},{2,6},{3,7},{4,0},{5,1},{6,2},{7,3},{8,12},{9,13},{10,... | collective-permute-start | bytes 884744 | tf_op jit(solution)/shard_map/ppermute | solution.py:93
  536.7 31.3 %collective-permute-start.124 = (bf16[288,512]{1,0:T(8,128)(2,1)S(1)}, bf16[288,512]{1,0:T(8,128)(2,1)S(1)}, u32[]{:S(2)}, u32[]{:S(2)}) collective-permute-start(bf16[288,512]{1,0:T(8,128)(2,1)S(1)} %get-tuple-element.65), channel_id=1, source_target_pairs={{0,2},{1,3},{2,0},{3,1},{4,6},{5,7},{6,4},{7,5},{8,10},{9,11},{10,... | collective-permute-start | bytes 884744 | tf_op jit(solution)/shard_map/ppermute | solution.py:93
  547.7 20.3 %collective-permute-start.125 = (bf16[288,512]{1,0:T(8,128)(2,1)S(1)}, bf16[288,512]{1,0:T(8,128)(2,1)S(1)}, u32[]{:S(2)}, u32[]{:S(2)}) collective-permute-start(bf16[288,512]{1,0:T(8,128)(2,1)S(1)} %get-tuple-element.59), channel_id=1, source_target_pairs={{0,1},{1,0},{2,3},{3,2},{4,5},{5,4},{6,7},{7,6},{8,9},{9,8},{10,11... | collective-permute-start | bytes 884744 | tf_op jit(solution)/shard_map/ppermute | solution.py:93
  559.9 57.1 %collective-permute-start.116 = (bf16[288,512]{1,0:T(8,128)(2,1)S(1)}, bf16[288,512]{1,0:T(8,128)(2,1)S(1)}, u32[]{:S(2)}, u32[]{:S(2)}) collective-permute-start(bf16[288,512]{1,0:T(8,128)(2,1)S(1)} %get-tuple-element.74), channel_id=1, source_target_pairs={{0,3},{1,2},{2,1},{3,0},{4,7},{5,6},{6,5},{7,4},{8,11},{9,10},{10,... | collective-permute-start | bytes 884744 | tf_op jit(solution)/shard_map/ppermute | solution.py:93
  565.5 33.4 %collective-permute-start.113 = (bf16[288,512]{1,0:T(8,128)(2,1)S(1)}, bf16[288,512]{1,0:T(8,128)(2,1)S(1)}, u32[]{:S(2)}, u32[]{:S(2)}) collective-permute-start(bf16[288,512]{1,0:T(8,128)(2,1)S(1)} %get-tuple-element.70), channel_id=1, source_target_pairs={{0,6},{1,7},{2,4},{3,5},{4,2},{5,3},{6,0},{7,1},{8,14},{9,15},{10,... | collective-permute-start | bytes 884744 | tf_op jit(solution)/shard_map/ppermute | solution.py:93
  567.9 43.1 %collective-permute-start.114 = (bf16[288,512]{1,0:T(8,128)(2,1)S(1)}, bf16[288,512]{1,0:T(8,128)(2,1)S(1)}, u32[]{:S(2)}, u32[]{:S(2)}) collective-permute-start(bf16[288,512]{1,0:T(8,128)(2,1)S(1)} %get-tuple-element.71), channel_id=1, source_target_pairs={{0,5},{1,4},{2,7},{3,6},{4,1},{5,0},{6,3},{7,2},{8,13},{9,12},{10,... | collective-permute-start | bytes 884744 | tf_op jit(solution)/shard_map/ppermute | solution.py:93
  568.0 46.0 %collective-permute-start.115 = (bf16[288,512]{1,0:T(8,128)(2,1)S(1)}, bf16[288,512]{1,0:T(8,128)(2,1)S(1)}, u32[]{:S(2)}, u32[]{:S(2)}) collective-permute-start(bf16[288,512]{1,0:T(8,128)(2,1)S(1)} %get-tuple-element.72), channel_id=1, source_target_pairs={{0,4},{1,5},{2,6},{3,7},{4,0},{5,1},{6,2},{7,3},{8,12},{9,13},{10,... | collective-permute-start | bytes 884744 | tf_op jit(solution)/shard_map/ppermute | solution.py:93
  575.8 43.7 %collective-permute-start.117 = (bf16[288,512]{1,0:T(8,128)(2,1)S(1)}, bf16[288,512]{1,0:T(8,128)(2,1)S(1)}, u32[]{:S(2)}, u32[]{:S(2)}) collective-permute-start(bf16[288,512]{1,0:T(8,128)(2,1)S(1)} %get-tuple-element.73), channel_id=1, source_target_pairs={{0,2},{1,3},{2,0},{3,1},{4,6},{5,7},{6,4},{7,5},{8,10},{9,11},{10,... | collective-permute-start | bytes 884744 | tf_op jit(solution)/shard_map/ppermute | solution.py:93
  598.9 21.1 %collective-permute-start.118 = (bf16[288,512]{1,0:T(8,128)(2,1)S(1)}, bf16[288,512]{1,0:T(8,128)(2,1)S(1)}, u32[]{:S(2)}, u32[]{:S(2)}) collective-permute-start(bf16[288,512]{1,0:T(8,128)(2,1)S(1)} %get-tuple-element.67), channel_id=1, source_target_pairs={{0,1},{1,0},{2,3},{3,2},{4,5},{5,4},{6,7},{7,6},{8,9},{9,8},{10,11... | collective-permute-start | bytes 884744 | tf_op jit(solution)/shard_map/ppermute | solution.py:93
  611.0 23.5 %collective-permute-start.109 = (bf16[288,512]{1,0:T(8,128)(2,1)S(1)}, bf16[288,512]{1,0:T(8,128)(2,1)S(1)}, u32[]{:S(2)}, u32[]{:S(2)}) collective-permute-start(bf16[288,512]{1,0:T(8,128)(2,1)S(1)} %get-tuple-element.82), channel_id=1, source_target_pairs={{0,3},{1,2},{2,1},{3,0},{4,7},{5,6},{6,5},{7,4},{8,11},{9,10},{10,... | collective-permute-start | bytes 884744 | tf_op jit(solution)/shard_map/ppermute | solution.py:93
  614.0 20.5 %collective-permute-start.105 = (bf16[288,512]{1,0:T(8,128)(2,1)S(1)}, bf16[288,512]{1,0:T(8,128)(2,1)S(1)}, u32[]{:S(2)}, u32[]{:S(2)}) collective-permute-start(bf16[288,512]{1,0:T(8,128)(2,1)S(1)} %get-tuple-element.77), channel_id=1, source_target_pairs={{0,7},{1,6},{2,5},{3,4},{4,3},{5,2},{6,1},{7,0},{8,15},{9,14},{10,... | collective-permute-start | bytes 884744 | tf_op jit(solution)/shard_map/ppermute | solution.py:93
  617.0 33.1 %collective-permute-start.106 = (bf16[288,512]{1,0:T(8,128)(2,1)S(1)}, bf16[288,512]{1,0:T(8,128)(2,1)S(1)}, u32[]{:S(2)}, u32[]{:S(2)}) collective-permute-start(bf16[288,512]{1,0:T(8,128)(2,1)S(1)} %get-tuple-element.78), channel_id=1, source_target_pairs={{0,6},{1,7},{2,4},{3,5},{4,2},{5,3},{6,0},{7,1},{8,14},{9,15},{10,... | collective-permute-start | bytes 884744 | tf_op jit(solution)/shard_map/ppermute | solution.py:93
  619.6 176.2 %collective-permute-start.51 = (bf16[1024,2048]{1,0:T(8,128)(2,1)}, bf16[1024,2048]{1,0:T(8,128)(2,1)}, u32[]{:S(2)}, u32[]{:S(2)}) collective-permute-start(bf16[1024,2048]{1,0:T(8,128)(2,1)} %slice.706), channel_id=1, source_target_pairs={{0,8},{8,0},{16,24},{24,16},{1,9},{9,1},{17,25},{25,17},{2,10},{10... | collective-permute-start | bytes 12582920 | tf_op jit(solution)/shard_map/ppermute | solution.py:93
  619.9 42.3 %collective-permute-start.107 = (bf16[288,512]{1,0:T(8,128)(2,1)S(1)}, bf16[288,512]{1,0:T(8,128)(2,1)S(1)}, u32[]{:S(2)}, u32[]{:S(2)}) collective-permute-start(bf16[288,512]{1,0:T(8,128)(2,1)S(1)} %get-tuple-element.79), channel_id=1, source_target_pairs={{0,5},{1,4},{2,7},{3,6},{4,1},{5,0},{6,3},{7,2},{8,13},{9,12},{10,... | collective-permute-start | bytes 884744 | tf_op jit(solution)/shard_map/ppermute | solution.py:93
  634.5 31.1 %collective-permute-start.108 = (bf16[288,512]{1,0:T(8,128)(2,1)S(1)}, bf16[288,512]{1,0:T(8,128)(2,1)S(1)}, u32[]{:S(2)}, u32[]{:S(2)}) collective-permute-start(bf16[288,512]{1,0:T(8,128)(2,1)S(1)} %get-tuple-element.80), channel_id=1, source_target_pairs={{0,4},{1,5},{2,6},{3,7},{4,0},{5,1},{6,2},{7,3},{8,12},{9,13},{10,... | collective-permute-start | bytes 884744 | tf_op jit(solution)/shard_map/ppermute | solution.py:93
  634.5 32.4 %collective-permute-start.110 = (bf16[288,512]{1,0:T(8,128)(2,1)S(1)}, bf16[288,512]{1,0:T(8,128)(2,1)S(1)}, u32[]{:S(2)}, u32[]{:S(2)}) collective-permute-start(bf16[288,512]{1,0:T(8,128)(2,1)S(1)} %get-tuple-element.81), channel_id=1, source_target_pairs={{0,2},{1,3},{2,0},{3,1},{4,6},{5,7},{6,4},{7,5},{8,10},{9,11},{10,... | collective-permute-start | bytes 884744 | tf_op jit(solution)/shard_map/ppermute | solution.py:93
  662.2 147.7 %collective-permute-start.69 = (bf16[1024,2048]{1,0:T(8,128)(2,1)}, bf16[1024,2048]{1,0:T(8,128)(2,1)}, u32[]{:S(2)}, u32[]{:S(2)}) collective-permute-start(bf16[1024,2048]{1,0:T(8,128)(2,1)} %slice.705), channel_id=1, source_target_pairs={{0,8},{8,0},{16,24},{24,16},{1,9},{9,1},{17,25},{25,17},{2,10},{10... | collective-permute-start | bytes 12582920 | tf_op jit(solution)/shard_map/ppermute | solution.py:93
  807.4 26.4 %collective-permute-start.52 = (bf16[256,2048]{1,0:T(8,128)(2,1)}, bf16[256,2048]{1,0:T(8,128)(2,1)}, u32[]{:S(2)}, u32[]{:S(2)}) collective-permute-start(bf16[256,2048]{1,0:T(8,128)(2,1)} %get-tuple-element.58), channel_id=1, source_target_pairs={{0,16},{8,24},{16,0},{24,8},{1,17},{9,25},{17,1},{25,9},{2,18},{10... | collective-permute-start | bytes 3145736 | tf_op jit(solution)/shard_map/ppermute | solution.py:93
  809.1 26.4 %collective-permute-start.54 = (bf16[256,2048]{1,0:T(8,128)(2,1)}, bf16[256,2048]{1,0:T(8,128)(2,1)}, u32[]{:S(2)}, u32[]{:S(2)}) collective-permute-start(bf16[256,2048]{1,0:T(8,128)(2,1)} %get-tuple-element.57), channel_id=1, source_target_pairs={{0,1},{1,0},{2,3},{3,2},{4,5},{5,4},{6,7},{7,6},{8,9},{9,8},{10,11... | collective-permute-start | bytes 3145736 | tf_op jit(solution)/shard_map/ppermute | solution.py:93
  821.6 34.6 %collective-permute-start.70 = (bf16[256,2048]{1,0:T(8,128)(2,1)}, bf16[256,2048]{1,0:T(8,128)(2,1)}, u32[]{:S(2)}, u32[]{:S(2)}) collective-permute-start(bf16[256,2048]{1,0:T(8,128)(2,1)} %get-tuple-element.56), channel_id=1, source_target_pairs={{0,16},{8,24},{16,0},{24,8},{1,17},{9,25},{17,1},{25,9},{2,18},{10... | collective-permute-start | bytes 3145736 | tf_op jit(solution)/shard_map/ppermute | solution.py:93
  822.1 34.3 %collective-permute-start.72 = (bf16[256,2048]{1,0:T(8,128)(2,1)}, bf16[256,2048]{1,0:T(8,128)(2,1)}, u32[]{:S(2)}, u32[]{:S(2)}) collective-permute-start(bf16[256,2048]{1,0:T(8,128)(2,1)} %get-tuple-element.55), channel_id=1, source_target_pairs={{0,1},{1,0},{2,3},{3,2},{4,5},{5,4},{6,7},{7,6},{8,9},{9,8},{10,11... | collective-permute-start | bytes 3145736 | tf_op jit(solution)/shard_map/ppermute | solution.py:93
  839.0 28.3 %collective-permute-start.55 = (bf16[128,2048]{1,0:T(8,128)(2,1)S(1)}, bf16[128,2048]{1,0:T(8,128)(2,1)S(1)}, u32[]{:S(2)}, u32[]{:S(2)}) collective-permute-start(bf16[128,2048]{1,0:T(8,128)(2,1)S(1)} %slice.710), channel_id=1, source_target_pairs={{0,16},{8,24},{16,0},{24,8},{1,17},{9,25},{17,1},{25,9},{2,18},{10... | collective-permute-start | bytes 1572872 | tf_op jit(solution)/shard_map/ppermute | solution.py:93
  926.9 23.1 %collective-permute-start.103 = (bf16[512,256]{1,0:T(8,128)(2,1)S(1)}, bf16[512,256]{1,0:T(8,128)(2,1)}, u32[]{:S(2)}, u32[]{:S(2)}) collective-permute-start(bf16[512,256]{1,0:T(8,128)(2,1)S(1)} %bitcast.441), channel_id=1, source_target_pairs={{0,16},{8,24},{16,0},{24,8},{1,17},{9,25},{17,1},{25,9},{2,18},{10... | collective-permute-start | bytes 786440 | tf_op jit(solution)/shard_map/ppermute | solution.py:93
  934.3 27.0 %collective-permute-start.82 = (bf16[128,2048]{1,0:T(8,128)(2,1)}, bf16[128,2048]{1,0:T(8,128)(2,1)}, u32[]{:S(2)}, u32[]{:S(2)}) collective-permute-start(bf16[128,2048]{1,0:T(8,128)(2,1)} %pad_maximum_fusion.25), channel_id=1, source_target_pairs={{0,8},{8,0},{16,24},{24,16},{1,9},{9,1},{17,25},{25,17},{2,10},{10... | collective-permute-start | bytes 1572872 | tf_op jit(solution)/shard_map/ppermute | solution.py:93
  951.8 25.4 %collective-permute-start.104 = (bf16[1024,256]{1,0:T(8,128)(2,1)}, bf16[1024,256]{1,0:T(8,128)(2,1)}, u32[]{:S(2)}, u32[]{:S(2)}) collective-permute-start(bf16[1024,256]{1,0:T(8,128)(2,1)} %pad_maximum_fusion.27), channel_id=1, source_target_pairs={{0,8},{8,0},{16,24},{24,16},{1,9},{9,1},{17,25},{25,17},{2,10},{10... | collective-permute-start | bytes 1572872 | tf_op jit(solution)/shard_map/ppermute | solution.py:93
  958.1 25.4 %collective-permute-start.60 = (bf16[128,2048]{1,0:T(8,128)(2,1)S(1)}, bf16[128,2048]{1,0:T(8,128)(2,1)S(1)}, u32[]{:S(2)}, u32[]{:S(2)}) collective-permute-start(bf16[128,2048]{1,0:T(8,128)(2,1)S(1)} %slice.709), channel_id=1, source_target_pairs={{0,8},{8,0},{16,24},{24,16},{1,9},{9,1},{17,25},{25,17},{2,10},{10... | collective-permute-start | bytes 1572872 | tf_op jit(solution)/shard_map/ppermute | solution.py:93
  984.0 43.4 %collective-permute-start.61 = (bf16[64,2048]{1,0:T(8,128)(2,1)S(1)}, bf16[64,2048]{1,0:T(8,128)(2,1)S(1)}, u32[]{:S(2)}, u32[]{:S(2)}) collective-permute-start(bf16[64,2048]{1,0:T(8,128)(2,1)S(1)} %slice.714), channel_id=1, source_target_pairs={{0,16},{8,24},{16,0},{24,8},{1,17},{9,25},{17,1},{25,9},{2,18},{10... | collective-permute-start | bytes 786440 | tf_op jit(solution)/shard_map/ppermute | solution.py:93
  (205 other events, 2642.8 us)
Sparse Core Ops, SparseCore 0:
  12.0 76.3 all-gather.6
  91.0 57.8 all-gather.8
  151.6 55.8 all-gather.10
  210.2 69.3 all-gather.16
  428.7 49.0 all-gather.14
  955.6 57.9 all-gather.12

commit v2 on v1

v2 whole, which is shorter than its diff:
```python
import math

import jax
import jax.numpy as jnp
from jax import lax
from jax.experimental import pallas as pl
from jax.experimental.pallas import tpu as pltpu
from jax.sharding import PartitionSpec as P

HEAD_SIZE = 256
LOOP_COUNT = 3


EPSILON = 1e-06
MASKED_SCORE = -1e30
precise = lax.Precision.HIGHEST
f32 = jnp.float32
bf16 = jnp.bfloat16


def rms_norm(inputs, gain):
    return inputs * lax.rsqrt(jnp.mean(inputs * inputs, axis=-1, keepdims=True) + EPSILON) * gain


def rotate(inputs, spots, direction):
    half_width = inputs.shape[-1] // 2
    frequency = jnp.exp(
        jnp.arange(half_width, dtype=jnp.float32) * (-2.0 * math.log(10000.0) / inputs.shape[-1])
    )
    angles = spots.astype(jnp.float32)[:, None] * frequency[None, :]
    cos_part = jnp.cos(angles)
    sin_part = jnp.sin(angles) * direction
    if inputs.ndim == 3:
        cos_part = cos_part[:, None, :]
        sin_part = sin_part[:, None, :]
    first_half = inputs[..., :half_width]
    second_half = inputs[..., half_width:]
    return jnp.concatenate(
        [
            first_half * cos_part - second_half * sin_part,
            second_half * cos_part + first_half * sin_part,
        ],
        axis=-1,
    )


def update_delta(left_factor, right_factor, factor_pairs):
    if factor_pairs:
        rank_half = left_factor.shape[1] // 2
        width_half = right_factor.shape[1] // 2
        key_half = jnp.dot(
            left_factor[:, :rank_half],
            right_factor[:, :width_half],
            preferred_element_type=jnp.float32,
        )
        value_half = jnp.dot(
            left_factor[:, rank_half:],
            right_factor[:, width_half:],
            preferred_element_type=jnp.float32,
        )
        return jnp.concatenate([key_half, value_half], axis=1)
    return jnp.dot(left_factor, right_factor, preferred_element_type=jnp.float32)


def attention_weights(queries, key_rows, query_seq, query_spots, key_seq, key_spots, score_scale):
    scores = (
        jnp.einsum("qhd,kd->hqk", queries, key_rows, preferred_element_type=jnp.float32)
        * score_scale
    )
    allowed = (query_seq[:, None] == key_seq[None, :]) & (
        key_spots[None, :] <= query_spots[:, None]
    )
    scores = jnp.where(allowed[None], scores, MASKED_SCORE)
    return jax.nn.softmax(scores, axis=-1)


def dot(left, right):
    return jnp.dot(left, right, preferred_element_type=f32)


def dot_rows(left, right):
    return lax.dot_general(left, right, (((0,), (0,)), ((), ())), preferred_element_type=f32)


def dot_cols(left, right):
    return lax.dot_general(left, right, (((1,), (1,)), ((), ())), preferred_element_type=f32)


def swap(value, axis, bit):
    count = lax.axis_size(axis)
    return lax.ppermute(value, axis, [(place, place ^ bit) for place in range(count)])


def exchange(blocks):
    return lax.all_to_all(blocks, "dp", 0, 0, tiled=True)


def far_bits():
    bit = lax.axis_size("dp") // 2
    bits = []
    while bit > 1:
        bits.append(bit)
        bit = bit // 2
    return bits


def grow(value, axis, bit):
    return jnp.concatenate([value, swap(value, axis, bit)], axis=0)


def fold(value, axis, bit):
    half = value.shape[0] // 2
    arrived = swap(value[half:].astype(bf16), axis, bit)
    return value[:half] + arrived.astype(f32)


def after(value, *others):
    total = jnp.zeros((), f32)
    for other in others:
        last = other[tuple(size - 1 for size in other.shape)]
        total = jnp.maximum(total, jnp.abs(last.astype(f32)))
    return value + jnp.minimum(total, 0.0).astype(value.dtype)


def halves(value):
    half = value.shape[0] // 2
    return value[:half], value[half:]


def gather_mp(value):
    place = lax.axis_index("mp")
    arrived = swap(value, "mp", 2)
    value = jnp.where(
        place < 2, jnp.stack([value, arrived], axis=0), jnp.stack([arrived, value], axis=0)
    )
    arrived = swap(value, "mp", 1)
    return jnp.where(
        place % 2 == 0, jnp.stack([value, arrived], axis=1), jnp.stack([arrived, value], axis=1)
    )


def scatter_mp(value):
    place = lax.axis_index("mp")
    for axis, bit, own in ((1, 1, place % 2), (0, 2, place // 2)):
        if axis == 1:
            value = value.reshape((2, 2, value.shape[0] // 4) + value.shape[1:])
        sent = lax.dynamic_index_in_dim(value, 1 - own, axis, keepdims=False)
        kept = lax.dynamic_index_in_dim(value, own, axis, keepdims=False)
        value = kept + swap(sent.astype(bf16), "mp", bit).astype(f32)
    return value


def gather_far(value):
    for bit in far_bits():
        value = grow(value, "dp", bit)
    return value


def gather_near(value):
    half = value.shape[0] // 2
    front = grow(grow(value[:half], "dp", 1), "mp", 2)
    rear = grow(grow(value[half:], "mp", 2), "dp", 1)
    return jnp.concatenate([front, rear], axis=0)


def other_core(value):
    return swap(value, "mp", 1)


def scatter_near(sent, kept):
    value = kept + swap(sent.astype(bf16), "mp", 1).astype(f32)
    half = value.shape[0] // 2
    front = fold(fold(value[:half], "mp", 2), "dp", 1)
    rear = fold(fold(value[half:], "dp", 1), "mp", 2)
    return jnp.concatenate([front, rear], axis=0)


def scatter_far(value):
    for bit in reversed(far_bits()):
        value = fold(value, "dp", bit)
    return value


def sum_all(value):
    for axis in ("mp", "dp"):
        bit = 1
        while bit < lax.axis_size(axis):
            value = value + swap(value, axis, bit)
            bit = bit * 2
    return value


def sum_mp(value):
    value = value + swap(value, "mp", 1)
    low = value.astype(bf16)
    return low.astype(f32) + swap(low, "mp", 2).astype(f32)


def merge_kernel(loop_ref, *refs):
    out_ref = refs[-1]
    width = refs[0].shape[1]
    for index in range(len(refs) // 3):
        base_ref, left_ref, right_ref = refs[3 * index : 3 * index + 3]
        delta = jnp.dot(left_ref[0], right_ref[0], preferred_element_type=f32)
        merged = base_ref[...].astype(f32) + delta
        out_ref[0, :, index * width : (index + 1) * width] = merged.astype(bf16)


def merge_blocks(loop, places, weights):
    rows, columns = weights[0][0].shape
    rank = weights[0][1].shape[2]
    width = columns // places
    specs = []
    arrays = []
    for base, left, right in weights:
        specs.append(pl.BlockSpec((rows, width), lambda place, loop_ref: (0, place)))
        specs.append(pl.BlockSpec((1, rows, rank), lambda place, loop_ref: (loop_ref[0], 0, 0)))
        specs.append(
            pl.BlockSpec((1, rank, width), lambda place, loop_ref: (loop_ref[0], 0, place))
        )
        arrays += [base, left, right]
    return pl.pallas_call(
        merge_kernel,
        out_shape=jax.ShapeDtypeStruct((places, rows, width * len(weights)), bf16),
        grid_spec=pltpu.PrefetchScalarGridSpec(
            num_scalar_prefetch=1,
            grid=(places,),
            in_specs=specs,
            out_specs=pl.BlockSpec(
                (1, rows, width * len(weights)), lambda place, loop_ref: (place, 0, 0)
            ),
        ),
        compiler_params=pltpu.CompilerParams(vmem_limit_bytes=48 * 2**20),
    )(loop, *arrays)


def receive_kernel(loop_ref, arrived_ref, right_ref, grad_ref, left_grad_ref):
    rows = grad_ref.shape[0]
    block = arrived_ref[0][:rows]
    grad_ref[...] = block.astype(f32)
    part = lax.dot_general(
        block, right_ref[0], (((1,), (1,)), ((), ())), preferred_element_type=f32
    )

    @pl.when(pl.program_id(0) == 0)
    def first():
        left_grad_ref[...] = part

    @pl.when(pl.program_id(0) > 0)
    def later():
        left_grad_ref[...] += part


def receive_grad(loop, arrived, right, rows):
    places, all_rows, width = arrived.shape
    rank = right.shape[1]
    return pl.pallas_call(
        receive_kernel,
        out_shape=(
            jax.ShapeDtypeStruct((rows, places * width), f32),
            jax.ShapeDtypeStruct((rows, rank), f32),
        ),
        grid_spec=pltpu.PrefetchScalarGridSpec(
            num_scalar_prefetch=1,
            grid=(places,),
            in_specs=[
                pl.BlockSpec((1, all_rows, width), lambda place, loop_ref: (place, 0, 0)),
                pl.BlockSpec((1, rank, width), lambda place, loop_ref: (loop_ref[0], 0, place)),
            ],
            out_specs=(
                pl.BlockSpec((rows, width), lambda place, loop_ref: (0, place)),
                pl.BlockSpec((rows, rank), lambda place, loop_ref: (0, 0)),
            ),
        ),
        compiler_params=pltpu.CompilerParams(vmem_limit_bytes=48 * 2**20),
    )(loop, arrived, right)


def feed_kernel(
    normed_ref, cotangent_ref, gate_down_ref, up_ref, hidden_ref, grads_ref, partial_ref
):
    width = up_ref.shape[1]
    normed = normed_ref[...]
    gate_act = jnp.dot(normed, gate_down_ref[:, :width], preferred_element_type=f32)
    up_act = jnp.dot(normed, up_ref[...], preferred_element_type=f32)
    hidden_grad = jnp.dot(
        cotangent_ref[...], gate_down_ref[:, width:], preferred_element_type=f32
    )
    scale = math.sqrt(2.0 / math.pi)
    square = gate_act * gate_act
    tanh_part = jnp.tanh(scale * (gate_act + 0.044715 * (gate_act * square)))
    half_sum = 0.5 * (1.0 + tanh_part)
    gelu = gate_act * half_sum
    slope = half_sum + (0.5 * gate_act) * (1.0 - tanh_part * tanh_part) * (
        scale * (1.0 + (3.0 * 0.044715) * square)
    )
    hidden_ref[...] = (gelu * up_act).astype(bf16)
    gate_grad = (hidden_grad * up_act * slope).astype(bf16)
    up_grad = (hidden_grad * gelu).astype(bf16)
    grads_ref[:, :width] = gate_grad
    grads_ref[:, width:] = up_grad
    partial = lax.dot_general(
        gate_grad,
        gate_down_ref[:, :width],
        (((1,), (1,)), ((), ())),
        preferred_element_type=f32,
    ) + lax.dot_general(
        up_grad, up_ref[...], (((1,), (1,)), ((), ())), preferred_element_type=f32
    )
    partial_ref[...] = partial.astype(partial_ref.dtype)


def feed_forward(normed, cotangent, gate_down, up, kind):
    rows, model_width = normed.shape
    width = up.shape[1]
    tile = math.gcd(rows, 256)
    row_block = pl.BlockSpec((tile, model_width), lambda step: (step, 0))
    return pl.pallas_call(
        feed_kernel,
        out_shape=(
            jax.ShapeDtypeStruct((rows, width), bf16),
            jax.ShapeDtypeStruct((rows, 2 * width), bf16),
            jax.ShapeDtypeStruct((rows, model_width), kind),
        ),
        grid=(rows // tile,),
        in_specs=[
            row_block,
            row_block,
            pl.BlockSpec((model_width, 2 * width), lambda step: (0, 0)),
            pl.BlockSpec((model_width, width), lambda step: (0, 0)),
        ],
        out_specs=(
            pl.BlockSpec((tile, width), lambda step: (step, 0)),
            pl.BlockSpec((tile, 2 * width), lambda step: (step, 0)),
            row_block,
        ),
        compiler_params=pltpu.CompilerParams(vmem_limit_bytes=56 * 2**20),
    )(normed, cotangent, gate_down, up)


def body(
    tokens,
    cotangent,
    token_sequence_index,
    positions,
    token_exit_loop,
    current_loop,
    attention_norm_gain,
    feedforward_norm_gain,
    probe,
    query_matrix,
    key_value_matrix,
    output_matrix,
    gate_matrix,
    up_matrix,
    down_matrix,
    query_update_left,
    query_update_right,
    key_value_update_left,
    key_value_update_right,
    output_update_left,
    output_update_right,
    gate_update_left,
    gate_update_right,
    up_update_left,
    up_update_right,
    down_update_left,
    down_update_right,
):
    loop_selection = current_loop[0]
    score_scale = HEAD_SIZE ** (-0.5)
    mp_count = lax.axis_size("mp")
    dp_count = lax.axis_size("dp")
    mp_place = lax.axis_index("mp")
    dp_place = lax.axis_index("dp")
    row_count, model_width = tokens.shape
    own_rows = row_count // mp_count
    block_width, query_cols = query_matrix.shape
    head_count = query_cols // HEAD_SIZE
    hidden_own = gate_matrix.shape[1] // dp_count
    rank = gate_update_left.shape[2]
    rank_own = rank // dp_count

    def pick(table):
        return lax.dynamic_index_in_dim(table, loop_selection, 0, keepdims=False)

    q_left, kv_left, o_left = map(
        pick, (query_update_left, key_value_update_left, output_update_left)
    )
    gate_left, up_left, down_left = map(pick, (gate_update_left, up_update_left, down_update_left))
    q_right, kv_right, o_right = map(
        pick, (query_update_right, key_value_update_right, output_update_right)
    )
    def merge(base, left, right, pairs=False):
        return (base.astype(f32) + update_delta(left, right, pairs)).astype(bf16)

    def own_slice(value):
        return lax.dynamic_slice_in_dim(value, mp_place * own_rows, own_rows, 0)

    def to_places(shard, width):
        blocks = [shard[:, place * width : (place + 1) * width] for place in range(dp_count)]
        return jnp.stack(blocks, axis=0)

    block_rows = block_width // mp_count

    def block_slice(value):
        return lax.dynamic_slice_in_dim(value, mp_place * block_rows, block_rows, 0)

    kv_full = lax.all_gather(
        merge(block_slice(key_value_matrix), block_slice(kv_left), kv_right, True),
        ("dp", "mp"),
        axis=0,
        tiled=True,
    )
    q_o_full = lax.all_gather(
        jnp.concatenate(
            [merge(query_matrix, q_left, q_right), merge(output_matrix, o_left, o_right)], axis=1
        ),
        "dp",
        axis=0,
        tiled=True,
    )
    q_full = q_o_full[:, :query_cols]
    o_full = q_o_full[:, query_cols:]

    cotangent_own = own_slice(cotangent)
    cotangent_front = gather_near(gather_far(cotangent_own))
    cotangent_rear = other_core(cotangent_front)

    tokens_own = own_slice(tokens).astype(f32)
    normed_b = rms_norm(tokens.astype(f32), attention_norm_gain).astype(bf16)

    def all_token_cols(rows_own):
        cols = exchange(to_places(rows_own, block_width)).reshape(-1, block_width)
        cols = gather_mp(cols).reshape(mp_count, dp_count, own_rows, block_width)
        return jnp.swapaxes(cols, 0, 1).reshape(dp_count * row_count, block_width)

    normed_cols = all_token_cols(own_slice(normed_b))
    pair_own = dot(own_slice(normed_b), kv_full)
    seq_own = own_slice(token_sequence_index)
    spots_own = own_slice(positions)
    marks = jnp.stack([seq_own, spots_own // 64, spots_own % 64], axis=0).astype(bf16)
    marks = jnp.pad(marks, ((0, 5), (0, 2 * HEAD_SIZE - own_rows)))
    outgoing = jnp.concatenate(
        [
            rotate(pair_own[:, :HEAD_SIZE], spots_own, 1.0).astype(bf16),
            pair_own[:, HEAD_SIZE:].astype(bf16),
        ],
        axis=1,
    )
    outgoing = jnp.concatenate([outgoing, marks], axis=0)
    pairs_far = after(gather_far(outgoing), *halves(cotangent_front))
    pairs_front = gather_near(pairs_far)
    all_pairs = jnp.concatenate([pairs_front, other_core(pairs_front)], axis=0)
    all_pairs = all_pairs.reshape(-1, own_rows + 8, 2 * HEAD_SIZE)
    all_keys = all_pairs[:, :own_rows, :HEAD_SIZE].reshape(-1, HEAD_SIZE)
    all_values = all_pairs[:, :own_rows, HEAD_SIZE:].reshape(-1, HEAD_SIZE)
    all_marks = all_pairs[:, own_rows : own_rows + 3, :own_rows].astype(jnp.int32)
    all_seq = all_marks[:, 0].reshape(-1)
    all_spots = (all_marks[:, 1] * 64 + all_marks[:, 2]).reshape(-1)
    queries = dot(normed_b, q_full)
    query_b = rotate(queries.reshape(row_count, head_count, HEAD_SIZE), positions, 1.0).astype(
        bf16
    )
    gate_down = exchange(
        merge_blocks(
            after(current_loop, *halves(pairs_front)),
            dp_count,
            [
                (gate_matrix, gate_update_left, gate_update_right),
                (down_matrix, down_update_left, down_update_right),
            ],
        )
    ).reshape(model_width, 2 * hidden_own)
    query_b = after(query_b, normed_cols)
    weights_soft = attention_weights(
        query_b, all_keys, token_sequence_index, positions, all_seq, all_spots, score_scale
    )
    weights_low = weights_soft.astype(bf16)
    attended = jnp.einsum("hqk,kd->qhd", weights_low, all_values, preferred_element_type=f32)
    attended_b = attended.reshape(row_count, query_cols).astype(bf16)
    middle = tokens_own + scatter_mp(dot_cols(attended_b, o_full))
    normed2_b = rms_norm(middle, feedforward_norm_gain).astype(bf16)

    normed2_far = gather_far(after(normed2_b, gate_down))
    up_own = exchange(
        merge_blocks(
            after(current_loop, normed2_far),
            dp_count,
            [(up_matrix, up_update_left, up_update_right)],
        )
    ).reshape(model_width, hidden_own)
    normed2_front = gather_near(normed2_far)
    normed2_rear = other_core(after(normed2_front, up_own))
    left_block = jnp.concatenate([gate_left, up_left, down_left], axis=1)
    left_all = lax.all_gather(
        after(block_slice(left_block), gate_down), ("dp", "mp"), axis=0, tiled=True
    )

    hidden_front, grads_front, partial_front = feed_forward(
        normed2_front, cotangent_front, gate_down, up_own, f32
    )
    hidden_rear, grads_rear, partial_rear = feed_forward(
        normed2_rear, cotangent_rear, gate_down, up_own, bf16
    )
    normed2_near = scatter_near(partial_rear, partial_front)

    def weight_grad(front, rear, grads_front, grads_rear):
        return (dot_rows(front, grads_front) + dot_rows(rear, grads_rear)).astype(bf16)

    def to_blocks(grad_b, left_cols):
        right_part = dot_rows(left_cols, grad_b).astype(bf16)
        return [
            grad_b.reshape(dp_count, block_width, hidden_own),
            right_part.reshape(dp_count, rank_own, hidden_own),
        ]

    down_grad_b = weight_grad(cotangent_front, cotangent_rear, hidden_front, hidden_rear)
    gate_up_grad_b = weight_grad(normed2_front, normed2_rear, grads_front, grads_rear)
    down_gate_sent = exchange(
        jnp.concatenate(
            to_blocks(down_grad_b, left_all[:, 2 * rank :])
            + to_blocks(gate_up_grad_b[:, :hidden_own], left_all[:, :rank]),
            axis=1,
        )
    )
    up_grad_blocks = jnp.concatenate(
        to_blocks(gate_up_grad_b[:, hidden_own:], left_all[:, rank : 2 * rank]), axis=1
    )
    normed2_grad = scatter_far(after(normed2_near, down_gate_sent))

    hidden_late = after(jnp.zeros((1, hidden_own), bf16), *halves(normed2_near))
    down_own = gate_down[:, hidden_own:]
    mlp_branch = scatter_far(
        scatter_near(
            dot_cols(hidden_rear + hidden_late, down_own),
            dot_cols(hidden_front + hidden_late, down_own),
        )
    )
    output_rows = middle + mlp_branch
    mixed = gather_mp(output_rows.astype(bf16)).reshape(row_count, model_width)
    confidence_own = jnp.sum(jax.nn.sigmoid(jnp.dot(output_rows, probe, precision=precise)))
    levels = jnp.arange(LOOP_COUNT, dtype=jnp.int32)
    exit_own = own_slice(token_exit_loop)
    depth_own = jnp.sum((exit_own[:, None] == levels[None, :]).astype(f32), axis=0)

    unused_norm, mlp_pull = jax.vjp(rms_norm, middle, feedforward_norm_gain)
    middle_norm_grad, mlp_gain_part = mlp_pull(normed2_grad)
    middle_grad = cotangent_own.astype(f32) + middle_norm_grad
    branch_grad_own = middle_grad.astype(bf16)
    branch_grad = gather_mp(branch_grad_own).reshape(row_count, model_width)
    up_sent = exchange(after(up_grad_blocks, normed2_grad))
    attended_grad_b = (
        dot(branch_grad, o_full).astype(bf16).reshape(row_count, head_count, HEAD_SIZE)
    )
    prob_grad = jnp.einsum("qhd,kd->hqk", attended_grad_b, all_values, preferred_element_type=f32)
    score_grad_b = (
        weights_soft * (prob_grad - jnp.sum(prob_grad * weights_soft, axis=-1, keepdims=True))
    ).astype(bf16)
    keys_grad = (
        jnp.einsum("hqk,qhd->kd", score_grad_b, query_b, preferred_element_type=f32) * score_scale
    )
    values_grad = jnp.einsum(
        "hqk,qhd->kd", weights_low, attended_grad_b, preferred_element_type=f32
    )
    pair_partial = jnp.concatenate([keys_grad, values_grad], axis=1)
    half = pair_partial.shape[0] // 2
    pair_partial = after(pair_partial, up_sent)
    pair_near = scatter_near(pair_partial[half:], pair_partial[:half])
    o_partial = dot_rows(branch_grad, attended_b).astype(bf16)
    o_sent = exchange(after(o_partial.reshape(dp_count, block_width, query_cols), up_sent))
    pair_grad_own = after(scatter_far(pair_near), o_sent)
    pair_grad_b = jnp.concatenate(
        [rotate(pair_grad_own[:, :HEAD_SIZE], spots_own, -1.0), pair_grad_own[:, HEAD_SIZE:]],
        axis=1,
    ).astype(bf16)
    query_grad = (
        jnp.einsum("hqk,kd->qhd", score_grad_b, all_keys, preferred_element_type=f32) * score_scale
    )
    query_grad_b = rotate(query_grad, positions, -1.0).reshape(row_count, query_cols).astype(bf16)
    normed_grad = scatter_mp(dot_cols(query_grad_b, q_full)) + dot_cols(pair_grad_b, kv_full)
    unused_first, attn_pull = jax.vjp(rms_norm, tokens_own, attention_norm_gain)
    inputs_norm_grad, attn_gain_part = attn_pull(normed_grad)
    tokens_grad = gather_mp(middle_grad + inputs_norm_grad).reshape(row_count, model_width)

    query_grad_all = lax.all_gather(query_grad_b, "dp", axis=0, tiled=True)
    pair_grad_all = lax.all_gather(pair_grad_b, ("dp", "mp"), axis=0, tiled=True)
    q_weight_grad = dot_rows(normed_cols, query_grad_all)
    kv_weight_grad = dot_rows(normed_cols, after(pair_grad_all, mlp_branch))
    o_weight_grad = jnp.sum(o_sent.astype(f32), axis=0)
    q_weight_b = q_weight_grad.astype(bf16)
    kv_weight_b = kv_weight_grad.astype(bf16)
    o_weight_b = o_weight_grad.astype(bf16)
    qo_lora_a = sum_mp(
        jnp.concatenate([dot_cols(q_weight_b, q_right), dot_cols(o_weight_b, o_right)], axis=1)
    )
    kv_lora_a = jnp.concatenate(
        [
            dot_cols(kv_weight_b[:, :HEAD_SIZE], kv_right[:, :HEAD_SIZE]),
            dot_cols(kv_weight_b[:, HEAD_SIZE:], kv_right[:, HEAD_SIZE:]),
        ],
        axis=1,
    )
    right_parts = jnp.concatenate(
        [
            dot_rows(q_left, q_weight_b),
            dot_rows(o_left, o_weight_b),
            dot_rows(kv_left[:, :rank], kv_weight_b[:, :HEAD_SIZE]),
            dot_rows(kv_left[:, rank:], kv_weight_b[:, HEAD_SIZE:]),
        ],
        axis=1,
    ).astype(bf16)
    right_grads = jnp.sum(
        exchange(right_parts.reshape(dp_count, rank_own, -1)).astype(f32), axis=0
    )

    block_all = block_width + rank_own

    def side_by_side(arrived, first):
        return jnp.concatenate(
            [arrived[place, first : first + rank_own].astype(f32) for place in range(dp_count)],
            axis=1,
        )

    down_arrived = down_gate_sent[:, :block_all]
    gate_arrived = down_gate_sent[:, block_all:]
    down_weight_grad, down_lora_a = receive_grad(
        current_loop, down_arrived, down_update_right, block_width
    )
    gate_weight_grad, gate_lora_a = receive_grad(
        current_loop, gate_arrived, gate_update_right, block_width
    )
    up_weight_grad, up_lora_a = receive_grad(
        current_loop, up_sent, up_update_right, block_width
    )
    down_lora_b = side_by_side(down_arrived, block_width)
    gate_lora_b = side_by_side(gate_arrived, block_width)
    up_lora_b = side_by_side(up_sent, block_width)
    mlp_lora_a = sum_mp(jnp.concatenate([gate_lora_a, up_lora_a, down_lora_a], axis=1))

    small = sum_all(
        jnp.concatenate([attn_gain_part, mlp_gain_part, depth_own, confidence_own.reshape(1)])
    )
    gain_width = model_width // dp_count
    attn_gain_grad = lax.dynamic_slice_in_dim(small, dp_place * gain_width, gain_width, 0)
    mlp_gain_grad = lax.dynamic_slice_in_dim(
        small, model_width + dp_place * gain_width, gain_width, 0
    )
    counts = small[2 * model_width : 2 * model_width + LOOP_COUNT].astype(jnp.int32)
    confidence = small[2 * model_width + LOOP_COUNT :] / (row_count * dp_count)

    def place_loop(grad_item):
        chosen = jnp.arange(LOOP_COUNT)[:, None, None] == loop_selection
        return jnp.where(chosen, grad_item[None], 0.0)

    return (
        counts,
        confidence,
        mixed,
        tokens_grad,
        attn_gain_grad,
        mlp_gain_grad,
        q_weight_grad,
        kv_weight_grad,
        o_weight_grad,
        gate_weight_grad,
        up_weight_grad,
        down_weight_grad,
        place_loop(qo_lora_a[:, :rank]),
        place_loop(right_grads[:, :query_cols]),
        place_loop(kv_lora_a),
        place_loop(right_grads[:, 2 * query_cols :]),
        place_loop(qo_lora_a[:, rank:]),
        place_loop(right_grads[:, query_cols : 2 * query_cols]),
        place_loop(mlp_lora_a[:, :rank]),
        place_loop(gate_lora_b),
        place_loop(mlp_lora_a[:, rank : 2 * rank]),
        place_loop(up_lora_b),
        place_loop(mlp_lora_a[:, 2 * rank :]),
        place_loop(down_lora_b),
    )


def solution(mesh):
    return jax.shard_map(
        body,
        mesh=mesh,
        in_specs=(
            P("dp", None),
            P("dp", None),
            P("dp"),
            P("dp"),
            P("dp"),
            P(),
            P(),
            P(),
            P(),
            P("dp", "mp"),
            P("dp", None),
            P("dp", "mp"),
            P("dp", "mp"),
            P("dp", "mp"),
            P("dp", "mp"),
            P(None, "dp", None),
            P(None, None, "mp"),
            P(None, "dp", None),
            P(),
            P(None, "dp", None),
            P(None, None, "mp"),
            P(None, "dp", None),
            P(None, None, "mp"),
            P(None, "dp", None),
            P(None, None, "mp"),
            P(None, "dp", None),
            P(None, None, "mp"),
        ),
        out_specs=(
            P(),
            P(),
            P("dp", None),
            P("dp", None),
            P("dp"),
            P("dp"),
            P("dp", "mp"),
            P("dp", None),
            P("dp", "mp"),
            P("dp", "mp"),
            P("dp", "mp"),
            P("dp", "mp"),
            P(None, "dp", None),
            P(None, "dp", "mp"),
            P(None, "dp", None),
            P(None, "dp", None),
            P(None, "dp", None),
            P(None, "dp", "mp"),
            P(None, "dp", None),
            P(None, "dp", "mp"),
            P(None, "dp", None),
            P(None, "dp", "mp"),
            P(None, "dp", None),
            P(None, "dp", "mp"),
        ),
        check_vma=False,
    )
```

time: 1120 us -> 910 us (0.81)
  starting transfers between devices: 228 us -> 93.9 us
  local copies, waits for them, and re-layouts: 217 us -> 116 us
  Pallas kernels: 0 us -> 69 us
  matrix products: 136 us -> 96.7 us
  blocking collectives: 32.3 us -> 0 us
  other arithmetic: 79.5 us -> 91.1 us
    ppermute x137 -> x63, starting transfers between devices: 227 us -> 56.9 us  [swap(): lax.ppermute(value, axis, [(place, place ^ bit) for place in range(count)])]
    dynamic_update_slice x82 -> x0, local copies, waits for them, and re-layouts: 107 us -> none  [the longest x63 102 us: exchange_dp(): result = lax.dynamic_update_index_in_dim(result, arrived, place, 0)]
    pallas_call x0 -> x7, Pallas kernels: none -> 69 us  [the longest x2 34 us: feed_forward(): pl.pallas_call(feed_kernel, out_shape=(jax.ShapeDtypeStruct((rows, width)...]
    ppermute x137 -> x63, waiting for transfers between devices: 381 us -> 322 us  [swap(): lax.ppermute(value, axis, [(place, place ^ bit) for place in range(count)])]
    all_to_all x0 -> x7, waiting for transfers between devices: none -> 39.8 us  [exchange(): return lax.all_to_all(blocks, 'dp', 0, 0, tiled=True)]
    all_to_all x0 -> x7, starting transfers between devices: none -> 36.6 us  [exchange(): return lax.all_to_all(blocks, 'dp', 0, 0, tiled=True)]
    all_gather x1 -> x0, blocking collectives: 32.3 us -> none  [body(): pair_grad_all = lax.all_gather(pair_grad_b, 'dp', axis=0, tiled=True)]
    all_gather x1, waiting for transfers between devices: 0.01 us -> 30 us  [body(): query_grad_all = lax.all_gather(query_grad_b, 'dp', axis=0, tiled=True)]
  transfers between devices with their start and end apart: 143 -> 75, of which waited for: 71 -> 43; matrix products, arithmetic and copies ran while one was open for 36% -> 31% of each run, Pallas kernels for 0% -> 7%
where the time goes in v2:
time: 910 us; the launch traced here: 901 us
  waiting for transfers between devices  406 us (45%)
  local copies, waits for them, and re-layouts  116 us (13%)
  matrix products  96.7 us (11%)
  starting transfers between devices  93.9 us (10%)
  other arithmetic  91.1 us (10%)
  Pallas kernels  69 us (8%)
  between operations  28.8 us (3%)
    ppermute x63, waiting for transfers between devices, swap(): lax.ppermute(value, axis, [(place, place ^ bit) for place in range(count)])  322 us
    ppermute x63, starting transfers between devices, swap(): lax.ppermute(value, axis, [(place, place ^ bit) for place in range(count)])  56.9 us
    unnamed x298, local copies, waits for them, and re-layouts  51.2 us
    dot_general x14, matrix products, dot_rows(): lax.dot_general(left, right, (((0,), (0,)), ((), ())), preferred_element_...  41.3 us
    all_to_all x7, waiting for transfers between devices, exchange(): return lax.all_to_all(blocks, 'dp', 0, 0, tiled=True)  39.8 us
    all_to_all x7, starting transfers between devices, exchange(): return lax.all_to_all(blocks, 'dp', 0, 0, tiled=True)  36.6 us
    pallas_call x2, Pallas kernels, feed_forward(): pl.pallas_call(feed_kernel, out_shape=(jax.ShapeDtypeStruct((rows, width)...  34 us
    all_gather x1, waiting for transfers between devices, body(): query_grad_all = lax.all_gather(query_grad_b, 'dp', axis=0, tiled=True)  30 us
  transfers between devices with their start and end apart: 75, of which 43 were waited for; matrix products, arithmetic and copies ran while one was open for 31% of the time, Pallas kernels for 7%

profile of v2, /device:TPU:0, one launch (start us, length us, event | category | flops | bytes accessed | tf_op | source)
XLA Modules:
  0.0 901.5 jit_solution(12275922230128865759)
XLA Ops:
  13.7 4.0 collective-permute-start.2
  21.4 8.9 collective-permute-done.2
  34.2 11.1 %collective-permute-done.5 = bf16[128,2048]{1,0:T(8,128)(2,1)} collective-permute-done((bf16[128,2048]{1,0:T(8,128)(2,1)}, bf16[128,2048]{1,0:T(8,128)(2,1)}, u32[]{:S(2)}, u32[]{:S(2)}) %collective-permute-start.5) | collective-permute-done | bytes 524320 | tf_op jit(solution)/shard_map/ppermute | solution.py:91
  49.6 10.7 %collective-permute-done.6 = bf16[128,2048]{1,0:T(8,128)(2,1)S(1)} collective-permute-done((bf16[128,2048]{1,0:T(8,128)(2,1)}, bf16[128,2048]{1,0:T(8,128)(2,1)S(1)}, u32[]{:S(2)}, u32[]{:S(2)}) %collective-permute-start.6) | collective-permute-done | bytes 524320 | tf_op jit(solution)/shard_map/ppermute | solution.py:91
  63.6 13.2 %all-gather.6.cloned.1.call-done = bf16[2048,512]{1,0:T(8,128)(2,1)} async-done(((bf16[64,512]{1,0:T(8,128)(2,1)}), bf16[2048,512]{1,0:T(8,128)(2,1)}) %all-gather.6.cloned.1.call-update) | async-done | bytes 2097168 | tf_op jit(solution)/shard_map/all_gather | solution.py:409
  80.1 6.0 collective-permute-done
  90.1 10.3 %collective-permute-done.1 = bf16[144,512]{1,0:T(8,128)(2,1)S(1)} collective-permute-done((bf16[144,512]{1,0:T(8,128)(2,1)S(1)}, bf16[144,512]{1,0:T(8,128)(2,1)S(1)}, u32[]{:S(2)}, u32[]{:S(2)}) %collective-permute-start.1) | collective-permute-done | bytes 147488 | tf_op jit(solution)/shard_map/ppermute | solution.py:91
  114.7 3.1 collective-permute-done.9
  122.4 4.0 all-to-all-start
  131.3 11.4 %collective-permute-done.11 = bf16[288,512]{1,0:T(8,128)(2,1)S(1)} collective-permute-done((bf16[288,512]{1,0:T(8,128)(2,1)S(1)}, bf16[288,512]{1,0:T(8,128)(2,1)S(1)}, u32[]{:S(2)}, u32[]{:S(2)}) %collective-permute-start.11) | collective-permute-done | bytes 294944 | tf_op jit(solution)/shard_map/ppermute | solution.py:91
  146.6 7.5 shard_map.442
  154.0 5.4 all-to-all-start.1
  166.7 7.2 collective-permute-done.13
  182.1 3.2 fusion.165
  187.6 3.1 fusion.25
  193.4 4.5 fusion.172
  197.9 4.0 convolution_convert_fusion.7
  213.4 7.1 collective-permute-done.16
  223.8 28.0 %all-to-all-done.1 = bf16[8,256,1024]{2,1,0:T(8,128)(2,1)} async-done(((bf16[8,256,1024]{2,1,0:T(8,128)(2,1)}), bf16[8,256,1024]{2,1,0:T(8,128)(2,1)}, u32[]{:S(2)}, u32[]{:S(2)}) %all-to-all-start.1) | async-done | bytes 4194336 | tf_op jit(solution)/shard_map/all_to_all | solution.py:95
  255.6 12.3 %collective-permute-done.17 = bf16[64,2048]{1,0:T(8,128)(2,1)S(1)} collective-permute-done((bf16[64,2048]{1,0:T(8,128)(2,1)S(1)}, bf16[64,2048]{1,0:T(8,128)(2,1)S(1)}, u32[]{:S(2)}, u32[]{:S(2)}) %collective-permute-start.17) | collective-permute-done | bytes 262176 | tf_op jit(solution)/shard_map/ppermute | solution.py:91
  268.6 13.0 %collective-permute-done.20 = bf16[128,2048]{1,0:T(8,128)(2,1)S(1)} collective-permute-done((bf16[128,2048]{1,0:T(8,128)(2,1)S(1)}, bf16[128,2048]{1,0:T(8,128)(2,1)S(1)}, u32[]{:S(2)}, u32[]{:S(2)}) %collective-permute-start.20) | collective-permute-done | bytes 524320 | tf_op jit(solution)/shard_map/ppermute | solution.py:91
  283.6 6.4 shard_map.443
  290.1 4.7 all-to-all-start.2
  306.1 24.1 %collective-permute-done.18 = bf16[128,2048]{1,0:T(8,128)(2,1)S(1)} collective-permute-done((bf16[128,2048]{1,0:T(8,128)(2,1)}, bf16[128,2048]{1,0:T(8,128)(2,1)S(1)}, u32[]{:S(2)}, u32[]{:S(2)}) %collective-permute-start.18) | collective-permute-done | bytes 524320 | tf_op jit(solution)/shard_map/ppermute | solution.py:91
  336.7 15.5 %collective-permute-done.19 = bf16[256,2048]{1,0:T(8,128)(2,1)S(1)} collective-permute-done((bf16[256,2048]{1,0:T(8,128)(2,1)S(1)}, bf16[256,2048]{1,0:T(8,128)(2,1)S(1)}, u32[]{:S(2)}, u32[]{:S(2)}) %collective-permute-start.19) | collective-permute-done | bytes 1048608 | tf_op jit(solution)/shard_map/ppermute | solution.py:91
  354.9 5.7 collective-permute-done.22
  363.1 4.4 broadcast_add_fusion
  369.2 17.4 %shard_map.444 = (bf16[1024,512]{1,0:T(8,128)(2,1)}, bf16[1024,1024]{1,0:T(8,128)(2,1)}, f32[1024,2048]{1,0:T(8,128)}) custom-call(bf16[1024,2048]{1,0:T(8,128)(2,1)} %constant_dynamic-update-slice_fusion.21.normed_ref, bf16[1024,2048]{1,0:T(8,128)(2,1)} %constant_dynamic-update-slice_fusion.28.cotangent_ref, bf16[2048,1024]{1,0:T(8,128)(2,1)} %bitcast.45.gate_down_ref, ...), custom_call_target="tpu_custom_call" | custom-call | tf_op jit(solution)/shard_map/pallas_call | solution.py:318
  386.6 16.6 %shard_map.445 = (bf16[1024,512]{1,0:T(8,128)(2,1)}, bf16[1024,1024]{1,0:T(8,128)(2,1)}, bf16[1024,2048]{1,0:T(8,128)(2,1)}) custom-call(bf16[1024,2048]{1,0:T(8,128)(2,1)} %collective-permute-done.23.normed_ref, bf16[1024,2048]{1,0:T(8,128)(2,1)} %collective-permute-done.24.cotangent_ref, bf16[2048,1024]{1,0:T(8,128)(2,1)} %bitcast.45.gate_down_ref, ...), custom_call_target="tpu_custom_call" | custom-call | tf_op jit(solution)/shard_map/pallas_call | solution.py:318
  403.7 5.0 fusion.175
  411.2 6.5 fusion.176
  417.8 8.5 add_convert_fusion
  436.0 4.6 all-to-all-start.3
  440.7 10.1 %fusion.159 = (bf16[1024,2048]{1,0:T(8,128)(2,1)S(1)}, f32[1024,2048]{1,0:T(8,128)}) fusion(f32[1024,2048]{1,0:T(8,128)} %get-tuple-element.36, bf16[1024,2048]{1,0:T(8,128)(2,1)} %collective-permute-done.25), kind=kLoop, calls=%fused_computation.427 | loop fusion | flops 6291456 | bytes 25165824 | tf_op jit(solution)/shard_map/convert.54
  460.3 17.4 %collective-permute-done.26 = bf16[256,2048]{1,0:T(8,128)(2,1)S(1)} collective-permute-done((bf16[256,2048]{1,0:T(8,128)(2,1)}, bf16[256,2048]{1,0:T(8,128)(2,1)S(1)}, u32[]{:S(2)}, u32[]{:S(2)}) %collective-permute-start.26) | collective-permute-done | bytes 1048608 | tf_op jit(solution)/shard_map/ppermute | solution.py:91
  477.7 38.9 %collective-permute-done.28 = bf16[256,2048]{1,0:T(8,128)(2,1)S(1)} collective-permute-done((bf16[256,2048]{1,0:T(8,128)(2,1)}, bf16[256,2048]{1,0:T(8,128)(2,1)S(1)}, u32[]{:S(2)}, u32[]{:S(2)}) %collective-permute-start.28) | collective-permute-done | bytes 1048608 | tf_op jit(solution)/shard_map/ppermute | solution.py:91
  516.6 3.0 slice_add_fusion.4
  524.6 17.8 %collective-permute-done.27 = bf16[128,2048]{1,0:T(8,128)(2,1)S(1)} collective-permute-done((bf16[128,2048]{1,0:T(8,128)(2,1)S(1)}, bf16[128,2048]{1,0:T(8,128)(2,1)S(1)}, u32[]{:S(2)}, u32[]{:S(2)}) %collective-permute-start.27) | collective-permute-done | bytes 524320 | tf_op jit(solution)/shard_map/ppermute | solution.py:91
  545.1 5.9 convolution_convert_fusion
  560.5 7.9 collective-permute-done.30
  574.5 8.9 collective-permute-done.31
  588.7 7.0 shard_map.446
  595.7 7.1 shard_map.448
  607.7 5.1 all-to-all-start.4
  620.2 3.4 fusion.1
  625.2 8.7 fusion.173
  646.0 15.0 %collective-permute-done.44 = bf16[256,2048]{1,0:T(8,128)(2,1)} collective-permute-done((bf16[256,2048]{1,0:T(8,128)(2,1)}, bf16[256,2048]{1,0:T(8,128)(2,1)}, u32[]{:S(2)}, u32[]{:S(2)}) %collective-permute-start.44) | collective-permute-done | bytes 1048608 | tf_op jit(solution)/shard_map/ppermute | solution.py:91
  661.0 9.8 %collective-permute-done.46 = bf16[256,2048]{1,0:T(8,128)(2,1)} collective-permute-done((bf16[256,2048]{1,0:T(8,128)(2,1)}, bf16[256,2048]{1,0:T(8,128)(2,1)}, u32[]{:S(2)}, u32[]{:S(2)}) %collective-permute-start.46) | collective-permute-done | bytes 1048608 | tf_op jit(solution)/shard_map/ppermute | solution.py:91
  670.9 5.1 slice_add_fusion
  680.8 5.2 convolution_bitcast_fusion
  693.8 3.7 collective-permute-start.48
  701.3 4.5 collective-permute-done.45
  705.8 7.7 collective-permute-done.48
  718.4 3.9 fusion.6
  722.2 9.1 %all-to-all-start.5 = ((bf16[8,256,512]{2,1,0:T(8,128)(2,1)}), bf16[8,256,512]{2,1,0:T(8,128)(2,1)}, u32[]{:S(2)}, u32[]{:S(2)}) async-start(bf16[8,256,512]{2,1,0:T(8,128)(2,1)} %bitcast.388), calls=%async_computation.5 | async-start | bytes 4194304 | tf_op jit(solution)/shard_map/all_to_all | solution.py:95
  734.4 7.0 shard_map.447
  749.7 30.0 %all-gather.12.cloned.1.call-done = bf16[2048,512]{0,1:T(8,128)(2,1)} async-done(((bf16[256,512]{0,1:T(8,128)(2,1)}), bf16[2048,512]{0,1:T(8,128)(2,1)}) %all-gather.12.cloned.1.call-update) | async-done | bytes 2097168 | tf_op jit(solution)/shard_map/all_gather | solution.py:586
  795.3 3.2 collective-permute-done.62
  830.7 17.4 %collective-permute-done.55 = bf16[64,2048]{1,0:T(8,128)(2,1)S(1)} collective-permute-done((bf16[64,2048]{1,0:T(8,128)(2,1)S(1)}, bf16[64,2048]{1,0:T(8,128)(2,1)S(1)}, u32[]{:S(2)}, u32[]{:S(2)}) %collective-permute-start.55) | collective-permute-done | bytes 262176 | tf_op jit(solution)/shard_map/ppermute | solution.py:91
  851.2 6.7 collective-permute-done.60
  863.9 3.2 fusion.174
  868.7 3.7 all-to-all-start.6
  872.5 3.1 broadcast_select_fusion.4
  880.9 11.8 %all-to-all-done.6 = bf16[8,32,1536]{2,1,0:T(8,128)(2,1)S(1)} async-done(((bf16[8,32,1536]{2,1,0:T(8,128)(2,1)}), bf16[8,32,1536]{2,1,0:T(8,128)(2,1)S(1)}, u32[]{:S(2)}, u32[]{:S(2)}) %all-to-all-start.6) | async-done | bytes 786464 | tf_op jit(solution)/shard_map/all_to_all | solution.py:95
  (610 shorter events, 283.6 us)
Async XLA Ops:
  7.2 69.6 %all-gather.6.cloned.1.call-start = ((), (), s32[]{:S(2)}) async-start(), calls=%async_computation.7 | async-start | bytes 2162688 | tf_op jit(solution)/shard_map/all_gather | solution.py:409
  11.9 175.7 %all-gather.8.cloned.1.call-start = ((), (), s32[]{:S(2)}) async-start(), calls=%async_computation.8 | async-start | bytes 4718592 | tf_op jit(solution)/shard_map/all_gather | solution.py:415
  13.7 16.6 %collective-permute-start.2 = (bf16[64,2048]{1,0:T(8,128)(2,1)S(1)}, bf16[64,2048]{1,0:T(8,128)(2,1)S(1)}, u32[]{:S(2)}, u32[]{:S(2)}) collective-permute-start(bf16[64,2048]{1,0:T(8,128)(2,1)S(1)} %get-tuple-element.62), channel_id=1, source_target_pairs={{0,4},{1,5},{2,6},{3,7},{4,0},{5,1},{6,2},{7,3},{8,12},{9,13},{10,... | collective-permute-start | bytes 786440 | tf_op jit(solution)/shard_map/ppermute | solution.py:91
  31.1 14.1 %collective-permute-start.5 = (bf16[128,2048]{1,0:T(8,128)(2,1)}, bf16[128,2048]{1,0:T(8,128)(2,1)}, u32[]{:S(2)}, u32[]{:S(2)}) collective-permute-start(bf16[128,2048]{1,0:T(8,128)(2,1)} %pad_maximum_fusion.6), channel_id=1, source_target_pairs={{0,2},{1,3},{2,0},{3,1},{4,6},{5,7},{6,4},{7,5},{8,10},{9,11},{10,... | collective-permute-start | bytes 1572872 | tf_op jit(solution)/shard_map/ppermute | solution.py:91
  32.6 14.5 %collective-permute-start.3 = (bf16[128,2048]{1,0:T(8,128)(2,1)}, bf16[128,2048]{1,0:T(8,128)(2,1)S(1)}, u32[]{:S(2)}, u32[]{:S(2)}) collective-permute-start(bf16[128,2048]{1,0:T(8,128)(2,1)} %pad_maximum_fusion.6), channel_id=1, source_target_pairs={{0,1},{1,0},{2,3},{3,2},{4,5},{5,4},{6,7},{7,6},{8,9},{9,8},{10,11... | collective-permute-start | bytes 1572872 | tf_op jit(solution)/shard_map/ppermute | solution.py:91
  45.3 15.1 %collective-permute-start.6 = (bf16[128,2048]{1,0:T(8,128)(2,1)}, bf16[128,2048]{1,0:T(8,128)(2,1)S(1)}, u32[]{:S(2)}, u32[]{:S(2)}) collective-permute-start(bf16[128,2048]{1,0:T(8,128)(2,1)} %collective-permute-done.5), channel_id=1, source_target_pairs={{0,16},{8,24},{16,0},{24,8},{1,17},{9,25},{17,1},{25,9},{2,18},{10... | collective-permute-start | bytes 1572872 | tf_op jit(solution)/shard_map/ppermute | solution.py:91
  48.2 38.1 %collective-permute-start.4 = (bf16[256,2048]{1,0:T(8,128)(2,1)}, bf16[256,2048]{1,0:T(8,128)(2,1)}, u32[]{:S(2)}, u32[]{:S(2)}) collective-permute-start(bf16[256,2048]{1,0:T(8,128)(2,1)} %pad_maximum_fusion.1), channel_id=1, source_target_pairs={{0,16},{8,24},{16,0},{24,8},{1,17},{9,25},{17,1},{25,9},{2,18},{10... | collective-permute-start | bytes 3145736 | tf_op jit(solution)/shard_map/ppermute | solution.py:91
  62.6 25.6 %collective-permute-start.7 = (bf16[256,2048]{1,0:T(8,128)(2,1)}, bf16[256,2048]{1,0:T(8,128)(2,1)}, u32[]{:S(2)}, u32[]{:S(2)}) collective-permute-start(bf16[256,2048]{1,0:T(8,128)(2,1)} %pad_maximum_fusion.2), channel_id=1, source_target_pairs={{0,1},{1,0},{2,3},{3,2},{4,5},{5,4},{6,7},{7,6},{8,9},{9,8},{10,11... | collective-permute-start | bytes 3145736 | tf_op jit(solution)/shard_map/ppermute | solution.py:91
  79.2 7.0 collective-permute-start
  86.2 14.3 %collective-permute-start.1 = (bf16[144,512]{1,0:T(8,128)(2,1)S(1)}, bf16[144,512]{1,0:T(8,128)(2,1)S(1)}, u32[]{:S(2)}, u32[]{:S(2)}) collective-permute-start(bf16[144,512]{1,0:T(8,128)(2,1)S(1)} %pad_maximum_fusion.13), channel_id=1, source_target_pairs={{0,2},{1,3},{2,0},{3,1},{4,6},{5,7},{6,4},{7,5},{8,10},{9,11},{10,... | collective-permute-start | bytes 442376 | tf_op jit(solution)/shard_map/ppermute | solution.py:91
  110.2 7.6 collective-permute-start.9
  122.4 31.7 %all-to-all-start = ((bf16[8,64,256]{2,1,0:T(8,128)(2,1)}), bf16[8,64,256]{2,1,0:T(8,128)(2,1)}, u32[]{:S(2)}, u32[]{:S(2)}) async-start(bf16[8,64,256]{2,1,0:T(8,128)(2,1)} %constant_dynamic-update-slice_fusion.13), calls=%async_computation | async-start | bytes 524288 | tf_op jit(solution)/shard_map/all_to_all | solution.py:95
  127.4 15.2 %collective-permute-start.11 = (bf16[288,512]{1,0:T(8,128)(2,1)S(1)}, bf16[288,512]{1,0:T(8,128)(2,1)S(1)}, u32[]{:S(2)}, u32[]{:S(2)}) collective-permute-start(bf16[288,512]{1,0:T(8,128)(2,1)S(1)} %pad_maximum_fusion.12), channel_id=1, source_target_pairs={{0,1},{1,0},{2,3},{3,2},{4,5},{5,4},{6,7},{7,6},{8,9},{9,8},{10,11... | collective-permute-start | bytes 884744 | tf_op jit(solution)/shard_map/ppermute | solution.py:91
  154.0 97.7 %all-to-all-start.1 = ((bf16[8,256,1024]{2,1,0:T(8,128)(2,1)}), bf16[8,256,1024]{2,1,0:T(8,128)(2,1)}, u32[]{:S(2)}, u32[]{:S(2)}) async-start(bf16[8,256,1024]{2,1,0:T(8,128)(2,1)} %shard_map.442), calls=%async_computation.1 | async-start | bytes 8388608 | tf_op jit(solution)/shard_map/all_to_all | solution.py:95
  164.9 15.1 %collective-permute-start.12 = (bf16[1152,512]{1,0:T(8,128)(2,1)}, bf16[1152,512]{1,0:T(8,128)(2,1)S(1)}, u32[]{:S(2)}, u32[]{:S(2)}) collective-permute-start(bf16[1152,512]{1,0:T(8,128)(2,1)} %get-tuple-element.116), channel_id=1, source_target_pairs={{0,8},{8,0},{16,24},{24,16},{1,9},{9,1},{17,25},{25,17},{2,10},{10... | collective-permute-start | bytes 3538952 | tf_op jit(solution)/shard_map/ppermute | solution.py:91
  164.9 9.0 collective-permute-start.13
  211.6 8.9 collective-permute-start.16
  255.6 12.3 %collective-permute-start.17 = (bf16[64,2048]{1,0:T(8,128)(2,1)S(1)}, bf16[64,2048]{1,0:T(8,128)(2,1)S(1)}, u32[]{:S(2)}, u32[]{:S(2)}) collective-permute-start(bf16[64,2048]{1,0:T(8,128)(2,1)S(1)} %get-tuple-element.64), channel_id=1, source_target_pairs={{0,4},{1,5},{2,6},{3,7},{4,0},{5,1},{6,2},{7,3},{8,12},{9,13},{10,... | collective-permute-start | bytes 786440 | tf_op jit(solution)/shard_map/ppermute | solution.py:91
  268.6 13.0 %collective-permute-start.20 = (bf16[128,2048]{1,0:T(8,128)(2,1)S(1)}, bf16[128,2048]{1,0:T(8,128)(2,1)S(1)}, u32[]{:S(2)}, u32[]{:S(2)}) collective-permute-start(bf16[128,2048]{1,0:T(8,128)(2,1)S(1)} %pad_maximum_fusion.8), channel_id=1, source_target_pairs={{0,2},{1,3},{2,0},{3,1},{4,6},{5,7},{6,4},{7,5},{8,10},{9,11},{10,... | collective-permute-start | bytes 1572872 | tf_op jit(solution)/shard_map/ppermute | solution.py:91
  290.1 71.6 %all-to-all-start.2 = ((bf16[8,256,512]{2,1,0:T(8,128)(2,1)}), bf16[8,256,512]{2,1,0:T(8,128)(2,1)S(1)}, u32[]{:S(2)}, u32[]{:S(2)}) async-start(bf16[8,256,512]{2,1,0:T(8,128)(2,1)} %shard_map.443), calls=%async_computation.2 | async-start | bytes 4194304 | tf_op jit(solution)/shard_map/all_to_all | solution.py:95
  294.8 132.8 %all-gather.10.cloned.1.call-start = ((), (), s32[]{:S(2)}) async-start(), calls=%async_computation.9 | async-start | bytes 3244032 | tf_op jit(solution)/shard_map/all_gather | solution.py:496
  296.6 33.6 %collective-permute-start.18 = (bf16[128,2048]{1,0:T(8,128)(2,1)}, bf16[128,2048]{1,0:T(8,128)(2,1)S(1)}, u32[]{:S(2)}, u32[]{:S(2)}) collective-permute-start(bf16[128,2048]{1,0:T(8,128)(2,1)} %copy-done.84), channel_id=1, source_target_pairs={{0,1},{1,0},{2,3},{3,2},{4,5},{5,4},{6,7},{7,6},{8,9},{9,8},{10,11... | collective-permute-start | bytes 1572872 | tf_op jit(solution)/shard_map/ppermute | solution.py:91
  304.7 30.2 %collective-permute-start.21 = (bf16[128,2048]{1,0:T(8,128)(2,1)S(1)}, bf16[128,2048]{1,0:T(8,128)(2,1)S(1)}, u32[]{:S(2)}, u32[]{:S(2)}) collective-permute-start(bf16[128,2048]{1,0:T(8,128)(2,1)S(1)} %copy-done.60), channel_id=1, source_target_pairs={{0,16},{8,24},{16,0},{24,8},{1,17},{9,25},{17,1},{25,9},{2,18},{10... | collective-permute-start | bytes 1572872 | tf_op jit(solution)/shard_map/ppermute | solution.py:91
  330.3 21.8 %collective-permute-start.19 = (bf16[256,2048]{1,0:T(8,128)(2,1)S(1)}, bf16[256,2048]{1,0:T(8,128)(2,1)S(1)}, u32[]{:S(2)}, u32[]{:S(2)}) collective-permute-start(bf16[256,2048]{1,0:T(8,128)(2,1)S(1)} %pad_maximum_fusion.3), channel_id=1, source_target_pairs={{0,16},{8,24},{16,0},{24,8},{1,17},{9,25},{17,1},{25,9},{2,18},{10... | collective-permute-start | bytes 3145736 | tf_op jit(solution)/shard_map/ppermute | solution.py:91
  334.9 51.7 %collective-permute-start.24 = (bf16[1024,2048]{1,0:T(8,128)(2,1)}, bf16[1024,2048]{1,0:T(8,128)(2,1)}, u32[]{:S(2)}, u32[]{:S(2)}) collective-permute-start(bf16[1024,2048]{1,0:T(8,128)(2,1)} %constant_dynamic-update-slice_fusion.28.cotangent_ref), channel_id=1, source_target_pairs={{0,8},{8,0},{16,24},{24,16},{1,9},{9,1},{17,25},{25,17},{2,10},{10... | collective-permute-start | bytes 12582920 | tf_op jit(solution)/shard_map/ppermute | solution.py:91
  335.0 25.6 %collective-permute-start.22 = (bf16[256,2048]{1,0:T(8,128)(2,1)S(1)}, bf16[256,2048]{1,0:T(8,128)(2,1)S(1)}, u32[]{:S(2)}, u32[]{:S(2)}) collective-permute-start(bf16[256,2048]{1,0:T(8,128)(2,1)S(1)} %pad_maximum_fusion.4), channel_id=1, source_target_pairs={{0,1},{1,0},{2,3},{3,2},{4,5},{5,4},{6,7},{7,6},{8,9},{9,8},{10,11... | collective-permute-start | bytes 3145736 | tf_op jit(solution)/shard_map/ppermute | solution.py:91
  367.5 19.1 %collective-permute-start.23 = (bf16[1024,2048]{1,0:T(8,128)(2,1)}, bf16[1024,2048]{1,0:T(8,128)(2,1)}, u32[]{:S(2)}, u32[]{:S(2)}) collective-permute-start(bf16[1024,2048]{1,0:T(8,128)(2,1)} %broadcast_add_fusion), channel_id=1, source_target_pairs={{0,8},{8,0},{16,24},{24,16},{1,9},{9,1},{17,25},{25,17},{2,10},{10... | collective-permute-start | bytes 12582920 | tf_op jit(solution)/shard_map/ppermute | solution.py:91
  403.2 37.4 %collective-permute-start.25 = (bf16[1024,2048]{1,0:T(8,128)(2,1)}, bf16[1024,2048]{1,0:T(8,128)(2,1)}, u32[]{:S(2)}, u32[]{:S(2)}) collective-permute-start(bf16[1024,2048]{1,0:T(8,128)(2,1)} %get-tuple-element.37), channel_id=1, source_target_pairs={{0,8},{8,0},{16,24},{24,16},{1,9},{9,1},{17,25},{25,17},{2,10},{10... | collective-permute-start | bytes 12582920 | tf_op jit(solution)/shard_map/ppermute | solution.py:91
  436.0 115.0 %all-to-all-start.3 = ((bf16[8,576,512]{2,1,0:T(8,128)(2,1)}), bf16[8,576,512]{2,1,0:T(8,128)(2,1)}, u32[]{:S(2)}, u32[]{:S(2)}) async-start(bf16[8,576,512]{2,1,0:T(8,128)(2,1)} %pad_maximum_fusion), calls=%async_computation.3 | async-start | bytes 9437184 | tf_op jit(solution)/shard_map/all_to_all | solution.py:95
  452.2 25.5 %collective-permute-start.26 = (bf16[256,2048]{1,0:T(8,128)(2,1)}, bf16[256,2048]{1,0:T(8,128)(2,1)S(1)}, u32[]{:S(2)}, u32[]{:S(2)}) collective-permute-start(bf16[256,2048]{1,0:T(8,128)(2,1)} %get-tuple-element.95), channel_id=1, source_target_pairs={{0,16},{8,24},{16,0},{24,8},{1,17},{9,25},{17,1},{25,9},{2,18},{10... | collective-permute-start | bytes 3145736 | tf_op jit(solution)/shard_map/ppermute | solution.py:91
  453.6 63.0 %collective-permute-start.28 = (bf16[256,2048]{1,0:T(8,128)(2,1)}, bf16[256,2048]{1,0:T(8,128)(2,1)S(1)}, u32[]{:S(2)}, u32[]{:S(2)}) collective-permute-start(bf16[256,2048]{1,0:T(8,128)(2,1)} %get-tuple-element.96), channel_id=1, source_target_pairs={{0,1},{1,0},{2,3},{3,2},{4,5},{5,4},{6,7},{7,6},{8,9},{9,8},{10,11... | collective-permute-start | bytes 3145736 | tf_op jit(solution)/shard_map/ppermute | solution.py:91
  519.7 22.7 %collective-permute-start.27 = (bf16[128,2048]{1,0:T(8,128)(2,1)S(1)}, bf16[128,2048]{1,0:T(8,128)(2,1)S(1)}, u32[]{:S(2)}, u32[]{:S(2)}) collective-permute-start(bf16[128,2048]{1,0:T(8,128)(2,1)S(1)} %slice.886), channel_id=1, source_target_pairs={{0,1},{1,0},{2,3},{3,2},{4,5},{5,4},{6,7},{7,6},{8,9},{9,8},{10,11... | collective-permute-start | bytes 1572872 | tf_op jit(solution)/shard_map/ppermute | solution.py:91
  520.4 23.4 %collective-permute-start.29 = (bf16[128,2048]{1,0:T(8,128)(2,1)S(1)}, bf16[128,2048]{1,0:T(8,128)(2,1)S(1)}, u32[]{:S(2)}, u32[]{:S(2)}) collective-permute-start(bf16[128,2048]{1,0:T(8,128)(2,1)S(1)} %slice.885), channel_id=1, source_target_pairs={{0,16},{8,24},{16,0},{24,8},{1,17},{9,25},{17,1},{25,9},{2,18},{10... | collective-permute-start | bytes 1572872 | tf_op jit(solution)/shard_map/ppermute | solution.py:91
  551.1 73.7 %collective-permute-start.43 = (bf16[1024,2048]{1,0:T(8,128)(2,1)}, bf16[1024,2048]{1,0:T(8,128)(2,1)}, u32[]{:S(2)}, u32[]{:S(2)}) collective-permute-start(bf16[1024,2048]{1,0:T(8,128)(2,1)} %convolution_convert_fusion), channel_id=1, source_target_pairs={{0,8},{8,0},{16,24},{24,16},{1,9},{9,1},{17,25},{25,17},{2,10},{10... | collective-permute-start | bytes 12582920 | tf_op jit(solution)/shard_map/ppermute | solution.py:91
  553.2 15.3 %collective-permute-start.30 = (bf16[128,2048]{1,0:T(8,128)(2,1)S(1)}, bf16[128,2048]{1,0:T(8,128)(2,1)S(1)}, u32[]{:S(2)}, u32[]{:S(2)}) collective-permute-start(bf16[128,2048]{1,0:T(8,128)(2,1)S(1)} %slice.884), channel_id=1, source_target_pairs={{0,2},{1,3},{2,0},{3,1},{4,6},{5,7},{6,4},{7,5},{8,10},{9,11},{10,... | collective-permute-start | bytes 1572872 | tf_op jit(solution)/shard_map/ppermute | solution.py:91
  568.6 14.7 %collective-permute-start.31 = (bf16[64,2048]{1,0:T(8,128)(2,1)S(1)}, bf16[64,2048]{1,0:T(8,128)(2,1)S(1)}, u32[]{:S(2)}, u32[]{:S(2)}) collective-permute-start(bf16[64,2048]{1,0:T(8,128)(2,1)S(1)} %slice.888), channel_id=1, source_target_pairs={{0,4},{1,5},{2,6},{3,7},{4,0},{5,1},{6,2},{7,3},{8,12},{9,13},{10,... | collective-permute-start | bytes 786440 | tf_op jit(solution)/shard_map/ppermute | solution.py:91
  584.4 18.4 %collective-permute-start.32 = (bf16[64,2048]{1,0:T(8,128)(2,1)S(1)}, bf16[64,2048]{1,0:T(8,128)(2,1)S(1)}, u32[]{:S(2)}, u32[]{:S(2)}) collective-permute-start(bf16[64,2048]{1,0:T(8,128)(2,1)S(1)} %fusion.157), channel_id=1, source_target_pairs={{0,16},{8,24},{16,0},{24,8},{1,17},{9,25},{17,1},{25,9},{2,18},{10... | collective-permute-start | bytes 786440 | tf_op jit(solution)/shard_map/ppermute | solution.py:91
  603.6 10.7 %collective-permute-start.33 = (bf16[2,64,2048]{2,1,0:T(8,128)(2,1)}, bf16[2,64,2048]{2,1,0:T(8,128)(2,1)}, u32[]{:S(2)}, u32[]{:S(2)}) collective-permute-start(bf16[2,64,2048]{2,1,0:T(8,128)(2,1)} %maximum_select_fusion.9), channel_id=1, source_target_pairs={{0,8},{8,0},{16,24},{24,16},{1,9},{9,1},{17,25},{25,17},{2,10},{10... | collective-permute-start | bytes 1572872 | tf_op jit(solution)/shard_map/ppermute | solution.py:91
  607.7 108.5 %all-to-all-start.4 = ((bf16[8,288,512]{2,1,0:T(8,128)(2,1)}), bf16[8,288,512]{2,1,0:T(8,128)(2,1)S(1)}, u32[]{:S(2)}, u32[]{:S(2)}) async-start(bf16[8,288,512]{2,1,0:T(8,128)(2,1)} %maximum_add_fusion.1), calls=%async_computation.4 | async-start | bytes 4718592 | tf_op jit(solution)/shard_map/all_to_all | solution.py:95
  612.8 167.0 %all-gather.12.cloned.1.call-start = ((), (), s32[]{:S(2)}) async-start(), calls=%async_computation.10 | async-start | bytes 2359296 | tf_op jit(solution)/shard_map/all_gather | solution.py:586
  635.4 25.6 %collective-permute-start.44 = (bf16[256,2048]{1,0:T(8,128)(2,1)}, bf16[256,2048]{1,0:T(8,128)(2,1)}, u32[]{:S(2)}, u32[]{:S(2)}) collective-permute-start(bf16[256,2048]{1,0:T(8,128)(2,1)} %get-tuple-element.92), channel_id=1, source_target_pairs={{0,16},{8,24},{16,0},{24,8},{1,17},{9,25},{17,1},{25,9},{2,18},{10... | collective-permute-start | bytes 3145736 | tf_op jit(solution)/shard_map/ppermute | solution.py:91
  636.0 34.8 %collective-permute-start.46 = (bf16[256,2048]{1,0:T(8,128)(2,1)}, bf16[256,2048]{1,0:T(8,128)(2,1)}, u32[]{:S(2)}, u32[]{:S(2)}) collective-permute-start(bf16[256,2048]{1,0:T(8,128)(2,1)} %get-tuple-element.91), channel_id=1, source_target_pairs={{0,1},{1,0},{2,3},{3,2},{4,5},{5,4},{6,7},{7,6},{8,9},{9,8},{10,11... | collective-permute-start | bytes 3145736 | tf_op jit(solution)/shard_map/ppermute | solution.py:91
  646.0 51.5 %collective-permute-start.34 = (bf16[2,64,2048]{2,1,0:T(8,128)(2,1)}, bf16[2,64,2048]{2,1,0:T(8,128)(2,1)}, u32[]{:S(2)}, u32[]{:S(2)}) collective-permute-start(bf16[2,64,2048]{2,1,0:T(8,128)(2,1)} %fusion.55), channel_id=1, source_target_pairs={{0,8},{8,0},{16,24},{24,16},{1,9},{9,1},{17,25},{25,17},{2,10},{10... | collective-permute-start | bytes 1572872 | tf_op jit(solution)/shard_map/ppermute | solution.py:91
  678.2 14.2 %collective-permute-start.47 = (bf16[128,2048]{1,0:T(8,128)(2,1)}, bf16[128,2048]{1,0:T(8,128)(2,1)}, u32[]{:S(2)}, u32[]{:S(2)}) collective-permute-start(bf16[128,2048]{1,0:T(8,128)(2,1)} %slice.882), channel_id=1, source_target_pairs={{0,16},{8,24},{16,0},{24,8},{1,17},{9,25},{17,1},{25,9},{2,18},{10... | collective-permute-start | bytes 1572872 | tf_op jit(solution)/shard_map/ppermute | solution.py:91
  689.3 16.4 %collective-permute-start.45 = (bf16[128,2048]{1,0:T(8,128)(2,1)S(1)}, bf16[128,2048]{1,0:T(8,128)(2,1)S(1)}, u32[]{:S(2)}, u32[]{:S(2)}) collective-permute-start(bf16[128,2048]{1,0:T(8,128)(2,1)S(1)} %slice.883), channel_id=1, source_target_pairs={{0,1},{1,0},{2,3},{3,2},{4,5},{5,4},{6,7},{7,6},{8,9},{9,8},{10,11... | collective-permute-start | bytes 1572872 | tf_op jit(solution)/shard_map/ppermute | solution.py:91
  693.8 19.6 %collective-permute-start.48 = (bf16[128,2048]{1,0:T(8,128)(2,1)S(1)}, bf16[128,2048]{1,0:T(8,128)(2,1)S(1)}, u32[]{:S(2)}, u32[]{:S(2)}) collective-permute-start(bf16[128,2048]{1,0:T(8,128)(2,1)S(1)} %fusion.37), channel_id=1, source_target_pairs={{0,2},{1,3},{2,0},{3,1},{4,6},{5,7},{6,4},{7,5},{8,10},{9,11},{10,... | collective-permute-start | bytes 1572872 | tf_op jit(solution)/shard_map/ppermute | solution.py:91
  699.5 104.6 %collective-permute-start.35 = (bf16[64,2048]{1,0:T(8,128)(2,1)}, bf16[64,2048]{1,0:T(8,128)(2,1)}, u32[]{:S(2)}, u32[]{:S(2)}) collective-permute-start(bf16[64,2048]{1,0:T(8,128)(2,1)} %fusion.64), channel_id=1, source_target_pairs={{0,16},{8,24},{16,0},{24,8},{1,17},{9,25},{17,1},{25,9},{2,18},{10... | collective-permute-start | bytes 786440 | tf_op jit(solution)/shard_map/ppermute | solution.py:91
  714.7 92.2 %collective-permute-start.49 = (bf16[64,2048]{1,0:T(8,128)(2,1)}, bf16[64,2048]{1,0:T(8,128)(2,1)}, u32[]{:S(2)}, u32[]{:S(2)}) collective-permute-start(bf16[64,2048]{1,0:T(8,128)(2,1)} %slice.887), channel_id=1, source_target_pairs={{0,4},{1,5},{2,6},{3,7},{4,0},{5,1},{6,2},{7,3},{8,12},{9,13},{10,... | collective-permute-start | bytes 786440 | tf_op jit(solution)/shard_map/ppermute | solution.py:91
  722.2 77.3 %all-to-all-start.5 = ((bf16[8,256,512]{2,1,0:T(8,128)(2,1)}), bf16[8,256,512]{2,1,0:T(8,128)(2,1)}, u32[]{:S(2)}, u32[]{:S(2)}) async-start(bf16[8,256,512]{2,1,0:T(8,128)(2,1)} %bitcast.388), calls=%async_computation.5 | async-start | bytes 4194304 | tf_op jit(solution)/shard_map/all_to_all | solution.py:95
  731.3 132.5 %all-gather.14.cloned.1.call-start = ((), (), s32[]{:S(2)}) async-start(), calls=%async_computation.11 | async-start | bytes 2162688 | tf_op jit(solution)/shard_map/all_gather | solution.py:587
  734.4 11.4 %collective-permute-start.36 = (bf16[1024,512]{1,0:T(8,128)(2,1)S(1)}, bf16[1024,512]{1,0:T(8,128)(2,1)S(1)}, u32[]{:S(2)}, u32[]{:S(2)}) collective-permute-start(bf16[1024,512]{1,0:T(8,128)(2,1)S(1)} %slice.881), channel_id=1, source_target_pairs={{0,8},{8,0},{16,24},{24,16},{1,9},{9,1},{17,25},{25,17},{2,10},{10... | collective-permute-start | bytes 3145736 | tf_op jit(solution)/shard_map/ppermute | solution.py:91
  742.9 43.3 %collective-permute-start.61 = (f32[256,768]{1,0:T(8,128)}, f32[256,768]{1,0:T(8,128)}, u32[]{:S(2)}, u32[]{:S(2)}) collective-permute-start(f32[256,768]{1,0:T(8,128)} %constant_dynamic-update-slice_fusion.35), channel_id=1, source_target_pairs={{0,8},{8,0},{16,24},{24,16},{1,9},{9,1},{17,25},{25,17},{2,10},{10... | collective-permute-start | bytes 2359304 | tf_op jit(solution)/shard_map/ppermute | solution.py:91
  747.0 36.5 %collective-permute-start.37 = (bf16[256,512]{1,0:T(8,128)(2,1)}, bf16[256,512]{1,0:T(8,128)(2,1)S(1)}, u32[]{:S(2)}, u32[]{:S(2)}) collective-permute-start(bf16[256,512]{1,0:T(8,128)(2,1)} %get-tuple-element.103), channel_id=1, source_target_pairs={{0,16},{8,24},{16,0},{24,8},{1,17},{9,25},{17,1},{25,9},{2,18},{10... | collective-permute-start | bytes 786440 | tf_op jit(solution)/shard_map/ppermute | solution.py:91
  747.8 35.7 %collective-permute-start.39 = (bf16[256,512]{1,0:T(8,128)(2,1)}, bf16[256,512]{1,0:T(8,128)(2,1)S(1)}, u32[]{:S(2)}, u32[]{:S(2)}) collective-permute-start(bf16[256,512]{1,0:T(8,128)(2,1)} %get-tuple-element.102), channel_id=1, source_target_pairs={{0,1},{1,0},{2,3},{3,2},{4,5},{5,4},{6,7},{7,6},{8,9},{9,8},{10,11... | collective-permute-start | bytes 786440 | tf_op jit(solution)/shard_map/ppermute | solution.py:91
  783.6 6.5 collective-permute-start.40
  787.7 10.9 %collective-permute-start.62 = (bf16[256,768]{1,0:T(8,128)(2,1)S(1)}, bf16[256,768]{1,0:T(8,128)(2,1)S(1)}, u32[]{:S(2)}, u32[]{:S(2)}) collective-permute-start(bf16[256,768]{1,0:T(8,128)(2,1)S(1)} %add_convert_fusion.2), channel_id=1, source_target_pairs={{0,16},{8,24},{16,0},{24,8},{1,17},{9,25},{17,1},{25,9},{2,18},{10... | collective-permute-start | bytes 1179656 | tf_op jit(solution)/shard_map/ppermute | solution.py:91
  795.2 6.3 collective-permute-start.42
  825.3 23.7 %collective-permute-start.59 = (f32[256,512]{0,1:T(8,128)S(1)}, f32[256,512]{0,1:T(8,128)S(1)}, u32[]{:S(2)}, u32[]{:S(2)}) collective-permute-start(f32[256,512]{0,1:T(8,128)S(1)} %pad_maximum_fusion.9), channel_id=1, source_target_pairs={{0,8},{8,0},{16,24},{24,16},{1,9},{9,1},{17,25},{25,17},{2,10},{10... | collective-permute-start | bytes 1572872 | tf_op jit(solution)/shard_map/ppermute | solution.py:91
  825.4 24.4 %collective-permute-start.57 = (f32[64,2048]{1,0:T(8,128)S(1)}, f32[64,2048]{1,0:T(8,128)S(1)}, u32[]{:S(2)}, u32[]{:S(2)}) collective-permute-start(f32[64,2048]{1,0:T(8,128)S(1)} %get-tuple-element.113), channel_id=1, source_target_pairs={{0,16},{8,24},{16,0},{24,8},{1,17},{9,25},{17,1},{25,9},{2,18},{10... | collective-permute-start | bytes 1572872 | tf_op jit(solution)/shard_map/ppermute | solution.py:91
  827.2 20.9 %collective-permute-start.55 = (bf16[64,2048]{1,0:T(8,128)(2,1)S(1)}, bf16[64,2048]{1,0:T(8,128)(2,1)S(1)}, u32[]{:S(2)}, u32[]{:S(2)}) collective-permute-start(bf16[64,2048]{1,0:T(8,128)(2,1)S(1)} %get-tuple-element.54), channel_id=1, source_target_pairs={{0,16},{8,24},{16,0},{24,8},{1,17},{9,25},{17,1},{25,9},{2,18},{10... | collective-permute-start | bytes 786440 | tf_op jit(solution)/shard_map/ppermute | solution.py:91
  849.0 12.5 %collective-permute-start.56 = (bf16[2,64,2048]{2,1,0:T(8,128)(2,1)}, bf16[2,64,2048]{2,1,0:T(8,128)(2,1)}, u32[]{:S(2)}, u32[]{:S(2)}) collective-permute-start(bf16[2,64,2048]{2,1,0:T(8,128)(2,1)} %maximum_select_fusion.10), channel_id=1, source_target_pairs={{0,8},{8,0},{16,24},{24,16},{1,9},{9,1},{17,25},{25,17},{2,10},{10... | collective-permute-start | bytes 1572872 | tf_op jit(solution)/shard_map/ppermute | solution.py:91
  849.2 8.8 collective-permute-start.60
  850.9 24.7 %collective-permute-start.58 = (f32[2,64,2048]{2,1,0:T(8,128)}, f32[2,64,2048]{2,1,0:T(8,128)}, u32[]{:S(2)}, u32[]{:S(2)}) collective-permute-start(f32[2,64,2048]{2,1,0:T(8,128)} %maximum_select_fusion.5), channel_id=1, source_target_pairs={{0,8},{8,0},{16,24},{24,16},{1,9},{9,1},{17,25},{25,17},{2,10},{10... | collective-permute-start | bytes 3145736 | tf_op jit(solution)/shard_map/ppermute | solution.py:91
  868.7 23.9 %all-to-all-start.6 = ((bf16[8,32,1536]{2,1,0:T(8,128)(2,1)}), bf16[8,32,1536]{2,1,0:T(8,128)(2,1)S(1)}, u32[]{:S(2)}, u32[]{:S(2)}) async-start(bf16[8,32,1536]{2,1,0:T(8,128)(2,1)} %pad_maximum_fusion.5), calls=%async_computation.6 | async-start | bytes 1572864 | tf_op jit(solution)/shard_map/all_to_all | solution.py:95
  (139 other events, 2764.7 us)
Sparse Core Ops, SparseCore 0:
  12.0 64.6 all-gather.5
  79.5 84.0 all-gather.7
  369.3 58.1 all-gather.9
  688.0 91.7 all-gather.11
  804.2 55.0 all-gather.13

commit v3 on v2

--- a/solution.py
+++ b/solution.py
@@ -167,8 +167,12 @@
     return swap(value, "mp", 1)
 
 
-def scatter_near(sent, kept):
-    value = kept + swap(sent.astype(bf16), "mp", 1).astype(f32)
+def add_core(sent, kept):
+    return kept + swap(sent.astype(bf16), "mp", 1).astype(f32)
+
+
+def scatter_near(value):
+    value = value.astype(f32)
     half = value.shape[0] // 2
     front = fold(fold(value[:half], "mp", 2), "dp", 1)
     rear = fold(fold(value[half:], "dp", 1), "mp", 2)
@@ -234,108 +238,140 @@
     )(loop, *arrays)
 
 
-def receive_kernel(loop_ref, arrived_ref, right_ref, grad_ref, left_grad_ref):
+def receive_kernel(loop_ref, arrived_ref, right_ref, grad_ref, left_grad_ref, right_grad_ref):
     rows = grad_ref.shape[0]
-    block = arrived_ref[0][:rows]
-    grad_ref[...] = block.astype(f32)
-    part = lax.dot_general(
-        block, right_ref[0], (((1,), (1,)), ((), ())), preferred_element_type=f32
-    )
+    width = arrived_ref.shape[2]
+    total = None
+    for place in range(arrived_ref.shape[0]):
+        columns = slice(place * width, (place + 1) * width)
+        block = arrived_ref[place, :rows, :]
+        grad_ref[:, columns] = block.astype(f32)
+        part = lax.dot_general(
+            block, right_ref[0, :, columns], (((1,), (1,)), ((), ())), preferred_element_type=f32
+        )
+        total = part if total is None else total + part
+        right_grad = arrived_ref[place, rows:, :].astype(f32)
+        for loop in range(LOOP_COUNT):
+            right_grad_ref[loop, :, columns] = jnp.where(loop_ref[0] == loop, right_grad, 0.0)
 
     @pl.when(pl.program_id(0) == 0)
     def first():
-        left_grad_ref[...] = part
+        left_grad_ref[...] = total
 
     @pl.when(pl.program_id(0) > 0)
     def later():
-        left_grad_ref[...] += part
-
-
-def receive_grad(loop, arrived, right, rows):
-    places, all_rows, width = arrived.shape
+        left_grad_ref[...] += total
+
+
+def receive_grad(loop, arrived, which, all_rows, right, rows):
+    places, _, width = arrived.shape
     rank = right.shape[1]
+    step = 2
     return pl.pallas_call(
         receive_kernel,
         out_shape=(
             jax.ShapeDtypeStruct((rows, places * width), f32),
             jax.ShapeDtypeStruct((rows, rank), f32),
+            jax.ShapeDtypeStruct((LOOP_COUNT, all_rows - rows, places * width), f32),
         ),
         grid_spec=pltpu.PrefetchScalarGridSpec(
             num_scalar_prefetch=1,
-            grid=(places,),
+            grid=(places // step,),
             in_specs=[
-                pl.BlockSpec((1, all_rows, width), lambda place, loop_ref: (place, 0, 0)),
-                pl.BlockSpec((1, rank, width), lambda place, loop_ref: (loop_ref[0], 0, place)),
+                pl.BlockSpec((step, all_rows, width), lambda place, loop_ref: (place, which, 0)),
+                pl.BlockSpec(
+                    (1, rank, step * width), lambda place, loop_ref: (loop_ref[0], 0, place)
+                ),
             ],
             out_specs=(
-                pl.BlockSpec((rows, width), lambda place, loop_ref: (0, place)),
+                pl.BlockSpec((rows, step * width), lambda place, loop_ref: (0, place)),
                 pl.BlockSpec((rows, rank), lambda place, loop_ref: (0, 0)),
+                pl.BlockSpec(
+                    (LOOP_COUNT, all_rows - rows, step * width),
+                    lambda place, loop_ref: (0, 0, place),
+                ),
             ),
         ),
         compiler_params=pltpu.CompilerParams(vmem_limit_bytes=48 * 2**20),
     )(loop, arrived, right)
 
 
-def feed_kernel(
-    normed_ref, cotangent_ref, gate_down_ref, up_ref, hidden_ref, grads_ref, partial_ref
-):
-    width = up_ref.shape[1]
+def feed_kernel(normed_ref, cotangent_ref, *refs):
+    weights, outs = refs[:-4], refs[-4:]
+    hidden_ref, grads_ref, partial_ref, branch_ref = outs
     normed = normed_ref[...]
-    gate_act = jnp.dot(normed, gate_down_ref[:, :width], preferred_element_type=f32)
-    up_act = jnp.dot(normed, up_ref[...], preferred_element_type=f32)
-    hidden_grad = jnp.dot(
-        cotangent_ref[...], gate_down_ref[:, width:], preferred_element_type=f32
-    )
+    cotangent = cotangent_ref[...]
     scale = math.sqrt(2.0 / math.pi)
-    square = gate_act * gate_act
-    tanh_part = jnp.tanh(scale * (gate_act + 0.044715 * (gate_act * square)))
-    half_sum = 0.5 * (1.0 + tanh_part)
-    gelu = gate_act * half_sum
-    slope = half_sum + (0.5 * gate_act) * (1.0 - tanh_part * tanh_part) * (
-        scale * (1.0 + (3.0 * 0.044715) * square)
-    )
-    hidden_ref[...] = (gelu * up_act).astype(bf16)
-    gate_grad = (hidden_grad * up_act * slope).astype(bf16)
-    up_grad = (hidden_grad * gelu).astype(bf16)
-    grads_ref[:, :width] = gate_grad
-    grads_ref[:, width:] = up_grad
-    partial = lax.dot_general(
-        gate_grad,
-        gate_down_ref[:, :width],
-        (((1,), (1,)), ((), ())),
-        preferred_element_type=f32,
-    ) + lax.dot_general(
-        up_grad, up_ref[...], (((1,), (1,)), ((), ())), preferred_element_type=f32
-    )
-    partial_ref[...] = partial.astype(partial_ref.dtype)
-
-
-def feed_forward(normed, cotangent, gate_down, up, kind):
+    partial = None
+    for index in range(len(weights) // 2):
+        gate_down_ref, up_ref = weights[2 * index : 2 * index + 2]
+        width = up_ref.shape[1]
+        gate_act = jnp.dot(normed, gate_down_ref[:, :width], preferred_element_type=f32)
+        up_act = jnp.dot(normed, up_ref[...], preferred_element_type=f32)
+        hidden_grad = jnp.dot(cotangent, gate_down_ref[:, width:], preferred_element_type=f32)
+        square = gate_act * gate_act
+        tanh_part = jnp.tanh(scale * (gate_act + 0.044715 * (gate_act * square)))
+        half_sum = 0.5 * (1.0 + tanh_part)
+        gelu = gate_act * half_sum
+        slope = half_sum + (0.5 * gate_act) * (1.0 - tanh_part * tanh_part) * (
+            scale * (1.0 + (3.0 * 0.044715) * square)
+        )
+        hidden = (gelu * up_act).astype(bf16)
+        gate_grad = (hidden_grad * up_act * slope).astype(bf16)
+        up_grad = (hidden_grad * gelu).astype(bf16)
+        hidden_ref[:, index * width : (index + 1) * width] = hidden
+        grads_ref[:, 2 * index * width : (2 * index + 1) * width] = gate_grad
+        grads_ref[:, (2 * index + 1) * width : (2 * index + 2) * width] = up_grad
+        sums = [
+            lax.dot_general(
+                left, right, (((1,), (1,)), ((), ())), preferred_element_type=f32
+            )
+            for left, right in (
+                (gate_grad, gate_down_ref[:, :width]),
+                (up_grad, up_ref[...]),
+                (hidden, gate_down_ref[:, width:]),
+            )
+        ]
+        if partial is None:
+            partial = sums[0] + sums[1]
+            branch = sums[2]
+        else:
+            partial = partial + sums[0] + sums[1]
+            branch = branch + sums[2]
+    partial_ref[...] = partial
+    branch_ref[...] = branch.astype(bf16)
+
+
+def feed_forward(normed, cotangent, weights):
     rows, model_width = normed.shape
-    width = up.shape[1]
+    width = weights[1].shape[1]
+    pairs = len(weights) // 2
     tile = math.gcd(rows, 256)
     row_block = pl.BlockSpec((tile, model_width), lambda step: (step, 0))
     return pl.pallas_call(
         feed_kernel,
         out_shape=(
-            jax.ShapeDtypeStruct((rows, width), bf16),
-            jax.ShapeDtypeStruct((rows, 2 * width), bf16),
-            jax.ShapeDtypeStruct((rows, model_width), kind),
+            jax.ShapeDtypeStruct((rows, pairs * width), bf16),
+            jax.ShapeDtypeStruct((rows, 2 * pairs * width), bf16),
+            jax.ShapeDtypeStruct((rows, model_width), f32),
+            jax.ShapeDtypeStruct((rows, model_width), bf16),
         ),
         grid=(rows // tile,),
-        in_specs=[
-            row_block,
-            row_block,
-            pl.BlockSpec((model_width, 2 * width), lambda step: (0, 0)),
-            pl.BlockSpec((model_width, width), lambda step: (0, 0)),
+        in_specs=[row_block, row_block]
+        + [
+            pl.BlockSpec(
+                weight.shape, lambda step: (0, 0), pipeline_mode=pl.Buffered(1)
+            )
+            for weight in weights
         ],
         out_specs=(
-            pl.BlockSpec((tile, width), lambda step: (step, 0)),
-            pl.BlockSpec((tile, 2 * width), lambda step: (step, 0)),
+            pl.BlockSpec((tile, pairs * width), lambda step: (step, 0)),
+            pl.BlockSpec((tile, 2 * pairs * width), lambda step: (step, 0)),
+            row_block,
             row_block,
         ),
         compiler_params=pltpu.CompilerParams(vmem_limit_bytes=56 * 2**20),
-    )(normed, cotangent, gate_down, up)
+    )(normed, cotangent, *weights)
 
 
 def body(
@@ -424,14 +460,14 @@
     o_full = q_o_full[:, query_cols:]
 
     cotangent_own = own_slice(cotangent)
-    cotangent_front = gather_near(gather_far(cotangent_own))
-    cotangent_rear = other_core(cotangent_front)
+    cotangent_rows = gather_near(gather_far(cotangent_own))
 
     tokens_own = own_slice(tokens).astype(f32)
     normed_b = rms_norm(tokens.astype(f32), attention_norm_gain).astype(bf16)
 
-    def all_token_cols(rows_own):
-        cols = exchange(to_places(rows_own, block_width)).reshape(-1, block_width)
+    def all_token_cols(rows_own, *others):
+        cols = exchange(after(to_places(rows_own, block_width), *others))
+        cols = cols.reshape(-1, block_width)
         cols = gather_mp(cols).reshape(mp_count, dp_count, own_rows, block_width)
         return jnp.swapaxes(cols, 0, 1).reshape(dp_count * row_count, block_width)
 
@@ -449,7 +485,7 @@
         axis=1,
     )
     outgoing = jnp.concatenate([outgoing, marks], axis=0)
-    pairs_far = after(gather_far(outgoing), *halves(cotangent_front))
+    pairs_far = after(gather_far(outgoing), *halves(cotangent_rows))
     pairs_front = gather_near(pairs_far)
     all_pairs = jnp.concatenate([pairs_front, other_core(pairs_front)], axis=0)
     all_pairs = all_pairs.reshape(-1, own_rows + 8, 2 * HEAD_SIZE)
@@ -490,23 +526,23 @@
             [(up_matrix, up_update_left, up_update_right)],
         )
     ).reshape(model_width, hidden_own)
-    normed2_front = gather_near(normed2_far)
-    normed2_rear = other_core(after(normed2_front, up_own))
+    normed2_rows = gather_near(normed2_far)
+    attended_all = lax.all_gather(attended_b, "dp", axis=0, tiled=True)
     left_block = jnp.concatenate([gate_left, up_left, down_left], axis=1)
     left_all = lax.all_gather(
         after(block_slice(left_block), gate_down), ("dp", "mp"), axis=0, tiled=True
     )
-
-    hidden_front, grads_front, partial_front = feed_forward(
-        normed2_front, cotangent_front, gate_down, up_own, f32
-    )
-    hidden_rear, grads_rear, partial_rear = feed_forward(
-        normed2_rear, cotangent_rear, gate_down, up_own, bf16
-    )
-    normed2_near = scatter_near(partial_rear, partial_front)
-
-    def weight_grad(front, rear, grads_front, grads_rear):
-        return (dot_rows(front, grads_front) + dot_rows(rear, grads_rear)).astype(bf16)
+    gate_down_other = swap(gate_down, "mp", 1)
+    up_other = swap(after(up_own, *halves(normed2_rows)), "mp", 1)
+    hidden_b, unit_grad_b, partial, branch_part = feed_forward(
+        normed2_rows, cotangent_rows, (gate_down, up_own, gate_down_other, up_other)
+    )
+    normed2_near = scatter_near(partial)
+
+    def weight_grad(rows, grads, width):
+        sent = dot_rows(rows, grads[:, width:]).astype(bf16)
+        kept = dot_rows(rows, grads[:, :width])
+        return (kept + swap(sent, "mp", 1).astype(f32)).astype(bf16)
 
     def to_blocks(grad_b, left_cols):
         right_part = dot_rows(left_cols, grad_b).astype(bf16)
@@ -515,28 +551,70 @@
             right_part.reshape(dp_count, rank_own, hidden_own),
         ]
 
-    down_grad_b = weight_grad(cotangent_front, cotangent_rear, hidden_front, hidden_rear)
-    gate_up_grad_b = weight_grad(normed2_front, normed2_rear, grads_front, grads_rear)
-    down_gate_sent = exchange(
-        jnp.concatenate(
-            to_blocks(down_grad_b, left_all[:, 2 * rank :])
-            + to_blocks(gate_up_grad_b[:, :hidden_own], left_all[:, :rank]),
-            axis=1,
-        )
-    )
-    up_grad_blocks = jnp.concatenate(
-        to_blocks(gate_up_grad_b[:, hidden_own:], left_all[:, rank : 2 * rank]), axis=1
-    )
-    normed2_grad = scatter_far(after(normed2_near, down_gate_sent))
-
-    hidden_late = after(jnp.zeros((1, hidden_own), bf16), *halves(normed2_near))
-    down_own = gate_down[:, hidden_own:]
-    mlp_branch = scatter_far(
-        scatter_near(
-            dot_cols(hidden_rear + hidden_late, down_own),
-            dot_cols(hidden_front + hidden_late, down_own),
-        )
-    )
+    down_grad_b = weight_grad(cotangent_rows, hidden_b, hidden_own)
+    gate_up_grad_b = weight_grad(normed2_rows, unit_grad_b, 2 * hidden_own)
+    down_sent = exchange(
+        jnp.concatenate(to_blocks(down_grad_b, after(left_all[:, 2 * rank :], attended_all)), axis=1)
+    )
+    gate_up_blocks = jnp.concatenate(
+        to_blocks(gate_up_grad_b[:, :hidden_own], left_all[:, :rank])
+        + to_blocks(gate_up_grad_b[:, hidden_own:], left_all[:, rank : 2 * rank]),
+        axis=1,
+    )
+    normed2_grad = scatter_far(after(normed2_near, down_sent, gate_up_blocks))
+    gate_up_sent = exchange(after(gate_up_blocks, normed2_grad))
+
+    unused_norm, mlp_pull = jax.vjp(rms_norm, middle, feedforward_norm_gain)
+    middle_norm_grad, mlp_gain_part = mlp_pull(normed2_grad)
+    middle_grad = cotangent_own.astype(f32) + middle_norm_grad
+    branch_grad_own = middle_grad.astype(bf16)
+    branch_grad = gather_mp(branch_grad_own).reshape(row_count, model_width)
+    attended_grad_b = (
+        dot(branch_grad, o_full).astype(bf16).reshape(row_count, head_count, HEAD_SIZE)
+    )
+    prob_grad = jnp.einsum("qhd,kd->hqk", attended_grad_b, all_values, preferred_element_type=f32)
+    score_grad_b = (
+        weights_soft * (prob_grad - jnp.sum(prob_grad * weights_soft, axis=-1, keepdims=True))
+    ).astype(bf16)
+    keys_grad = (
+        jnp.einsum("hqk,qhd->kd", score_grad_b, query_b, preferred_element_type=f32) * score_scale
+    )
+    values_grad = jnp.einsum(
+        "hqk,qhd->kd", weights_low, attended_grad_b, preferred_element_type=f32
+    )
+    pair_partial = jnp.concatenate([keys_grad, values_grad], axis=1)
+    half = pair_partial.shape[0] // 2
+    block_all = block_width + rank_own
+
+    down_weight_grad, down_lora_a, down_lora_b = receive_grad(
+        after(current_loop, attended_grad_b), down_sent, 0, block_all, down_update_right, block_width
+    )
+    pair_near = scatter_near(add_core(pair_partial[half:], pair_partial[:half]))
+    branch_near = scatter_near(after(branch_part, normed2_grad))
+    query_grad = (
+        jnp.einsum("hqk,kd->qhd", score_grad_b, all_keys, preferred_element_type=f32) * score_scale
+    )
+    query_grad_b = rotate(query_grad, positions, -1.0).reshape(row_count, query_cols).astype(bf16)
+    query_grad_all = lax.all_gather(query_grad_b, "dp", axis=0, tiled=True)
+    branch_cols = all_token_cols(branch_grad_own, gate_up_sent)
+    q_weight_grad = dot_rows(normed_cols, query_grad_all)
+    o_weight_grad = dot_rows(branch_cols, attended_all)
+    q_weight_b = q_weight_grad.astype(bf16)
+    o_weight_b = o_weight_grad.astype(bf16)
+    qo_lora_a = sum_mp(
+        jnp.concatenate([dot_cols(q_weight_b, q_right), dot_cols(o_weight_b, o_right)], axis=1)
+    )
+    qo_right = jnp.concatenate(
+        [dot_rows(q_left, q_weight_b), dot_rows(o_left, o_weight_b)], axis=1
+    ).astype(bf16)
+    pair_grad_own = scatter_far(
+        after(pair_near, gate_up_sent, qo_right, qo_lora_a, *halves(branch_near))
+    )
+    pair_grad_b = jnp.concatenate(
+        [rotate(pair_grad_own[:, :HEAD_SIZE], spots_own, -1.0), pair_grad_own[:, HEAD_SIZE:]],
+        axis=1,
+    ).astype(bf16)
+    mlp_branch = scatter_far(after(branch_near, *halves(pair_near)))
     output_rows = middle + mlp_branch
     mixed = gather_mp(output_rows.astype(bf16)).reshape(row_count, model_width)
     confidence_own = jnp.sum(jax.nn.sigmoid(jnp.dot(output_rows, probe, precision=precise)))
@@ -544,56 +622,17 @@
     exit_own = own_slice(token_exit_loop)
     depth_own = jnp.sum((exit_own[:, None] == levels[None, :]).astype(f32), axis=0)
 
-    unused_norm, mlp_pull = jax.vjp(rms_norm, middle, feedforward_norm_gain)
-    middle_norm_grad, mlp_gain_part = mlp_pull(normed2_grad)
-    middle_grad = cotangent_own.astype(f32) + middle_norm_grad
-    branch_grad_own = middle_grad.astype(bf16)
-    branch_grad = gather_mp(branch_grad_own).reshape(row_count, model_width)
-    up_sent = exchange(after(up_grad_blocks, normed2_grad))
-    attended_grad_b = (
-        dot(branch_grad, o_full).astype(bf16).reshape(row_count, head_count, HEAD_SIZE)
-    )
-    prob_grad = jnp.einsum("qhd,kd->hqk", attended_grad_b, all_values, preferred_element_type=f32)
-    score_grad_b = (
-        weights_soft * (prob_grad - jnp.sum(prob_grad * weights_soft, axis=-1, keepdims=True))
-    ).astype(bf16)
-    keys_grad = (
-        jnp.einsum("hqk,qhd->kd", score_grad_b, query_b, preferred_element_type=f32) * score_scale
-    )
-    values_grad = jnp.einsum(
-        "hqk,qhd->kd", weights_low, attended_grad_b, preferred_element_type=f32
-    )
-    pair_partial = jnp.concatenate([keys_grad, values_grad], axis=1)
-    half = pair_partial.shape[0] // 2
-    pair_partial = after(pair_partial, up_sent)
-    pair_near = scatter_near(pair_partial[half:], pair_partial[:half])
-    o_partial = dot_rows(branch_grad, attended_b).astype(bf16)
-    o_sent = exchange(after(o_partial.reshape(dp_count, block_width, query_cols), up_sent))
-    pair_grad_own = after(scatter_far(pair_near), o_sent)
-    pair_grad_b = jnp.concatenate(
-        [rotate(pair_grad_own[:, :HEAD_SIZE], spots_own, -1.0), pair_grad_own[:, HEAD_SIZE:]],
-        axis=1,
-    ).astype(bf16)
-    query_grad = (
-        jnp.einsum("hqk,kd->qhd", score_grad_b, all_keys, preferred_element_type=f32) * score_scale
-    )
-    query_grad_b = rotate(query_grad, positions, -1.0).reshape(row_count, query_cols).astype(bf16)
     normed_grad = scatter_mp(dot_cols(query_grad_b, q_full)) + dot_cols(pair_grad_b, kv_full)
     unused_first, attn_pull = jax.vjp(rms_norm, tokens_own, attention_norm_gain)
     inputs_norm_grad, attn_gain_part = attn_pull(normed_grad)
     tokens_grad = gather_mp(middle_grad + inputs_norm_grad).reshape(row_count, model_width)
 
-    query_grad_all = lax.all_gather(query_grad_b, "dp", axis=0, tiled=True)
     pair_grad_all = lax.all_gather(pair_grad_b, ("dp", "mp"), axis=0, tiled=True)
-    q_weight_grad = dot_rows(normed_cols, query_grad_all)
-    kv_weight_grad = dot_rows(normed_cols, after(pair_grad_all, mlp_branch))
-    o_weight_grad = jnp.sum(o_sent.astype(f32), axis=0)
-    q_weight_b = q_weight_grad.astype(bf16)
+    small = sum_all(
+        jnp.concatenate([attn_gain_part, mlp_gain_part, depth_own, confidence_own.reshape(1)])
+    )
+    kv_weight_grad = dot_rows(normed_cols, after(pair_grad_all, small, tokens_grad))
     kv_weight_b = kv_weight_grad.astype(bf16)
-    o_weight_b = o_weight_grad.astype(bf16)
-    qo_lora_a = sum_mp(
-        jnp.concatenate([dot_cols(q_weight_b, q_right), dot_cols(o_weight_b, o_right)], axis=1)
-    )
     kv_lora_a = jnp.concatenate(
         [
             dot_cols(kv_weight_b[:, :HEAD_SIZE], kv_right[:, :HEAD_SIZE]),
@@ -603,44 +642,25 @@
     )
     right_parts = jnp.concatenate(
         [
-            dot_rows(q_left, q_weight_b),
-            dot_rows(o_left, o_weight_b),
-            dot_rows(kv_left[:, :rank], kv_weight_b[:, :HEAD_SIZE]),
-            dot_rows(kv_left[:, rank:], kv_weight_b[:, HEAD_SIZE:]),
+            qo_right,
+            dot_rows(kv_left[:, :rank], kv_weight_b[:, :HEAD_SIZE]).astype(bf16),
+            dot_rows(kv_left[:, rank:], kv_weight_b[:, HEAD_SIZE:]).astype(bf16),
         ],
         axis=1,
-    ).astype(bf16)
+    )
     right_grads = jnp.sum(
         exchange(right_parts.reshape(dp_count, rank_own, -1)).astype(f32), axis=0
     )
 
-    block_all = block_width + rank_own
-
-    def side_by_side(arrived, first):
-        return jnp.concatenate(
-            [arrived[place, first : first + rank_own].astype(f32) for place in range(dp_count)],
-            axis=1,
-        )
-
-    down_arrived = down_gate_sent[:, :block_all]
-    gate_arrived = down_gate_sent[:, block_all:]
-    down_weight_grad, down_lora_a = receive_grad(
-        current_loop, down_arrived, down_update_right, block_width
-    )
-    gate_weight_grad, gate_lora_a = receive_grad(
-        current_loop, gate_arrived, gate_update_right, block_width
-    )
-    up_weight_grad, up_lora_a = receive_grad(
-        current_loop, up_sent, up_update_right, block_width
-    )
-    down_lora_b = side_by_side(down_arrived, block_width)
-    gate_lora_b = side_by_side(gate_arrived, block_width)
-    up_lora_b = side_by_side(up_sent, block_width)
+    late_loop = after(current_loop, pair_grad_own)
+    gate_weight_grad, gate_lora_a, gate_lora_b = receive_grad(
+        late_loop, gate_up_sent, 0, block_all, gate_update_right, block_width
+    )
+    up_weight_grad, up_lora_a, up_lora_b = receive_grad(
+        late_loop, gate_up_sent, 1, block_all, up_update_right, block_width
+    )
     mlp_lora_a = sum_mp(jnp.concatenate([gate_lora_a, up_lora_a, down_lora_a], axis=1))
 
-    small = sum_all(
-        jnp.concatenate([attn_gain_part, mlp_gain_part, depth_own, confidence_own.reshape(1)])
-    )
     gain_width = model_width // dp_count
     attn_gain_grad = lax.dynamic_slice_in_dim(small, dp_place * gain_width, gain_width, 0)
     mlp_gain_grad = lax.dynamic_slice_in_dim(
@@ -673,11 +693,11 @@
         place_loop(qo_lora_a[:, rank:]),
         place_loop(right_grads[:, query_cols : 2 * query_cols]),
         place_loop(mlp_lora_a[:, :rank]),
-        place_loop(gate_lora_b),
+        gate_lora_b,
         place_loop(mlp_lora_a[:, rank : 2 * rank]),
-        place_loop(up_lora_b),
+        up_lora_b,
         place_loop(mlp_lora_a[:, 2 * rank :]),
-        place_loop(down_lora_b),
+        down_lora_b,
     )
 
 

time: 910 us -> 881 us (0.968)
  matrix products: 96.7 us -> 82.6 us
  other arithmetic: 91.1 us -> 79.6 us
  starting transfers between devices: 93.9 us -> 104 us
    all_to_all x7, waiting for transfers between devices: 39.8 us -> 98.4 us  [exchange(): return lax.all_to_all(blocks, 'dp', 0, 0, tiled=True)]
    ppermute x63 -> x65, waiting for transfers between devices: 322 us -> 287 us  [swap(): lax.ppermute(value, axis, [(place, place ^ bit) for place in range(count)])]
    all_gather x1, waiting for transfers between devices: 30 us -> 0.01 us  [body(): query_grad_all = lax.all_gather(query_grad_b, 'dp', axis=0, tiled=True)]
    dot_general x9 -> x7, matrix products: 24.8 us -> 9.33 us  [dot_cols(): lax.dot_general(left, right, (((1,), (1,)), ((), ())), preferred_element_...]
    ppermute x63 -> x65, starting transfers between devices: 56.9 us -> 69.6 us  [swap(): lax.ppermute(value, axis, [(place, place ^ bit) for place in range(count)])]
    slice x15 -> x23, local copies, waits for them, and re-layouts: 12.9 us -> 20.2 us  [after(): last = other[tuple((size - 1 for size in other.shape))]]
    unnamed x298 -> x285, local copies, waits for them, and re-layouts: 51.2 us -> 45.9 us
    pallas_call x2 -> x1, Pallas kernels: 34 us -> 34.4 us  [feed_forward(): pl.pallas_call(feed_kernel, out_shape=(jax.ShapeDtypeStruct((rows, pairs...]
  transfers between devices with their start and end apart: 75 -> 78, of which waited for: 43 -> 43; matrix products, arithmetic and copies ran while one was open for 31% -> 26% of each run, Pallas kernels for 7% -> 7%
where the time goes in v3:
time: 881 us; the launch traced here: 873 us
  waiting for transfers between devices  399 us (45%)
  local copies, waits for them, and re-layouts  108 us (12%)
  starting transfers between devices  104 us (12%)
  matrix products  82.6 us (9%)
  other arithmetic  79.6 us (9%)
  Pallas kernels  65.1 us (7%)
  between operations  35.4 us (4%)
    ppermute x65, waiting for transfers between devices, swap(): lax.ppermute(value, axis, [(place, place ^ bit) for place in range(count)])  287 us
    all_to_all x7, waiting for transfers between devices, exchange(): return lax.all_to_all(blocks, 'dp', 0, 0, tiled=True)  98.4 us
    ppermute x65, starting transfers between devices, swap(): lax.ppermute(value, axis, [(place, place ^ bit) for place in range(count)])  69.6 us
    unnamed x285, local copies, waits for them, and re-layouts  45.9 us
    dot_general x14, matrix products, dot_rows(): lax.dot_general(left, right, (((0,), (0,)), ((), ())), preferred_element_...  42.9 us
    pallas_call x1, Pallas kernels, feed_forward(): pl.pallas_call(feed_kernel, out_shape=(jax.ShapeDtypeStruct((rows, pairs...  34.4 us
    all_to_all x7, starting transfers between devices, exchange(): return lax.all_to_all(blocks, 'dp', 0, 0, tiled=True)  33.8 us
    slice x23, local copies, waits for them, and re-layouts, after(): last = other[tuple((size - 1 for size in other.shape))]  20.2 us
  transfers between devices with their start and end apart: 78, of which 43 were waited for; matrix products, arithmetic and copies ran while one was open for 26% of the time, Pallas kernels for 7%

profile of v3, /device:TPU:0, one launch (start us, length us, event | category | flops | bytes accessed | tf_op | source)
XLA Modules:
  0.0 873.4 jit_solution(533252510734715402)
XLA Ops:
  13.7 4.0 collective-permute-start.2
  21.4 8.9 %collective-permute-done.2 = bf16[64,2048]{1,0:T(8,128)(2,1)S(1)} collective-permute-done((bf16[64,2048]{1,0:T(8,128)(2,1)S(1)}, bf16[64,2048]{1,0:T(8,128)(2,1)S(1)}, u32[]{:S(2)}, u32[]{:S(2)}) %collective-permute-start.2) | collective-permute-done | bytes 262176 | tf_op jit(solution)/shard_map/ppermute | solution.py:91
  34.2 11.1 %collective-permute-done.5 = bf16[128,2048]{1,0:T(8,128)(2,1)} collective-permute-done((bf16[128,2048]{1,0:T(8,128)(2,1)}, bf16[128,2048]{1,0:T(8,128)(2,1)}, u32[]{:S(2)}, u32[]{:S(2)}) %collective-permute-start.5) | collective-permute-done | bytes 524320 | tf_op jit(solution)/shard_map/ppermute | solution.py:91
  49.6 10.7 %collective-permute-done.6 = bf16[128,2048]{1,0:T(8,128)(2,1)S(1)} collective-permute-done((bf16[128,2048]{1,0:T(8,128)(2,1)}, bf16[128,2048]{1,0:T(8,128)(2,1)S(1)}, u32[]{:S(2)}, u32[]{:S(2)}) %collective-permute-start.6) | collective-permute-done | bytes 524320 | tf_op jit(solution)/shard_map/ppermute | solution.py:91
  63.6 13.2 %all-gather.7.cloned.1.call-done = bf16[2048,512]{1,0:T(8,128)(2,1)} async-done(((bf16[64,512]{1,0:T(8,128)(2,1)}), bf16[2048,512]{1,0:T(8,128)(2,1)}) %all-gather.7.cloned.1.call-update) | async-done | bytes 2097168 | tf_op jit(solution)/shard_map/all_gather | solution.py:445
  80.2 6.0 collective-permute-done
  90.3 10.3 %collective-permute-done.1 = bf16[144,512]{1,0:T(8,128)(2,1)S(1)} collective-permute-done((bf16[144,512]{1,0:T(8,128)(2,1)S(1)}, bf16[144,512]{1,0:T(8,128)(2,1)S(1)}, u32[]{:S(2)}, u32[]{:S(2)}) %collective-permute-start.1) | collective-permute-done | bytes 147488 | tf_op jit(solution)/shard_map/ppermute | solution.py:91
  111.9 3.7 collective-permute-done.9
  120.2 3.4 all-to-all-start
  128.5 11.7 %collective-permute-done.11 = bf16[288,512]{1,0:T(8,128)(2,1)S(1)} collective-permute-done((bf16[288,512]{1,0:T(8,128)(2,1)S(1)}, bf16[288,512]{1,0:T(8,128)(2,1)S(1)}, u32[]{:S(2)}, u32[]{:S(2)}) %collective-permute-start.11) | collective-permute-done | bytes 294944 | tf_op jit(solution)/shard_map/ppermute | solution.py:91
  144.2 7.6 shard_map.442
  151.7 4.9 all-to-all-start.1
  163.3 7.0 collective-permute-done.13
  182.2 3.1 fusion.27
  187.0 4.5 fusion.173
  191.6 3.3 convolution_convert_fusion.7
  204.2 6.7 collective-permute-done.16
  213.7 38.4 %all-to-all-done.1 = bf16[8,256,1024]{2,1,0:T(8,128)(2,1)} async-done(((bf16[8,256,1024]{2,1,0:T(8,128)(2,1)}), bf16[8,256,1024]{2,1,0:T(8,128)(2,1)}, u32[]{:S(2)}, u32[]{:S(2)}) %all-to-all-start.1) | async-done | bytes 4194336 | tf_op jit(solution)/shard_map/all_to_all | solution.py:95
  255.9 12.5 %collective-permute-done.17 = bf16[64,2048]{1,0:T(8,128)(2,1)S(1)} collective-permute-done((bf16[64,2048]{1,0:T(8,128)(2,1)S(1)}, bf16[64,2048]{1,0:T(8,128)(2,1)S(1)}, u32[]{:S(2)}, u32[]{:S(2)}) %collective-permute-start.17) | collective-permute-done | bytes 262176 | tf_op jit(solution)/shard_map/ppermute | solution.py:91
  271.7 16.2 %collective-permute-done.20 = bf16[128,2048]{1,0:T(8,128)(2,1)} collective-permute-done((bf16[128,2048]{1,0:T(8,128)(2,1)}, bf16[128,2048]{1,0:T(8,128)(2,1)}, u32[]{:S(2)}, u32[]{:S(2)}) %collective-permute-start.20) | collective-permute-done | bytes 524320 | tf_op jit(solution)/shard_map/ppermute | solution.py:91
  289.9 6.5 shard_map.443
  296.3 3.6 all-to-all-start.2
  303.7 38.8 %collective-permute-done.18 = bf16[128,2048]{1,0:T(8,128)(2,1)S(1)} collective-permute-done((bf16[128,2048]{1,0:T(8,128)(2,1)}, bf16[128,2048]{1,0:T(8,128)(2,1)S(1)}, u32[]{:S(2)}, u32[]{:S(2)}) %collective-permute-start.18) | collective-permute-done | bytes 524320 | tf_op jit(solution)/shard_map/ppermute | solution.py:91
  354.6 12.8 %collective-permute-done.19 = bf16[256,2048]{1,0:T(8,128)(2,1)} collective-permute-done((bf16[256,2048]{1,0:T(8,128)(2,1)}, bf16[256,2048]{1,0:T(8,128)(2,1)}, u32[]{:S(2)}, u32[]{:S(2)}) %collective-permute-start.19) | collective-permute-done | bytes 1048608 | tf_op jit(solution)/shard_map/ppermute | solution.py:91
  369.3 4.1 collective-permute-done.22
  387.8 34.4 %shard_map.444 = (bf16[1024,1024]{1,0:T(8,128)(2,1)}, bf16[1024,2048]{1,0:T(8,128)(2,1)}, f32[1024,2048]{1,0:T(8,128)}, bf16[1024,2048]{1,0:T(8,128)(2,1)}) custom-call(bf16[1024,2048]{1,0:T(8,128)(2,1)} %copy-done.21, bf16[1024,2048]{1,0:T(8,128)(2,1)} %constant_dynamic-update-slice_fusion.28.cotangent_ref, bf16[2048,1024]{1,0:T(8,128)(2,1)} %bitcast.46.refs_0_, ...), custom_call_target="tpu_custom_call" | custom-call | tf_op jit(solution)/shard_map/pallas_call | solution.py:351
  422.3 4.9 convolution_convert_fusion.1
  429.5 9.5 %convolution_convert_fusion = bf16[2048,1024]{1,0:T(8,128)(2,1)} fusion(bf16[1024,2048]{1,0:T(8,128)(2,1)} %copy-done.21, bf16[1024,2048]{1,0:T(8,128)(2,1)} %get-tuple-element.39), kind=kOutput, calls=%fused_computation.13 | convolution fusion | flops 4297064448 | bytes 10485760 | tf_op jit(solution)/shard_map/dot_general | solution.py:82
  444.4 5.3 add_convert_fusion.1
  453.3 9.7 %all-to-all-start.3 = ((bf16[8,288,512]{2,1,0:T(8,128)(2,1)}), bf16[8,288,512]{2,1,0:T(8,128)(2,1)S(1)}, u32[]{:S(2)}, u32[]{:S(2)}) async-start(bf16[8,288,512]{2,1,0:T(8,128)(2,1)} %pad_maximum_fusion), calls=%async_computation.3 | async-start | bytes 4718592 | tf_op jit(solution)/shard_map/all_to_all | solution.py:95
  463.1 3.9 collective-permute-done.25
  467.0 13.7 %collective-permute-done.27 = bf16[256,2048]{1,0:T(8,128)(2,1)} collective-permute-done((bf16[256,2048]{1,0:T(8,128)(2,1)}, bf16[256,2048]{1,0:T(8,128)(2,1)}, u32[]{:S(2)}, u32[]{:S(2)}) %collective-permute-start.27) | collective-permute-done | bytes 1048608 | tf_op jit(solution)/shard_map/ppermute | solution.py:91
  480.8 3.6 convert_add_fusion.1
  492.0 12.5 %collective-permute-done.26 = bf16[128,2048]{1,0:T(8,128)(2,1)S(1)} collective-permute-done((bf16[128,2048]{1,0:T(8,128)(2,1)S(1)}, bf16[128,2048]{1,0:T(8,128)(2,1)S(1)}, u32[]{:S(2)}, u32[]{:S(2)}) %collective-permute-start.26) | collective-permute-done | bytes 524320 | tf_op jit(solution)/shard_map/ppermute | solution.py:91
  506.8 6.6 add_convert_fusion
  520.7 9.1 %collective-permute-start.31 = (bf16[128,2048]{1,0:T(8,128)(2,1)S(1)}, bf16[128,2048]{1,0:T(8,128)(2,1)S(1)}, u32[]{:S(2)}, u32[]{:S(2)}) collective-permute-start(bf16[128,2048]{1,0:T(8,128)(2,1)S(1)} %slice.813), channel_id=1, source_target_pairs={{0,2},{1,3},{2,0},{3,1},{4,6},{5,7},{6,4},{7,5},{8,10},{9,11},{10,... | collective-permute-start | bytes 1572872 | tf_op jit(solution)/shard_map/ppermute | solution.py:91
  530.1 6.8 collective-permute-done.31
  537.1 3.7 collective-permute-start.32
  542.9 7.9 collective-permute-done.32
  552.5 4.6 collective-permute-start.33
  557.8 4.1 fusion.159
  566.5 4.6 all-to-all-start.4
  580.1 5.2 convolution_bitcast_fusion
  585.3 3.4 fusion.1
  602.6 5.2 shard_map.447
  607.8 9.3 %collective-permute-done.48 = bf16[256,2048]{1,0:T(8,128)(2,1)} collective-permute-done((bf16[256,2048]{1,0:T(8,128)(2,1)}, bf16[256,2048]{1,0:T(8,128)(2,1)}, u32[]{:S(2)}, u32[]{:S(2)}) %collective-permute-start.48) | collective-permute-done | bytes 1048608 | tf_op jit(solution)/shard_map/ppermute | solution.py:91
  626.6 5.2 collective-permute-done.49
  634.7 23.5 %collective-permute-done.40 = bf16[256,512]{1,0:T(8,128)(2,1)S(1)} collective-permute-done((bf16[256,512]{1,0:T(8,128)(2,1)S(1)}, bf16[256,512]{1,0:T(8,128)(2,1)S(1)}, u32[]{:S(2)}, u32[]{:S(2)}) %collective-permute-start.40) | collective-permute-done | bytes 262176 | tf_op jit(solution)/shard_map/ppermute | solution.py:91
  660.6 40.1 %all-to-all-done.4.arrived_ref = bf16[8,576,512]{2,1,0:T(8,128)(2,1)} async-done(((bf16[8,576,512]{2,1,0:T(8,128)(2,1)}), bf16[8,576,512]{2,1,0:T(8,128)(2,1)}, u32[]{:S(2)}, u32[]{:S(2)}) %all-to-all-start.4) | async-done | bytes 4718624 | tf_op jit(solution)/shard_map/all_to_all | solution.py:95
  703.3 3.5 all-to-all-start.5
  711.2 4.7 all-to-all-done.5
  739.6 6.4 collective-permute-done.52
  760.0 4.0 collective-permute-done.50
  765.8 4.5 collective-permute-done.51
  778.2 4.1 fusion.53
  791.5 5.8 shard_map.445
  798.9 5.8 shard_map.446
  804.8 3.7 collective-permute-done.57
  810.0 3.3 collective-permute-done.58
  816.3 3.7 collective-permute-done.59
  824.0 8.1 collective-permute-done.64
  835.3 3.2 fusion.174
  840.5 4.1 all-to-all-start.6
  848.8 15.3 %all-to-all-done.6 = bf16[8,32,1536]{2,1,0:T(8,128)(2,1)S(1)} async-done(((bf16[8,32,1536]{2,1,0:T(8,128)(2,1)}), bf16[8,32,1536]{2,1,0:T(8,128)(2,1)S(1)}, u32[]{:S(2)}, u32[]{:S(2)}) %all-to-all-start.6) | async-done | bytes 786464 | tf_op jit(solution)/shard_map/all_to_all | solution.py:95
  (615 shorter events, 268.2 us)
Async XLA Ops:
  7.2 69.6 %all-gather.7.cloned.1.call-start = ((), (), s32[]{:S(2)}) async-start(), calls=%async_computation.7 | async-start | bytes 2162688 | tf_op jit(solution)/shard_map/all_gather | solution.py:445
  11.9 170.3 %all-gather.9.cloned.1.call-start = ((), (), s32[]{:S(2)}) async-start(), calls=%async_computation.8 | async-start | bytes 4718592 | tf_op jit(solution)/shard_map/all_gather | solution.py:451
  13.7 16.6 %collective-permute-start.2 = (bf16[64,2048]{1,0:T(8,128)(2,1)S(1)}, bf16[64,2048]{1,0:T(8,128)(2,1)S(1)}, u32[]{:S(2)}, u32[]{:S(2)}) collective-permute-start(bf16[64,2048]{1,0:T(8,128)(2,1)S(1)} %get-tuple-element.62), channel_id=1, source_target_pairs={{0,4},{1,5},{2,6},{3,7},{4,0},{5,1},{6,2},{7,3},{8,12},{9,13},{10,... | collective-permute-start | bytes 786440 | tf_op jit(solution)/shard_map/ppermute | solution.py:91
  31.2 14.1 %collective-permute-start.5 = (bf16[128,2048]{1,0:T(8,128)(2,1)}, bf16[128,2048]{1,0:T(8,128)(2,1)}, u32[]{:S(2)}, u32[]{:S(2)}) collective-permute-start(bf16[128,2048]{1,0:T(8,128)(2,1)} %pad_maximum_fusion.7), channel_id=1, source_target_pairs={{0,2},{1,3},{2,0},{3,1},{4,6},{5,7},{6,4},{7,5},{8,10},{9,11},{10,... | collective-permute-start | bytes 1572872 | tf_op jit(solution)/shard_map/ppermute | solution.py:91
  32.6 14.5 %collective-permute-start.3 = (bf16[128,2048]{1,0:T(8,128)(2,1)}, bf16[128,2048]{1,0:T(8,128)(2,1)S(1)}, u32[]{:S(2)}, u32[]{:S(2)}) collective-permute-start(bf16[128,2048]{1,0:T(8,128)(2,1)} %pad_maximum_fusion.7), channel_id=1, source_target_pairs={{0,1},{1,0},{2,3},{3,2},{4,5},{5,4},{6,7},{7,6},{8,9},{9,8},{10,11... | collective-permute-start | bytes 1572872 | tf_op jit(solution)/shard_map/ppermute | solution.py:91
  45.3 15.1 %collective-permute-start.6 = (bf16[128,2048]{1,0:T(8,128)(2,1)}, bf16[128,2048]{1,0:T(8,128)(2,1)S(1)}, u32[]{:S(2)}, u32[]{:S(2)}) collective-permute-start(bf16[128,2048]{1,0:T(8,128)(2,1)} %collective-permute-done.5), channel_id=1, source_target_pairs={{0,16},{8,24},{16,0},{24,8},{1,17},{9,25},{17,1},{25,9},{2,18},{10... | collective-permute-start | bytes 1572872 | tf_op jit(solution)/shard_map/ppermute | solution.py:91
  48.2 38.2 %collective-permute-start.4 = (bf16[256,2048]{1,0:T(8,128)(2,1)}, bf16[256,2048]{1,0:T(8,128)(2,1)}, u32[]{:S(2)}, u32[]{:S(2)}) collective-permute-start(bf16[256,2048]{1,0:T(8,128)(2,1)} %pad_maximum_fusion.2), channel_id=1, source_target_pairs={{0,16},{8,24},{16,0},{24,8},{1,17},{9,25},{17,1},{25,9},{2,18},{10... | collective-permute-start | bytes 3145736 | tf_op jit(solution)/shard_map/ppermute | solution.py:91
  62.6 25.7 %collective-permute-start.7 = (bf16[256,2048]{1,0:T(8,128)(2,1)}, bf16[256,2048]{1,0:T(8,128)(2,1)}, u32[]{:S(2)}, u32[]{:S(2)}) collective-permute-start(bf16[256,2048]{1,0:T(8,128)(2,1)} %pad_maximum_fusion.3), channel_id=1, source_target_pairs={{0,1},{1,0},{2,3},{3,2},{4,5},{5,4},{6,7},{7,6},{8,9},{9,8},{10,11... | collective-permute-start | bytes 3145736 | tf_op jit(solution)/shard_map/ppermute | solution.py:91
  86.2 14.3 %collective-permute-start.1 = (bf16[144,512]{1,0:T(8,128)(2,1)S(1)}, bf16[144,512]{1,0:T(8,128)(2,1)S(1)}, u32[]{:S(2)}, u32[]{:S(2)}) collective-permute-start(bf16[144,512]{1,0:T(8,128)(2,1)S(1)} %pad_maximum_fusion.14), channel_id=1, source_target_pairs={{0,2},{1,3},{2,0},{3,1},{4,6},{5,7},{6,4},{7,5},{8,10},{9,11},{10,... | collective-permute-start | bytes 442376 | tf_op jit(solution)/shard_map/ppermute | solution.py:91
  108.4 7.2 collective-permute-start.9
  120.2 31.6 %all-to-all-start = ((bf16[8,64,256]{2,1,0:T(8,128)(2,1)}), bf16[8,64,256]{2,1,0:T(8,128)(2,1)S(1)}, u32[]{:S(2)}, u32[]{:S(2)}) async-start(bf16[8,64,256]{2,1,0:T(8,128)(2,1)} %constant_dynamic-update-slice_fusion.13), calls=%async_computation | async-start | bytes 524288 | tf_op jit(solution)/shard_map/all_to_all | solution.py:95
  125.3 15.0 %collective-permute-start.11 = (bf16[288,512]{1,0:T(8,128)(2,1)S(1)}, bf16[288,512]{1,0:T(8,128)(2,1)S(1)}, u32[]{:S(2)}, u32[]{:S(2)}) collective-permute-start(bf16[288,512]{1,0:T(8,128)(2,1)S(1)} %pad_maximum_fusion.13), channel_id=1, source_target_pairs={{0,1},{1,0},{2,3},{3,2},{4,5},{5,4},{6,7},{7,6},{8,9},{9,8},{10,11... | collective-permute-start | bytes 884744 | tf_op jit(solution)/shard_map/ppermute | solution.py:91
  151.7 100.3 %all-to-all-start.1 = ((bf16[8,256,1024]{2,1,0:T(8,128)(2,1)}), bf16[8,256,1024]{2,1,0:T(8,128)(2,1)}, u32[]{:S(2)}, u32[]{:S(2)}) async-start(bf16[8,256,1024]{2,1,0:T(8,128)(2,1)} %shard_map.442), calls=%async_computation.1 | async-start | bytes 8388608 | tf_op jit(solution)/shard_map/all_to_all | solution.py:95
  156.6 270.9 %all-gather.13.cloned.1.call-start = ((), (), s32[]{:S(2)}) async-start(), calls=%async_computation.10 | async-start | bytes 2359296 | tf_op jit(solution)/shard_map/all_gather | solution.py:530
  161.4 13.6 %collective-permute-start.12 = (bf16[1152,512]{1,0:T(8,128)(2,1)}, bf16[1152,512]{1,0:T(8,128)(2,1)S(1)}, u32[]{:S(2)}, u32[]{:S(2)}) collective-permute-start(bf16[1152,512]{1,0:T(8,128)(2,1)} %get-tuple-element.99), channel_id=1, source_target_pairs={{0,8},{8,0},{16,24},{24,16},{1,9},{9,1},{17,25},{25,17},{2,10},{10... | collective-permute-start | bytes 3538952 | tf_op jit(solution)/shard_map/ppermute | solution.py:91
  161.4 8.8 %collective-permute-start.13 = (bf16[512,256]{1,0:T(8,128)(2,1)S(1)}, bf16[512,256]{1,0:T(8,128)(2,1)S(1)}, u32[]{:S(2)}, u32[]{:S(2)}) collective-permute-start(bf16[512,256]{1,0:T(8,128)(2,1)S(1)} %bitcast.327), channel_id=1, source_target_pairs={{0,16},{8,24},{16,0},{24,8},{1,17},{9,25},{17,1},{25,9},{2,18},{10... | collective-permute-start | bytes 786440 | tf_op jit(solution)/shard_map/ppermute | solution.py:91
  202.4 8.5 collective-permute-start.16
  255.9 12.5 %collective-permute-start.17 = (bf16[64,2048]{1,0:T(8,128)(2,1)S(1)}, bf16[64,2048]{1,0:T(8,128)(2,1)S(1)}, u32[]{:S(2)}, u32[]{:S(2)}) collective-permute-start(bf16[64,2048]{1,0:T(8,128)(2,1)S(1)} %get-tuple-element.64), channel_id=1, source_target_pairs={{0,4},{1,5},{2,6},{3,7},{4,0},{5,1},{6,2},{7,3},{8,12},{9,13},{10,... | collective-permute-start | bytes 786440 | tf_op jit(solution)/shard_map/ppermute | solution.py:91
  269.9 18.0 %collective-permute-start.20 = (bf16[128,2048]{1,0:T(8,128)(2,1)}, bf16[128,2048]{1,0:T(8,128)(2,1)}, u32[]{:S(2)}, u32[]{:S(2)}) collective-permute-start(bf16[128,2048]{1,0:T(8,128)(2,1)} %pad_maximum_fusion.9), channel_id=1, source_target_pairs={{0,2},{1,3},{2,0},{3,1},{4,6},{5,7},{6,4},{7,5},{8,10},{9,11},{10,... | collective-permute-start | bytes 1572872 | tf_op jit(solution)/shard_map/ppermute | solution.py:91
  296.3 79.0 %all-to-all-start.2 = ((bf16[8,256,512]{2,1,0:T(8,128)(2,1)}), bf16[8,256,512]{2,1,0:T(8,128)(2,1)S(1)}, u32[]{:S(2)}, u32[]{:S(2)}) async-start(bf16[8,256,512]{2,1,0:T(8,128)(2,1)} %shard_map.443), calls=%async_computation.2 | async-start | bytes 4194304 | tf_op jit(solution)/shard_map/all_to_all | solution.py:95
  299.9 149.8 %all-gather.11.cloned.1.call-start = ((), (), s32[]{:S(2)}) async-start(), calls=%async_computation.9 | async-start | bytes 3244032 | tf_op jit(solution)/shard_map/all_gather | solution.py:532
  300.2 42.2 %collective-permute-start.18 = (bf16[128,2048]{1,0:T(8,128)(2,1)}, bf16[128,2048]{1,0:T(8,128)(2,1)S(1)}, u32[]{:S(2)}, u32[]{:S(2)}) collective-permute-start(bf16[128,2048]{1,0:T(8,128)(2,1)} %pad_maximum_fusion.9), channel_id=1, source_target_pairs={{0,1},{1,0},{2,3},{3,2},{4,5},{5,4},{6,7},{7,6},{8,9},{9,8},{10,11... | collective-permute-start | bytes 1572872 | tf_op jit(solution)/shard_map/ppermute | solution.py:91
  302.1 44.6 %collective-permute-start.21 = (bf16[128,2048]{1,0:T(8,128)(2,1)}, bf16[128,2048]{1,0:T(8,128)(2,1)S(1)}, u32[]{:S(2)}, u32[]{:S(2)}) collective-permute-start(bf16[128,2048]{1,0:T(8,128)(2,1)} %collective-permute-done.20), channel_id=1, source_target_pairs={{0,16},{8,24},{16,0},{24,8},{1,17},{9,25},{17,1},{25,9},{2,18},{10... | collective-permute-start | bytes 1572872 | tf_op jit(solution)/shard_map/ppermute | solution.py:91
  303.6 82.2 %collective-permute-start.23 = (bf16[2048,1024]{1,0:T(8,128)(2,1)}, bf16[2048,1024]{1,0:T(8,128)(2,1)}, u32[]{:S(2)}, u32[]{:S(2)}) collective-permute-start(bf16[2048,1024]{1,0:T(8,128)(2,1)} %bitcast.46.refs_0_), channel_id=1, source_target_pairs={{0,8},{8,0},{16,24},{24,16},{1,9},{9,1},{17,25},{25,17},{2,10},{10... | collective-permute-start | bytes 12582920 | tf_op jit(solution)/shard_map/ppermute | solution.py:91
  345.2 22.1 %collective-permute-start.19 = (bf16[256,2048]{1,0:T(8,128)(2,1)}, bf16[256,2048]{1,0:T(8,128)(2,1)}, u32[]{:S(2)}, u32[]{:S(2)}) collective-permute-start(bf16[256,2048]{1,0:T(8,128)(2,1)} %pad_maximum_fusion.4), channel_id=1, source_target_pairs={{0,16},{8,24},{16,0},{24,8},{1,17},{9,25},{17,1},{25,9},{2,18},{10... | collective-permute-start | bytes 3145736 | tf_op jit(solution)/shard_map/ppermute | solution.py:91
  349.0 24.4 %collective-permute-start.22 = (bf16[256,2048]{1,0:T(8,128)(2,1)}, bf16[256,2048]{1,0:T(8,128)(2,1)}, u32[]{:S(2)}, u32[]{:S(2)}) collective-permute-start(bf16[256,2048]{1,0:T(8,128)(2,1)} %pad_maximum_fusion.5), channel_id=1, source_target_pairs={{0,1},{1,0},{2,3},{3,2},{4,5},{5,4},{6,7},{7,6},{8,9},{9,8},{10,11... | collective-permute-start | bytes 3145736 | tf_op jit(solution)/shard_map/ppermute | solution.py:91
  376.6 9.2 %collective-permute-start.24 = (bf16[2048,512]{1,0:T(8,128)(2,1)S(1)}, bf16[2048,512]{1,0:T(8,128)(2,1)}, u32[]{:S(2)}, u32[]{:S(2)}) collective-permute-start(bf16[2048,512]{1,0:T(8,128)(2,1)S(1)} %broadcast_add_fusion.1), channel_id=1, source_target_pairs={{0,8},{8,0},{16,24},{24,16},{1,9},{9,1},{17,25},{25,17},{2,10},{10... | collective-permute-start | bytes 6291464 | tf_op jit(solution)/shard_map/ppermute | solution.py:91
  427.1 17.3 %collective-permute-start.29 = (bf16[2048,512]{1,0:T(8,128)(2,1)S(1)}, bf16[2048,512]{1,0:T(8,128)(2,1)}, u32[]{:S(2)}, u32[]{:S(2)}) collective-permute-start(bf16[2048,512]{1,0:T(8,128)(2,1)S(1)} %convolution_convert_fusion.1), channel_id=1, source_target_pairs={{0,8},{8,0},{16,24},{24,16},{1,9},{9,1},{17,25},{25,17},{2,10},{10... | collective-permute-start | bytes 6291464 | tf_op jit(solution)/shard_map/ppermute | solution.py:91
  439.0 67.7 %collective-permute-start.30 = (bf16[2048,1024]{1,0:T(8,128)(2,1)}, bf16[2048,1024]{1,0:T(8,128)(2,1)}, u32[]{:S(2)}, u32[]{:S(2)}) collective-permute-start(bf16[2048,1024]{1,0:T(8,128)(2,1)} %convolution_convert_fusion), channel_id=1, source_target_pairs={{0,8},{8,0},{16,24},{24,16},{1,9},{9,1},{17,25},{25,17},{2,10},{10... | collective-permute-start | bytes 12582920 | tf_op jit(solution)/shard_map/ppermute | solution.py:91
  441.3 25.7 %collective-permute-start.25 = (bf16[256,2048]{1,0:T(8,128)(2,1)}, bf16[256,2048]{1,0:T(8,128)(2,1)}, u32[]{:S(2)}, u32[]{:S(2)}) collective-permute-start(bf16[256,2048]{1,0:T(8,128)(2,1)} %get-tuple-element.77), channel_id=1, source_target_pairs={{0,16},{8,24},{16,0},{24,8},{1,17},{9,25},{17,1},{25,9},{2,18},{10... | collective-permute-start | bytes 3145736 | tf_op jit(solution)/shard_map/ppermute | solution.py:91
  441.9 38.9 %collective-permute-start.27 = (bf16[256,2048]{1,0:T(8,128)(2,1)}, bf16[256,2048]{1,0:T(8,128)(2,1)}, u32[]{:S(2)}, u32[]{:S(2)}) collective-permute-start(bf16[256,2048]{1,0:T(8,128)(2,1)} %get-tuple-element.78), channel_id=1, source_target_pairs={{0,1},{1,0},{2,3},{3,2},{4,5},{5,4},{6,7},{7,6},{8,9},{9,8},{10,11... | collective-permute-start | bytes 3145736 | tf_op jit(solution)/shard_map/ppermute | solution.py:91
  453.3 64.2 %all-to-all-start.3 = ((bf16[8,288,512]{2,1,0:T(8,128)(2,1)}), bf16[8,288,512]{2,1,0:T(8,128)(2,1)S(1)}, u32[]{:S(2)}, u32[]{:S(2)}) async-start(bf16[8,288,512]{2,1,0:T(8,128)(2,1)} %pad_maximum_fusion), calls=%async_computation.3 | async-start | bytes 4718592 | tf_op jit(solution)/shard_map/all_to_all | solution.py:95
  484.4 20.1 %collective-permute-start.26 = (bf16[128,2048]{1,0:T(8,128)(2,1)S(1)}, bf16[128,2048]{1,0:T(8,128)(2,1)S(1)}, u32[]{:S(2)}, u32[]{:S(2)}) collective-permute-start(bf16[128,2048]{1,0:T(8,128)(2,1)S(1)} %slice.815), channel_id=1, source_target_pairs={{0,1},{1,0},{2,3},{3,2},{4,5},{5,4},{6,7},{7,6},{8,9},{9,8},{10,11... | collective-permute-start | bytes 1572872 | tf_op jit(solution)/shard_map/ppermute | solution.py:91
  490.1 15.5 %collective-permute-start.28 = (bf16[128,2048]{1,0:T(8,128)(2,1)S(1)}, bf16[128,2048]{1,0:T(8,128)(2,1)S(1)}, u32[]{:S(2)}, u32[]{:S(2)}) collective-permute-start(bf16[128,2048]{1,0:T(8,128)(2,1)S(1)} %slice.814), channel_id=1, source_target_pairs={{0,16},{8,24},{16,0},{24,8},{1,17},{9,25},{17,1},{25,9},{2,18},{10... | collective-permute-start | bytes 1572872 | tf_op jit(solution)/shard_map/ppermute | solution.py:91
  520.7 16.3 %collective-permute-start.31 = (bf16[128,2048]{1,0:T(8,128)(2,1)S(1)}, bf16[128,2048]{1,0:T(8,128)(2,1)S(1)}, u32[]{:S(2)}, u32[]{:S(2)}) collective-permute-start(bf16[128,2048]{1,0:T(8,128)(2,1)S(1)} %slice.813), channel_id=1, source_target_pairs={{0,2},{1,3},{2,0},{3,1},{4,6},{5,7},{6,4},{7,5},{8,10},{9,11},{10,... | collective-permute-start | bytes 1572872 | tf_op jit(solution)/shard_map/ppermute | solution.py:91
  537.1 13.7 %collective-permute-start.32 = (bf16[64,2048]{1,0:T(8,128)(2,1)S(1)}, bf16[64,2048]{1,0:T(8,128)(2,1)S(1)}, u32[]{:S(2)}, u32[]{:S(2)}) collective-permute-start(bf16[64,2048]{1,0:T(8,128)(2,1)S(1)} %slice.817), channel_id=1, source_target_pairs={{0,4},{1,5},{2,6},{3,7},{4,0},{5,1},{6,2},{7,3},{8,12},{9,13},{10,... | collective-permute-start | bytes 786440 | tf_op jit(solution)/shard_map/ppermute | solution.py:91
  552.5 18.9 %collective-permute-start.33 = (bf16[64,2048]{1,0:T(8,128)(2,1)S(1)}, bf16[64,2048]{1,0:T(8,128)(2,1)}, u32[]{:S(2)}, u32[]{:S(2)}) collective-permute-start(bf16[64,2048]{1,0:T(8,128)(2,1)S(1)} %fusion.158), channel_id=1, source_target_pairs={{0,16},{8,24},{16,0},{24,8},{1,17},{9,25},{17,1},{25,9},{2,18},{10... | collective-permute-start | bytes 786440 | tf_op jit(solution)/shard_map/ppermute | solution.py:91
  563.4 44.4 %collective-permute-start.46 = (bf16[256,2048]{1,0:T(8,128)(2,1)}, bf16[256,2048]{1,0:T(8,128)(2,1)}, u32[]{:S(2)}, u32[]{:S(2)}) collective-permute-start(bf16[256,2048]{1,0:T(8,128)(2,1)} %get-tuple-element.74), channel_id=1, source_target_pairs={{0,16},{8,24},{16,0},{24,8},{1,17},{9,25},{17,1},{25,9},{2,18},{10... | collective-permute-start | bytes 3145736 | tf_op jit(solution)/shard_map/ppermute | solution.py:91
  563.4 53.8 %collective-permute-start.48 = (bf16[256,2048]{1,0:T(8,128)(2,1)}, bf16[256,2048]{1,0:T(8,128)(2,1)}, u32[]{:S(2)}, u32[]{:S(2)}) collective-permute-start(bf16[256,2048]{1,0:T(8,128)(2,1)} %get-tuple-element.73), channel_id=1, source_target_pairs={{0,1},{1,0},{2,3},{3,2},{4,5},{5,4},{6,7},{7,6},{8,9},{9,8},{10,11... | collective-permute-start | bytes 3145736 | tf_op jit(solution)/shard_map/ppermute | solution.py:91
  566.5 134.1 %all-to-all-start.4 = ((bf16[8,576,512]{2,1,0:T(8,128)(2,1)}), bf16[8,576,512]{2,1,0:T(8,128)(2,1)}, u32[]{:S(2)}, u32[]{:S(2)}) async-start(bf16[8,576,512]{2,1,0:T(8,128)(2,1)} %maximum_add_fusion), calls=%async_computation.4 | async-start | bytes 9437184 | tf_op jit(solution)/shard_map/all_to_all | solution.py:95
  571.1 152.0 %all-gather.15.cloned.1.call-start = ((), (), s32[]{:S(2)}) async-start(), calls=%async_computation.11 | async-start | bytes 2359296 | tf_op jit(solution)/shard_map/all_gather | solution.py:598
  598.3 26.3 %collective-permute-start.37 = (bf16[1024,512]{1,0:T(8,128)(2,1)}, bf16[1024,512]{1,0:T(8,128)(2,1)}, u32[]{:S(2)}, u32[]{:S(2)}) collective-permute-start(bf16[1024,512]{1,0:T(8,128)(2,1)} %fusion.11), channel_id=1, source_target_pairs={{0,8},{8,0},{16,24},{24,16},{1,9},{9,1},{17,25},{25,17},{2,10},{10... | collective-permute-start | bytes 3145736 | tf_op jit(solution)/shard_map/ppermute | solution.py:91
  601.3 131.8 %collective-permute-start.35 = (bf16[2,64,2048]{2,1,0:T(8,128)(2,1)}, bf16[2,64,2048]{2,1,0:T(8,128)(2,1)}, u32[]{:S(2)}, u32[]{:S(2)}) collective-permute-start(bf16[2,64,2048]{2,1,0:T(8,128)(2,1)} %fusion.55), channel_id=1, source_target_pairs={{0,8},{8,0},{16,24},{24,16},{1,9},{9,1},{17,25},{25,17},{2,10},{10... | collective-permute-start | bytes 1572872 | tf_op jit(solution)/shard_map/ppermute | solution.py:91
  619.3 12.6 %collective-permute-start.49 = (bf16[128,2048]{1,0:T(8,128)(2,1)S(1)}, bf16[128,2048]{1,0:T(8,128)(2,1)S(1)}, u32[]{:S(2)}, u32[]{:S(2)}) collective-permute-start(bf16[128,2048]{1,0:T(8,128)(2,1)S(1)} %slice.811), channel_id=1, source_target_pairs={{0,16},{8,24},{16,0},{24,8},{1,17},{9,25},{17,1},{25,9},{2,18},{10... | collective-permute-start | bytes 1572872 | tf_op jit(solution)/shard_map/ppermute | solution.py:91
  622.1 84.9 %collective-permute-start.47 = (bf16[128,2048]{1,0:T(8,128)(2,1)}, bf16[128,2048]{1,0:T(8,128)(2,1)}, u32[]{:S(2)}, u32[]{:S(2)}) collective-permute-start(bf16[128,2048]{1,0:T(8,128)(2,1)} %slice.812), channel_id=1, source_target_pairs={{0,1},{1,0},{2,3},{3,2},{4,5},{5,4},{6,7},{7,6},{8,9},{9,8},{10,11... | collective-permute-start | bytes 1572872 | tf_op jit(solution)/shard_map/ppermute | solution.py:91
  626.3 8.4 collective-permute-start.38
  626.6 31.5 %collective-permute-start.40 = (bf16[256,512]{1,0:T(8,128)(2,1)S(1)}, bf16[256,512]{1,0:T(8,128)(2,1)S(1)}, u32[]{:S(2)}, u32[]{:S(2)}) collective-permute-start(bf16[256,512]{1,0:T(8,128)(2,1)S(1)} %get-tuple-element.85), channel_id=1, source_target_pairs={{0,1},{1,0},{2,3},{3,2},{4,5},{5,4},{6,7},{7,6},{8,9},{9,8},{10,11... | collective-permute-start | bytes 786440 | tf_op jit(solution)/shard_map/ppermute | solution.py:91
  660.6 56.2 %collective-permute-start.39 = (bf16[128,512]{1,0:T(8,128)(2,1)}, bf16[128,512]{1,0:T(8,128)(2,1)S(1)}, u32[]{:S(2)}, u32[]{:S(2)}) collective-permute-start(bf16[128,512]{1,0:T(8,128)(2,1)} %slice.820), channel_id=1, source_target_pairs={{0,1},{1,0},{2,3},{3,2},{4,5},{5,4},{6,7},{7,6},{8,9},{9,8},{10,11... | collective-permute-start | bytes 393224 | tf_op jit(solution)/shard_map/ppermute | solution.py:91
  703.3 12.6 %all-to-all-start.5 = ((bf16[8,64,256]{2,1,0:T(8,128)(2,1)}), bf16[8,64,256]{2,1,0:T(8,128)(2,1)S(1)}, u32[]{:S(2)}, u32[]{:S(2)}) async-start(bf16[8,64,256]{2,1,0:T(8,128)(2,1)} %broadcast_add_fusion.2), calls=%async_computation.5 | async-start | bytes 524288 | tf_op jit(solution)/shard_map/all_to_all | solution.py:95
  706.8 128.5 %all-gather.17.cloned.1.call-start = ((), (), s32[]{:S(2)}) async-start(), calls=%async_computation.12 | async-start | bytes 2162688 | tf_op jit(solution)/shard_map/all_gather | solution.py:630
  710.3 8.7 collective-permute-start.41
  732.0 13.9 %collective-permute-start.52 = (bf16[128,2048]{1,0:T(8,128)(2,1)S(1)}, bf16[128,2048]{1,0:T(8,128)(2,1)S(1)}, u32[]{:S(2)}, u32[]{:S(2)}) collective-permute-start(bf16[128,2048]{1,0:T(8,128)(2,1)S(1)} %slice.810), channel_id=1, source_target_pairs={{0,2},{1,3},{2,0},{3,1},{4,6},{5,7},{6,4},{7,5},{8,10},{9,11},{10,... | collective-permute-start | bytes 1572872 | tf_op jit(solution)/shard_map/ppermute | solution.py:91
  738.7 13.5 %collective-permute-start.45 = (bf16[256,512]{0,1:T(8,128)(2,1)}, bf16[256,512]{0,1:T(8,128)(2,1)}, u32[]{:S(2)}, u32[]{:S(2)}) collective-permute-start(bf16[256,512]{0,1:T(8,128)(2,1)} %add_convert_fusion.3), channel_id=1, source_target_pairs={{0,16},{8,24},{16,0},{24,8},{1,17},{9,25},{17,1},{25,9},{2,18},{10... | collective-permute-start | bytes 786440 | tf_op jit(solution)/shard_map/ppermute | solution.py:91
  746.9 17.7 %collective-permute-start.53 = (bf16[64,2048]{1,0:T(8,128)(2,1)}, bf16[64,2048]{1,0:T(8,128)(2,1)S(1)}, u32[]{:S(2)}, u32[]{:S(2)}) collective-permute-start(bf16[64,2048]{1,0:T(8,128)(2,1)} %slice.816), channel_id=1, source_target_pairs={{0,4},{1,5},{2,6},{3,7},{4,0},{5,1},{6,2},{7,3},{8,12},{9,13},{10,... | collective-permute-start | bytes 786440 | tf_op jit(solution)/shard_map/ppermute | solution.py:91
  756.4 7.5 collective-permute-start.50
  759.1 19.1 %collective-permute-start.36 = (bf16[64,2048]{1,0:T(8,128)(2,1)}, bf16[64,2048]{1,0:T(8,128)(2,1)}, u32[]{:S(2)}, u32[]{:S(2)}) collective-permute-start(bf16[64,2048]{1,0:T(8,128)(2,1)} %fusion.63), channel_id=1, source_target_pairs={{0,16},{8,24},{16,0},{24,8},{1,17},{9,25},{17,1},{25,9},{2,18},{10... | collective-permute-start | bytes 786440 | tf_op jit(solution)/shard_map/ppermute | solution.py:91
  786.5 10.7 %collective-permute-start.55 = (f32[4100]{0:T(1024)S(1)}, f32[4100]{0:T(1024)S(1)}, u32[]{:S(2)}, u32[]{:S(2)}) collective-permute-start(f32[4100]{0:T(1024)S(1)} %add.442), channel_id=1, source_target_pairs={{0,16},{8,24},{16,0},{24,8},{1,17},{9,25},{17,1},{25,9},{2,18},{10... | collective-permute-start | bytes 49208 | tf_op jit(solution)/shard_map/ppermute | solution.py:91
  789.6 30.5 %collective-permute-start.61 = (f32[64,2048]{1,0:T(8,128)S(1)}, f32[64,2048]{1,0:T(8,128)S(1)}, u32[]{:S(2)}, u32[]{:S(2)}) collective-permute-start(f32[64,2048]{1,0:T(8,128)S(1)} %get-tuple-element.95), channel_id=1, source_target_pairs={{0,16},{8,24},{16,0},{24,8},{1,17},{9,25},{17,1},{25,9},{2,18},{10... | collective-permute-start | bytes 1572872 | tf_op jit(solution)/shard_map/ppermute | solution.py:91
  797.2 7.5 collective-permute-start.56
  808.9 12.0 %collective-permute-start.63 = (f32[256,768]{1,0:T(8,128)S(1)}, f32[256,768]{1,0:T(8,128)S(1)}, u32[]{:S(2)}, u32[]{:S(2)}) collective-permute-start(f32[256,768]{1,0:T(8,128)S(1)} %constant_dynamic-update-slice_fusion.43), channel_id=1, source_target_pairs={{0,8},{8,0},{16,24},{24,16},{1,9},{9,1},{17,25},{25,17},{2,10},{10... | collective-permute-start | bytes 2359304 | tf_op jit(solution)/shard_map/ppermute | solution.py:91
  809.0 11.0 %collective-permute-start.59 = (bf16[64,2048]{1,0:T(8,128)(2,1)S(1)}, bf16[64,2048]{1,0:T(8,128)(2,1)S(1)}, u32[]{:S(2)}, u32[]{:S(2)}) collective-permute-start(bf16[64,2048]{1,0:T(8,128)(2,1)S(1)} %get-tuple-element.96), channel_id=1, source_target_pairs={{0,16},{8,24},{16,0},{24,8},{1,17},{9,25},{17,1},{25,9},{2,18},{10... | collective-permute-start | bytes 786440 | tf_op jit(solution)/shard_map/ppermute | solution.py:91
  820.2 12.0 %collective-permute-start.62 = (f32[2,64,2048]{2,1,0:T(8,128)S(1)}, f32[2,64,2048]{2,1,0:T(8,128)S(1)}, u32[]{:S(2)}, u32[]{:S(2)}) collective-permute-start(f32[2,64,2048]{2,1,0:T(8,128)S(1)} %maximum_select_fusion.5), channel_id=1, source_target_pairs={{0,8},{8,0},{16,24},{24,16},{1,9},{9,1},{17,25},{25,17},{2,10},{10... | collective-permute-start | bytes 3145736 | tf_op jit(solution)/shard_map/ppermute | solution.py:91
  821.0 11.1 %collective-permute-start.64 = (bf16[256,768]{1,0:T(8,128)(2,1)S(1)}, bf16[256,768]{1,0:T(8,128)(2,1)S(1)}, u32[]{:S(2)}, u32[]{:S(2)}) collective-permute-start(bf16[256,768]{1,0:T(8,128)(2,1)S(1)} %add_convert_fusion.2), channel_id=1, source_target_pairs={{0,16},{8,24},{16,0},{24,8},{1,17},{9,25},{17,1},{25,9},{2,18},{10... | collective-permute-start | bytes 1179656 | tf_op jit(solution)/shard_map/ppermute | solution.py:91
  840.5 23.7 %all-to-all-start.6 = ((bf16[8,32,1536]{2,1,0:T(8,128)(2,1)}), bf16[8,32,1536]{2,1,0:T(8,128)(2,1)S(1)}, u32[]{:S(2)}, u32[]{:S(2)}) async-start(bf16[8,32,1536]{2,1,0:T(8,128)(2,1)} %bitcast.128), calls=%async_computation.6 | async-start | bytes 1572864 | tf_op jit(solution)/shard_map/all_to_all | solution.py:95
  (139 other events, 1953.2 us)
Sparse Core Ops, SparseCore 0:
  12.0 64.8 all-gather.6
  79.6 86.0 all-gather.8
  271.8 83.5 all-gather.12
  358.7 57.7 all-gather.10
  594.9 107.2 all-gather.14
  772.0 57.3 all-gather.16

commit v4 on v3

--- a/solution.py
+++ b/solution.py
@@ -465,13 +465,15 @@
     tokens_own = own_slice(tokens).astype(f32)
     normed_b = rms_norm(tokens.astype(f32), attention_norm_gain).astype(bf16)
 
-    def all_token_cols(rows_own, *others):
-        cols = exchange(after(to_places(rows_own, block_width), *others))
-        cols = cols.reshape(-1, block_width)
-        cols = gather_mp(cols).reshape(mp_count, dp_count, own_rows, block_width)
+    def send_cols(rows_own):
+        return exchange(to_places(rows_own, block_width))
+
+    def all_token_cols(arrived):
+        cols = gather_mp(arrived.reshape(-1, block_width))
+        cols = cols.reshape(mp_count, dp_count, own_rows, block_width)
         return jnp.swapaxes(cols, 0, 1).reshape(dp_count * row_count, block_width)
 
-    normed_cols = all_token_cols(own_slice(normed_b))
+    normed_cols = all_token_cols(send_cols(own_slice(normed_b)))
     pair_own = dot(own_slice(normed_b), kv_full)
     seq_own = own_slice(token_sequence_index)
     spots_own = own_slice(positions)
@@ -527,11 +529,12 @@
         )
     ).reshape(model_width, hidden_own)
     normed2_rows = gather_near(normed2_far)
-    attended_all = lax.all_gather(attended_b, "dp", axis=0, tiled=True)
     left_block = jnp.concatenate([gate_left, up_left, down_left], axis=1)
     left_all = lax.all_gather(
         after(block_slice(left_block), gate_down), ("dp", "mp"), axis=0, tiled=True
     )
+    attended_late = after(lax.optimization_barrier(attended_b), left_all)
+    attended_all = lax.all_gather(attended_late, "dp", axis=0, tiled=True)
     gate_down_other = swap(gate_down, "mp", 1)
     up_other = swap(after(up_own, *halves(normed2_rows)), "mp", 1)
     hidden_b, unit_grad_b, partial, branch_part = feed_forward(
@@ -562,12 +565,13 @@
         axis=1,
     )
     normed2_grad = scatter_far(after(normed2_near, down_sent, gate_up_blocks))
-    gate_up_sent = exchange(after(gate_up_blocks, normed2_grad))
 
     unused_norm, mlp_pull = jax.vjp(rms_norm, middle, feedforward_norm_gain)
     middle_norm_grad, mlp_gain_part = mlp_pull(normed2_grad)
     middle_grad = cotangent_own.astype(f32) + middle_norm_grad
     branch_grad_own = middle_grad.astype(bf16)
+    branch_sent = send_cols(branch_grad_own)
+    gate_up_sent = exchange(after(gate_up_blocks, branch_sent))
     branch_grad = gather_mp(branch_grad_own).reshape(row_count, model_width)
     attended_grad_b = (
         dot(branch_grad, o_full).astype(bf16).reshape(row_count, head_count, HEAD_SIZE)
@@ -590,14 +594,15 @@
         after(current_loop, attended_grad_b), down_sent, 0, block_all, down_update_right, block_width
     )
     pair_near = scatter_near(add_core(pair_partial[half:], pair_partial[:half]))
-    branch_near = scatter_near(after(branch_part, normed2_grad))
+    branch_near = scatter_near(after(branch_part, attended_grad_b))
     query_grad = (
         jnp.einsum("hqk,kd->qhd", score_grad_b, all_keys, preferred_element_type=f32) * score_scale
     )
     query_grad_b = rotate(query_grad, positions, -1.0).reshape(row_count, query_cols).astype(bf16)
     query_grad_all = lax.all_gather(query_grad_b, "dp", axis=0, tiled=True)
-    branch_cols = all_token_cols(branch_grad_own, gate_up_sent)
-    q_weight_grad = dot_rows(normed_cols, query_grad_all)
+    pair_grad_own = scatter_far(after(pair_near, gate_up_sent))
+    branch_cols = all_token_cols(branch_sent)
+    q_weight_grad = dot_rows(after(normed_cols, pair_grad_own), query_grad_all)
     o_weight_grad = dot_rows(branch_cols, attended_all)
     q_weight_b = q_weight_grad.astype(bf16)
     o_weight_b = o_weight_grad.astype(bf16)
@@ -607,14 +612,11 @@
     qo_right = jnp.concatenate(
         [dot_rows(q_left, q_weight_b), dot_rows(o_left, o_weight_b)], axis=1
     ).astype(bf16)
-    pair_grad_own = scatter_far(
-        after(pair_near, gate_up_sent, qo_right, qo_lora_a, *halves(branch_near))
-    )
     pair_grad_b = jnp.concatenate(
         [rotate(pair_grad_own[:, :HEAD_SIZE], spots_own, -1.0), pair_grad_own[:, HEAD_SIZE:]],
         axis=1,
     ).astype(bf16)
-    mlp_branch = scatter_far(after(branch_near, *halves(pair_near)))
+    mlp_branch = scatter_far(after(branch_near, pair_grad_own))
     output_rows = middle + mlp_branch
     mixed = gather_mp(output_rows.astype(bf16)).reshape(row_count, model_width)
     confidence_own = jnp.sum(jax.nn.sigmoid(jnp.dot(output_rows, probe, precision=precise)))
@@ -631,7 +633,7 @@
     small = sum_all(
         jnp.concatenate([attn_gain_part, mlp_gain_part, depth_own, confidence_own.reshape(1)])
     )
-    kv_weight_grad = dot_rows(normed_cols, after(pair_grad_all, small, tokens_grad))
+    kv_weight_grad = dot_rows(normed_cols, after(pair_grad_all, small))
     kv_weight_b = kv_weight_grad.astype(bf16)
     kv_lora_a = jnp.concatenate(
         [

time: 881 us -> 838 us (0.951)
  waiting for transfers between devices: 399 us -> 345 us
  other arithmetic: 79.6 us -> 95.1 us
    all_to_all x7, waiting for transfers between devices: 98.4 us -> 60.7 us  [exchange(): return lax.all_to_all(blocks, 'dp', 0, 0, tiled=True)]
    ppermute x65, waiting for transfers between devices: 287 us -> 272 us  [swap(): lax.ppermute(value, axis, [(place, place ^ bit) for place in range(count)])]
    unnamed x285 -> x291, local copies, waits for them, and re-layouts: 45.9 us -> 51.9 us
    slice x23 -> x17, local copies, waits for them, and re-layouts: 20.2 us -> 16.2 us  [after(): last = other[tuple((size - 1 for size in other.shape))]]
  transfers between devices with their start and end apart: 78 -> 78, of which waited for: 43 -> 41; matrix products, arithmetic and copies ran while one was open for 26% -> 30% of each run, Pallas kernels for 7% -> 8%
where the time goes in v4:
time: 838 us; the launch traced here: 830 us
  waiting for transfers between devices  345 us (41%)
  local copies, waits for them, and re-layouts  107 us (13%)
  starting transfers between devices  106 us (13%)
  other arithmetic  95.1 us (11%)
  matrix products  80.7 us (10%)
  Pallas kernels  65.4 us (8%)
  between operations  31.3 us (4%)
    ppermute x65, waiting for transfers between devices, swap(): lax.ppermute(value, axis, [(place, place ^ bit) for place in range(count)])  272 us
    ppermute x65, starting transfers between devices, swap(): lax.ppermute(value, axis, [(place, place ^ bit) for place in range(count)])  68.7 us
    all_to_all x7, waiting for transfers between devices, exchange(): return lax.all_to_all(blocks, 'dp', 0, 0, tiled=True)  60.7 us
    unnamed x291, local copies, waits for them, and re-layouts  51.9 us
    dot_general x14, matrix products, dot_rows(): lax.dot_general(left, right, (((0,), (0,)), ((), ())), preferred_element_...  41.6 us
    all_to_all x7, starting transfers between devices, exchange(): return lax.all_to_all(blocks, 'dp', 0, 0, tiled=True)  36 us
    pallas_call x1, Pallas kernels, feed_forward(): pl.pallas_call(feed_kernel, out_shape=(jax.ShapeDtypeStruct((rows, pairs...  34.6 us
    pallas_call x3, Pallas kernels, receive_grad(): pl.pallas_call(receive_kernel, out_shape=(jax.ShapeDtypeStruct((rows, pla...  16.8 us
  transfers between devices with their start and end apart: 78, of which 41 were waited for; matrix products, arithmetic and copies ran while one was open for 30% of the time, Pallas kernels for 8%

profile of v4, /device:TPU:0, one launch (start us, length us, event | category | flops | bytes accessed | tf_op | source)
XLA Modules:
  0.0 830.4 jit_solution(7749161876845369191)
XLA Ops:
  13.7 4.0 collective-permute-start.2
  21.4 8.9 %collective-permute-done.2 = bf16[64,2048]{1,0:T(8,128)(2,1)S(1)} collective-permute-done((bf16[64,2048]{1,0:T(8,128)(2,1)S(1)}, bf16[64,2048]{1,0:T(8,128)(2,1)S(1)}, u32[]{:S(2)}, u32[]{:S(2)}) %collective-permute-start.2) | collective-permute-done | bytes 262176 | tf_op jit(solution)/shard_map/ppermute | solution.py:91
  34.2 11.1 %collective-permute-done.5 = bf16[128,2048]{1,0:T(8,128)(2,1)} collective-permute-done((bf16[128,2048]{1,0:T(8,128)(2,1)}, bf16[128,2048]{1,0:T(8,128)(2,1)}, u32[]{:S(2)}, u32[]{:S(2)}) %collective-permute-start.5) | collective-permute-done | bytes 524320 | tf_op jit(solution)/shard_map/ppermute | solution.py:91
  49.6 10.7 %collective-permute-done.6 = bf16[128,2048]{1,0:T(8,128)(2,1)S(1)} collective-permute-done((bf16[128,2048]{1,0:T(8,128)(2,1)}, bf16[128,2048]{1,0:T(8,128)(2,1)S(1)}, u32[]{:S(2)}, u32[]{:S(2)}) %collective-permute-start.6) | collective-permute-done | bytes 524320 | tf_op jit(solution)/shard_map/ppermute | solution.py:91
  64.0 12.7 %all-gather.7.cloned.1.call-done = bf16[2048,512]{1,0:T(8,128)(2,1)} async-done(((bf16[64,512]{1,0:T(8,128)(2,1)}), bf16[2048,512]{1,0:T(8,128)(2,1)}) %all-gather.7.cloned.1.call-update) | async-done | bytes 2097168 | tf_op jit(solution)/shard_map/all_gather | solution.py:445
  80.0 6.0 collective-permute-done
  90.1 9.8 %collective-permute-done.1 = bf16[144,512]{1,0:T(8,128)(2,1)S(1)} collective-permute-done((bf16[144,512]{1,0:T(8,128)(2,1)S(1)}, bf16[144,512]{1,0:T(8,128)(2,1)S(1)}, u32[]{:S(2)}, u32[]{:S(2)}) %collective-permute-start.1) | collective-permute-done | bytes 147488 | tf_op jit(solution)/shard_map/ppermute | solution.py:91
  111.3 3.5 collective-permute-done.9
  119.4 3.9 all-to-all-start
  128.3 11.6 %collective-permute-done.11 = bf16[288,512]{1,0:T(8,128)(2,1)S(1)} collective-permute-done((bf16[288,512]{1,0:T(8,128)(2,1)S(1)}, bf16[288,512]{1,0:T(8,128)(2,1)S(1)}, u32[]{:S(2)}, u32[]{:S(2)}) %collective-permute-start.11) | collective-permute-done | bytes 294944 | tf_op jit(solution)/shard_map/ppermute | solution.py:91
  143.8 7.5 shard_map.442
  151.4 5.0 all-to-all-start.1
  163.1 7.0 collective-permute-done.13
  176.9 2.8 fusion.170
  182.0 3.1 fusion.27
  186.8 4.5 fusion.177
  191.4 3.3 convolution_convert_fusion.7
  204.0 6.6 collective-permute-done.16
  213.3 38.6 %all-to-all-done.1 = bf16[8,256,1024]{2,1,0:T(8,128)(2,1)} async-done(((bf16[8,256,1024]{2,1,0:T(8,128)(2,1)}), bf16[8,256,1024]{2,1,0:T(8,128)(2,1)}, u32[]{:S(2)}, u32[]{:S(2)}) %all-to-all-start.1) | async-done | bytes 4194336 | tf_op jit(solution)/shard_map/all_to_all | solution.py:95
  256.7 11.5 %collective-permute-done.17 = bf16[64,2048]{1,0:T(8,128)(2,1)S(1)} collective-permute-done((bf16[64,2048]{1,0:T(8,128)(2,1)S(1)}, bf16[64,2048]{1,0:T(8,128)(2,1)S(1)}, u32[]{:S(2)}, u32[]{:S(2)}) %collective-permute-start.17) | collective-permute-done | bytes 262176 | tf_op jit(solution)/shard_map/ppermute | solution.py:91
  270.4 14.2 %collective-permute-done.20 = bf16[128,2048]{1,0:T(8,128)(2,1)} collective-permute-done((bf16[128,2048]{1,0:T(8,128)(2,1)}, bf16[128,2048]{1,0:T(8,128)(2,1)}, u32[]{:S(2)}, u32[]{:S(2)}) %collective-permute-start.20) | collective-permute-done | bytes 524320 | tf_op jit(solution)/shard_map/ppermute | solution.py:91
  286.5 6.4 shard_map.443
  293.0 3.7 all-to-all-start.2
  300.2 28.0 %collective-permute-done.18 = bf16[128,2048]{1,0:T(8,128)(2,1)S(1)} collective-permute-done((bf16[128,2048]{1,0:T(8,128)(2,1)}, bf16[128,2048]{1,0:T(8,128)(2,1)S(1)}, u32[]{:S(2)}, u32[]{:S(2)}) %collective-permute-start.18) | collective-permute-done | bytes 524320 | tf_op jit(solution)/shard_map/ppermute | solution.py:91
  338.2 17.8 %collective-permute-done.19 = bf16[256,2048]{1,0:T(8,128)(2,1)S(1)} collective-permute-done((bf16[256,2048]{1,0:T(8,128)(2,1)S(1)}, bf16[256,2048]{1,0:T(8,128)(2,1)S(1)}, u32[]{:S(2)}, u32[]{:S(2)}) %collective-permute-start.19) | collective-permute-done | bytes 1048608 | tf_op jit(solution)/shard_map/ppermute | solution.py:91
  357.3 3.1 collective-permute-done.22
  377.6 34.6 %shard_map.444 = (bf16[1024,1024]{1,0:T(8,128)(2,1)}, bf16[1024,2048]{1,0:T(8,128)(2,1)}, f32[1024,2048]{1,0:T(8,128)}, bf16[1024,2048]{1,0:T(8,128)(2,1)}) custom-call(bf16[1024,2048]{1,0:T(8,128)(2,1)} %constant_dynamic-update-slice_fusion.21.normed_ref, bf16[1024,2048]{1,0:T(8,128)(2,1)} %constant_dynamic-update-slice_fusion.28.cotangent_ref, ...), custom_call_target="tpu_custom_call" | custom-call | tf_op jit(solution)/shard_map/pallas_call | solution.py:351
  412.2 5.0 convolution_convert_fusion.1
  417.8 6.6 convolution_convert_fusion
  428.8 4.7 add_convert_fusion.1
  439.1 9.1 %all-to-all-start.3 = ((bf16[8,288,512]{2,1,0:T(8,128)(2,1)}), bf16[8,288,512]{2,1,0:T(8,128)(2,1)S(1)}, u32[]{:S(2)}, u32[]{:S(2)}) async-start(bf16[8,288,512]{2,1,0:T(8,128)(2,1)} %pad_maximum_fusion), calls=%async_computation.3 | async-start | bytes 4718592 | tf_op jit(solution)/shard_map/all_to_all | solution.py:95
  448.3 4.2 collective-permute-done.25
  452.4 12.1 %collective-permute-done.27 = bf16[256,2048]{1,0:T(8,128)(2,1)} collective-permute-done((bf16[256,2048]{1,0:T(8,128)(2,1)}, bf16[256,2048]{1,0:T(8,128)(2,1)}, u32[]{:S(2)}, u32[]{:S(2)}) %collective-permute-start.27) | collective-permute-done | bytes 1048608 | tf_op jit(solution)/shard_map/ppermute | solution.py:91
  464.5 3.6 convert_add_fusion.1
  468.2 3.0 collective-permute-start.26
  474.7 15.4 %collective-permute-done.26 = bf16[128,2048]{1,0:T(8,128)(2,1)S(1)} collective-permute-done((bf16[128,2048]{1,0:T(8,128)(2,1)S(1)}, bf16[128,2048]{1,0:T(8,128)(2,1)S(1)}, u32[]{:S(2)}, u32[]{:S(2)}) %collective-permute-start.26) | collective-permute-done | bytes 524320 | tf_op jit(solution)/shard_map/ppermute | solution.py:91
  492.3 6.6 add_convert_fusion
  498.9 2.8 convolution_convert_fusion.5
  506.2 8.7 %collective-permute-start.31 = (bf16[128,2048]{1,0:T(8,128)(2,1)S(1)}, bf16[128,2048]{1,0:T(8,128)(2,1)S(1)}, u32[]{:S(2)}, u32[]{:S(2)}) collective-permute-start(bf16[128,2048]{1,0:T(8,128)(2,1)S(1)} %slice.789), channel_id=1, source_target_pairs={{0,2},{1,3},{2,0},{3,1},{4,6},{5,7},{6,4},{7,5},{8,10},{9,11},{10,... | collective-permute-start | bytes 1572872 | tf_op jit(solution)/shard_map/ppermute | solution.py:91
  517.2 4.9 collective-permute-done.31
  522.3 2.9 collective-permute-start.32
  525.2 2.7 convolution_convert_fusion.4
  527.9 8.5 %collective-permute-done.32 = bf16[64,2048]{1,0:T(8,128)(2,1)S(1)} collective-permute-done((bf16[64,2048]{1,0:T(8,128)(2,1)S(1)}, bf16[64,2048]{1,0:T(8,128)(2,1)S(1)}, u32[]{:S(2)}, u32[]{:S(2)}) %collective-permute-start.32) | collective-permute-done | bytes 262176 | tf_op jit(solution)/shard_map/ppermute | solution.py:91
  544.2 5.4 all-to-all-start.4
  553.4 4.7 all-to-all-done.4
  561.1 4.2 maximum_add_fusion
  565.3 4.6 all-to-all-start.5
  580.5 3.5 fusion.1
  589.4 5.3 convolution_bitcast_fusion
  600.5 4.1 fusion.161
  615.0 5.2 shard_map.447
  633.1 4.8 collective-permute-done.38
  637.9 25.4 %collective-permute-done.40 = bf16[256,512]{1,0:T(8,128)(2,1)S(1)} collective-permute-done((bf16[256,512]{1,0:T(8,128)(2,1)S(1)}, bf16[256,512]{1,0:T(8,128)(2,1)S(1)}, u32[]{:S(2)}, u32[]{:S(2)}) %collective-permute-start.40) | collective-permute-done | bytes 262176 | tf_op jit(solution)/shard_map/ppermute | solution.py:91
  673.8 13.2 %collective-permute-done.41 = bf16[128,512]{1,0:T(8,128)(2,1)S(1)} collective-permute-done((bf16[128,512]{1,0:T(8,128)(2,1)S(1)}, bf16[128,512]{1,0:T(8,128)(2,1)S(1)}, u32[]{:S(2)}, u32[]{:S(2)}) %collective-permute-start.41) | collective-permute-done | bytes 131104 | tf_op jit(solution)/shard_map/ppermute | solution.py:91
  687.8 4.4 all-to-all-done.5.arrived_ref
  697.8 4.1 collective-permute-done.42
  701.9 3.0 collective-permute-start.43
  719.4 5.8 shard_map.445
  725.9 5.9 shard_map.446
  743.2 11.3 %collective-permute-done.57 = f32[64,2048]{1,0:T(8,128)S(1)} collective-permute-done((f32[64,2048]{1,0:T(8,128)S(1)}, f32[64,2048]{1,0:T(8,128)S(1)}, u32[]{:S(2)}, u32[]{:S(2)}) %collective-permute-start.57) | collective-permute-done | bytes 524320 | tf_op jit(solution)/shard_map/ppermute | solution.py:91
  782.6 4.7 collective-permute-done.55
  791.3 3.2 fusion.178
  795.9 4.3 all-to-all-start.6
  807.9 13.0 %all-to-all-done.6 = bf16[8,32,1536]{2,1,0:T(8,128)(2,1)S(1)} async-done(((bf16[8,32,1536]{2,1,0:T(8,128)(2,1)}), bf16[8,32,1536]{2,1,0:T(8,128)(2,1)S(1)}, u32[]{:S(2)}, u32[]{:S(2)}) %all-to-all-start.6) | async-done | bytes 786464 | tf_op jit(solution)/shard_map/all_to_all | solution.py:95
  (616 shorter events, 278.4 us)
Async XLA Ops:
  7.2 69.5 %all-gather.7.cloned.1.call-start = ((), (), s32[]{:S(2)}) async-start(), calls=%async_computation.7 | async-start | bytes 2162688 | tf_op jit(solution)/shard_map/all_gather | solution.py:445
  11.9 170.1 %all-gather.9.cloned.1.call-start = ((), (), s32[]{:S(2)}) async-start(), calls=%async_computation.8 | async-start | bytes 4718592 | tf_op jit(solution)/shard_map/all_gather | solution.py:451
  13.7 16.6 %collective-permute-start.2 = (bf16[64,2048]{1,0:T(8,128)(2,1)S(1)}, bf16[64,2048]{1,0:T(8,128)(2,1)S(1)}, u32[]{:S(2)}, u32[]{:S(2)}) collective-permute-start(bf16[64,2048]{1,0:T(8,128)(2,1)S(1)} %get-tuple-element.63), channel_id=1, source_target_pairs={{0,4},{1,5},{2,6},{3,7},{4,0},{5,1},{6,2},{7,3},{8,12},{9,13},{10,... | collective-permute-start | bytes 786440 | tf_op jit(solution)/shard_map/ppermute | solution.py:91
  31.1 14.1 %collective-permute-start.5 = (bf16[128,2048]{1,0:T(8,128)(2,1)}, bf16[128,2048]{1,0:T(8,128)(2,1)}, u32[]{:S(2)}, u32[]{:S(2)}) collective-permute-start(bf16[128,2048]{1,0:T(8,128)(2,1)} %pad_maximum_fusion.7), channel_id=1, source_target_pairs={{0,2},{1,3},{2,0},{3,1},{4,6},{5,7},{6,4},{7,5},{8,10},{9,11},{10,... | collective-permute-start | bytes 1572872 | tf_op jit(solution)/shard_map/ppermute | solution.py:91
  32.6 14.5 %collective-permute-start.3 = (bf16[128,2048]{1,0:T(8,128)(2,1)}, bf16[128,2048]{1,0:T(8,128)(2,1)S(1)}, u32[]{:S(2)}, u32[]{:S(2)}) collective-permute-start(bf16[128,2048]{1,0:T(8,128)(2,1)} %pad_maximum_fusion.7), channel_id=1, source_target_pairs={{0,1},{1,0},{2,3},{3,2},{4,5},{5,4},{6,7},{7,6},{8,9},{9,8},{10,11... | collective-permute-start | bytes 1572872 | tf_op jit(solution)/shard_map/ppermute | solution.py:91
  45.3 15.1 %collective-permute-start.6 = (bf16[128,2048]{1,0:T(8,128)(2,1)}, bf16[128,2048]{1,0:T(8,128)(2,1)S(1)}, u32[]{:S(2)}, u32[]{:S(2)}) collective-permute-start(bf16[128,2048]{1,0:T(8,128)(2,1)} %collective-permute-done.5), channel_id=1, source_target_pairs={{0,16},{8,24},{16,0},{24,8},{1,17},{9,25},{17,1},{25,9},{2,18},{10... | collective-permute-start | bytes 1572872 | tf_op jit(solution)/shard_map/ppermute | solution.py:91
  48.2 38.0 %collective-permute-start.4 = (bf16[256,2048]{1,0:T(8,128)(2,1)}, bf16[256,2048]{1,0:T(8,128)(2,1)}, u32[]{:S(2)}, u32[]{:S(2)}) collective-permute-start(bf16[256,2048]{1,0:T(8,128)(2,1)} %pad_maximum_fusion.2), channel_id=1, source_target_pairs={{0,16},{8,24},{16,0},{24,8},{1,17},{9,25},{17,1},{25,9},{2,18},{10... | collective-permute-start | bytes 3145736 | tf_op jit(solution)/shard_map/ppermute | solution.py:91
  62.6 25.5 %collective-permute-start.7 = (bf16[256,2048]{1,0:T(8,128)(2,1)}, bf16[256,2048]{1,0:T(8,128)(2,1)}, u32[]{:S(2)}, u32[]{:S(2)}) collective-permute-start(bf16[256,2048]{1,0:T(8,128)(2,1)} %pad_maximum_fusion.3), channel_id=1, source_target_pairs={{0,1},{1,0},{2,3},{3,2},{4,5},{5,4},{6,7},{7,6},{8,9},{9,8},{10,11... | collective-permute-start | bytes 3145736 | tf_op jit(solution)/shard_map/ppermute | solution.py:91
  86.0 13.9 %collective-permute-start.1 = (bf16[144,512]{1,0:T(8,128)(2,1)S(1)}, bf16[144,512]{1,0:T(8,128)(2,1)S(1)}, u32[]{:S(2)}, u32[]{:S(2)}) collective-permute-start(bf16[144,512]{1,0:T(8,128)(2,1)S(1)} %pad_maximum_fusion.14), channel_id=1, source_target_pairs={{0,2},{1,3},{2,0},{3,1},{4,6},{5,7},{6,4},{7,5},{8,10},{9,11},{10,... | collective-permute-start | bytes 442376 | tf_op jit(solution)/shard_map/ppermute | solution.py:91
  119.4 32.0 %all-to-all-start = ((bf16[8,64,256]{2,1,0:T(8,128)(2,1)}), bf16[8,64,256]{2,1,0:T(8,128)(2,1)S(1)}, u32[]{:S(2)}, u32[]{:S(2)}) async-start(bf16[8,64,256]{2,1,0:T(8,128)(2,1)} %constant_dynamic-update-slice_fusion.13), calls=%async_computation | async-start | bytes 524288 | tf_op jit(solution)/shard_map/all_to_all | solution.py:95
  124.4 15.5 %collective-permute-start.11 = (bf16[288,512]{1,0:T(8,128)(2,1)S(1)}, bf16[288,512]{1,0:T(8,128)(2,1)S(1)}, u32[]{:S(2)}, u32[]{:S(2)}) collective-permute-start(bf16[288,512]{1,0:T(8,128)(2,1)S(1)} %pad_maximum_fusion.13), channel_id=1, source_target_pairs={{0,1},{1,0},{2,3},{3,2},{4,5},{5,4},{6,7},{7,6},{8,9},{9,8},{10,11... | collective-permute-start | bytes 884744 | tf_op jit(solution)/shard_map/ppermute | solution.py:91
  151.4 100.5 %all-to-all-start.1 = ((bf16[8,256,1024]{2,1,0:T(8,128)(2,1)}), bf16[8,256,1024]{2,1,0:T(8,128)(2,1)}, u32[]{:S(2)}, u32[]{:S(2)}) async-start(bf16[8,256,1024]{2,1,0:T(8,128)(2,1)} %shard_map.442), calls=%async_computation.1 | async-start | bytes 8388608 | tf_op jit(solution)/shard_map/all_to_all | solution.py:95
  156.4 216.6 %all-gather.11.cloned.1.call-start = ((), (), s32[]{:S(2)}) async-start(), calls=%async_computation.9 | async-start | bytes 3244032 | tf_op jit(solution)/shard_map/all_gather | solution.py:533
  161.3 13.6 %collective-permute-start.12 = (bf16[1152,512]{1,0:T(8,128)(2,1)}, bf16[1152,512]{1,0:T(8,128)(2,1)S(1)}, u32[]{:S(2)}, u32[]{:S(2)}) collective-permute-start(bf16[1152,512]{1,0:T(8,128)(2,1)} %get-tuple-element.98), channel_id=1, source_target_pairs={{0,8},{8,0},{16,24},{24,16},{1,9},{9,1},{17,25},{25,17},{2,10},{10... | collective-permute-start | bytes 3538952 | tf_op jit(solution)/shard_map/ppermute | solution.py:91
  161.3 8.8 %collective-permute-start.13 = (bf16[512,256]{1,0:T(8,128)(2,1)S(1)}, bf16[512,256]{1,0:T(8,128)(2,1)S(1)}, u32[]{:S(2)}, u32[]{:S(2)}) collective-permute-start(bf16[512,256]{1,0:T(8,128)(2,1)S(1)} %bitcast.321), channel_id=1, source_target_pairs={{0,16},{8,24},{16,0},{24,8},{1,17},{9,25},{17,1},{25,9},{2,18},{10... | collective-permute-start | bytes 786440 | tf_op jit(solution)/shard_map/ppermute | solution.py:91
  255.7 12.5 %collective-permute-start.17 = (bf16[64,2048]{1,0:T(8,128)(2,1)S(1)}, bf16[64,2048]{1,0:T(8,128)(2,1)S(1)}, u32[]{:S(2)}, u32[]{:S(2)}) collective-permute-start(bf16[64,2048]{1,0:T(8,128)(2,1)S(1)} %get-tuple-element.65), channel_id=1, source_target_pairs={{0,4},{1,5},{2,6},{3,7},{4,0},{5,1},{6,2},{7,3},{8,12},{9,13},{10,... | collective-permute-start | bytes 786440 | tf_op jit(solution)/shard_map/ppermute | solution.py:91
  269.7 14.9 %collective-permute-start.20 = (bf16[128,2048]{1,0:T(8,128)(2,1)}, bf16[128,2048]{1,0:T(8,128)(2,1)}, u32[]{:S(2)}, u32[]{:S(2)}) collective-permute-start(bf16[128,2048]{1,0:T(8,128)(2,1)} %pad_maximum_fusion.9), channel_id=1, source_target_pairs={{0,2},{1,3},{2,0},{3,1},{4,6},{5,7},{6,4},{7,5},{8,10},{9,11},{10,... | collective-permute-start | bytes 1572872 | tf_op jit(solution)/shard_map/ppermute | solution.py:91
  293.0 68.8 %all-to-all-start.2 = ((bf16[8,256,512]{2,1,0:T(8,128)(2,1)}), bf16[8,256,512]{2,1,0:T(8,128)(2,1)S(1)}, u32[]{:S(2)}, u32[]{:S(2)}) async-start(bf16[8,256,512]{2,1,0:T(8,128)(2,1)} %shard_map.443), calls=%async_computation.2 | async-start | bytes 4194304 | tf_op jit(solution)/shard_map/all_to_all | solution.py:95
  296.7 136.8 %all-gather.13.cloned.1.call-start = ((), (), s32[]{:S(2)}) async-start(), calls=%async_computation.10 | async-start | bytes 2359296 | tf_op jit(solution)/shard_map/all_gather | solution.py:537
  296.7 31.5 %collective-permute-start.18 = (bf16[128,2048]{1,0:T(8,128)(2,1)}, bf16[128,2048]{1,0:T(8,128)(2,1)S(1)}, u32[]{:S(2)}, u32[]{:S(2)}) collective-permute-start(bf16[128,2048]{1,0:T(8,128)(2,1)} %pad_maximum_fusion.9), channel_id=1, source_target_pairs={{0,1},{1,0},{2,3},{3,2},{4,5},{5,4},{6,7},{7,6},{8,9},{9,8},{10,11... | collective-permute-start | bytes 1572872 | tf_op jit(solution)/shard_map/ppermute | solution.py:91
  298.8 32.0 %collective-permute-start.21 = (bf16[128,2048]{1,0:T(8,128)(2,1)}, bf16[128,2048]{1,0:T(8,128)(2,1)S(1)}, u32[]{:S(2)}, u32[]{:S(2)}) collective-permute-start(bf16[128,2048]{1,0:T(8,128)(2,1)} %collective-permute-done.20), channel_id=1, source_target_pairs={{0,16},{8,24},{16,0},{24,8},{1,17},{9,25},{17,1},{25,9},{2,18},{10... | collective-permute-start | bytes 1572872 | tf_op jit(solution)/shard_map/ppermute | solution.py:91
  300.2 77.3 %collective-permute-start.23 = (bf16[2048,1024]{1,0:T(8,128)(2,1)}, bf16[2048,1024]{1,0:T(8,128)(2,1)}, u32[]{:S(2)}, u32[]{:S(2)}) collective-permute-start(bf16[2048,1024]{1,0:T(8,128)(2,1)} %bitcast.46.refs_0_), channel_id=1, source_target_pairs={{0,8},{8,0},{16,24},{24,16},{1,9},{9,1},{17,25},{25,17},{2,10},{10... | collective-permute-start | bytes 12582920 | tf_op jit(solution)/shard_map/ppermute | solution.py:91
  329.5 26.5 %collective-permute-start.19 = (bf16[256,2048]{1,0:T(8,128)(2,1)S(1)}, bf16[256,2048]{1,0:T(8,128)(2,1)S(1)}, u32[]{:S(2)}, u32[]{:S(2)}) collective-permute-start(bf16[256,2048]{1,0:T(8,128)(2,1)S(1)} %pad_maximum_fusion.4), channel_id=1, source_target_pairs={{0,16},{8,24},{16,0},{24,8},{1,17},{9,25},{17,1},{25,9},{2,18},{10... | collective-permute-start | bytes 3145736 | tf_op jit(solution)/shard_map/ppermute | solution.py:91
  332.1 28.3 %collective-permute-start.22 = (bf16[256,2048]{1,0:T(8,128)(2,1)S(1)}, bf16[256,2048]{1,0:T(8,128)(2,1)S(1)}, u32[]{:S(2)}, u32[]{:S(2)}) collective-permute-start(bf16[256,2048]{1,0:T(8,128)(2,1)S(1)} %pad_maximum_fusion.5), channel_id=1, source_target_pairs={{0,1},{1,0},{2,3},{3,2},{4,5},{5,4},{6,7},{7,6},{8,9},{9,8},{10,11... | collective-permute-start | bytes 3145736 | tf_op jit(solution)/shard_map/ppermute | solution.py:91
  363.8 13.8 %collective-permute-start.24 = (bf16[2048,512]{1,0:T(8,128)(2,1)}, bf16[2048,512]{1,0:T(8,128)(2,1)}, u32[]{:S(2)}, u32[]{:S(2)}) collective-permute-start(bf16[2048,512]{1,0:T(8,128)(2,1)} %broadcast_add_fusion.1), channel_id=1, source_target_pairs={{0,8},{8,0},{16,24},{24,16},{1,9},{9,1},{17,25},{25,17},{2,10},{10... | collective-permute-start | bytes 6291464 | tf_op jit(solution)/shard_map/ppermute | solution.py:91
  417.2 11.6 %collective-permute-start.29 = (bf16[2048,512]{1,0:T(8,128)(2,1)S(1)}, bf16[2048,512]{1,0:T(8,128)(2,1)S(1)}, u32[]{:S(2)}, u32[]{:S(2)}) collective-permute-start(bf16[2048,512]{1,0:T(8,128)(2,1)S(1)} %convolution_convert_fusion.1), channel_id=1, source_target_pairs={{0,8},{8,0},{16,24},{24,16},{1,9},{9,1},{17,25},{25,17},{2,10},{10... | collective-permute-start | bytes 6291464 | tf_op jit(solution)/shard_map/ppermute | solution.py:91
  424.4 67.9 %collective-permute-start.30 = (bf16[2048,1024]{1,0:T(8,128)(2,1)}, bf16[2048,1024]{1,0:T(8,128)(2,1)}, u32[]{:S(2)}, u32[]{:S(2)}) collective-permute-start(bf16[2048,1024]{1,0:T(8,128)(2,1)} %convolution_convert_fusion), channel_id=1, source_target_pairs={{0,8},{8,0},{16,24},{24,16},{1,9},{9,1},{17,25},{25,17},{2,10},{10... | collective-permute-start | bytes 12582920 | tf_op jit(solution)/shard_map/ppermute | solution.py:91
  426.6 25.8 %collective-permute-start.25 = (bf16[256,2048]{1,0:T(8,128)(2,1)}, bf16[256,2048]{1,0:T(8,128)(2,1)}, u32[]{:S(2)}, u32[]{:S(2)}) collective-permute-start(bf16[256,2048]{1,0:T(8,128)(2,1)} %get-tuple-element.78), channel_id=1, source_target_pairs={{0,16},{8,24},{16,0},{24,8},{1,17},{9,25},{17,1},{25,9},{2,18},{10... | collective-permute-start | bytes 3145736 | tf_op jit(solution)/shard_map/ppermute | solution.py:91
  428.1 36.5 %collective-permute-start.27 = (bf16[256,2048]{1,0:T(8,128)(2,1)}, bf16[256,2048]{1,0:T(8,128)(2,1)}, u32[]{:S(2)}, u32[]{:S(2)}) collective-permute-start(bf16[256,2048]{1,0:T(8,128)(2,1)} %get-tuple-element.79), channel_id=1, source_target_pairs={{0,1},{1,0},{2,3},{3,2},{4,5},{5,4},{6,7},{7,6},{8,9},{9,8},{10,11... | collective-permute-start | bytes 3145736 | tf_op jit(solution)/shard_map/ppermute | solution.py:91
  439.1 64.0 %all-to-all-start.3 = ((bf16[8,288,512]{2,1,0:T(8,128)(2,1)}), bf16[8,288,512]{2,1,0:T(8,128)(2,1)S(1)}, u32[]{:S(2)}, u32[]{:S(2)}) async-start(bf16[8,288,512]{2,1,0:T(8,128)(2,1)} %pad_maximum_fusion), calls=%async_computation.3 | async-start | bytes 4718592 | tf_op jit(solution)/shard_map/all_to_all | solution.py:95
  468.2 21.9 %collective-permute-start.26 = (bf16[128,2048]{1,0:T(8,128)(2,1)S(1)}, bf16[128,2048]{1,0:T(8,128)(2,1)S(1)}, u32[]{:S(2)}, u32[]{:S(2)}) collective-permute-start(bf16[128,2048]{1,0:T(8,128)(2,1)S(1)} %slice.791), channel_id=1, source_target_pairs={{0,1},{1,0},{2,3},{3,2},{4,5},{5,4},{6,7},{7,6},{8,9},{9,8},{10,11... | collective-permute-start | bytes 1572872 | tf_op jit(solution)/shard_map/ppermute | solution.py:91
  474.1 17.1 %collective-permute-start.28 = (bf16[128,2048]{1,0:T(8,128)(2,1)S(1)}, bf16[128,2048]{1,0:T(8,128)(2,1)S(1)}, u32[]{:S(2)}, u32[]{:S(2)}) collective-permute-start(bf16[128,2048]{1,0:T(8,128)(2,1)S(1)} %slice.790), channel_id=1, source_target_pairs={{0,16},{8,24},{16,0},{24,8},{1,17},{9,25},{17,1},{25,9},{2,18},{10... | collective-permute-start | bytes 1572872 | tf_op jit(solution)/shard_map/ppermute | solution.py:91
  506.2 15.9 %collective-permute-start.31 = (bf16[128,2048]{1,0:T(8,128)(2,1)S(1)}, bf16[128,2048]{1,0:T(8,128)(2,1)S(1)}, u32[]{:S(2)}, u32[]{:S(2)}) collective-permute-start(bf16[128,2048]{1,0:T(8,128)(2,1)S(1)} %slice.789), channel_id=1, source_target_pairs={{0,2},{1,3},{2,0},{3,1},{4,6},{5,7},{6,4},{7,5},{8,10},{9,11},{10,... | collective-permute-start | bytes 1572872 | tf_op jit(solution)/shard_map/ppermute | solution.py:91
  522.3 14.1 %collective-permute-start.32 = (bf16[64,2048]{1,0:T(8,128)(2,1)S(1)}, bf16[64,2048]{1,0:T(8,128)(2,1)S(1)}, u32[]{:S(2)}, u32[]{:S(2)}) collective-permute-start(bf16[64,2048]{1,0:T(8,128)(2,1)S(1)} %slice.793), channel_id=1, source_target_pairs={{0,4},{1,5},{2,6},{3,7},{4,0},{5,1},{6,2},{7,3},{8,12},{9,13},{10,... | collective-permute-start | bytes 786440 | tf_op jit(solution)/shard_map/ppermute | solution.py:91
  538.8 10.8 %collective-permute-start.33 = (bf16[64,2048]{1,0:T(8,128)(2,1)S(1)}, bf16[64,2048]{1,0:T(8,128)(2,1)}, u32[]{:S(2)}, u32[]{:S(2)}) collective-permute-start(bf16[64,2048]{1,0:T(8,128)(2,1)S(1)} %get-tuple-element.60), channel_id=1, source_target_pairs={{0,16},{8,24},{16,0},{24,8},{1,17},{9,25},{17,1},{25,9},{2,18},{10... | collective-permute-start | bytes 786440 | tf_op jit(solution)/shard_map/ppermute | solution.py:91
  544.2 13.9 %all-to-all-start.4 = ((bf16[8,64,256]{2,1,0:T(8,128)(2,1)}), bf16[8,64,256]{2,1,0:T(8,128)(2,1)}, u32[]{:S(2)}, u32[]{:S(2)}) async-start(bf16[8,64,256]{2,1,0:T(8,128)(2,1)} %constant_dynamic-update-slice_fusion.35), calls=%async_computation.4 | async-start | bytes 524288 | tf_op jit(solution)/shard_map/all_to_all | solution.py:95
  551.5 22.5 %collective-permute-start.34 = (bf16[2,64,2048]{2,1,0:T(8,128)(2,1)}, bf16[2,64,2048]{2,1,0:T(8,128)(2,1)}, u32[]{:S(2)}, u32[]{:S(2)}) collective-permute-start(bf16[2,64,2048]{2,1,0:T(8,128)(2,1)} %maximum_select_fusion.8), channel_id=1, source_target_pairs={{0,8},{8,0},{16,24},{24,16},{1,9},{9,1},{17,25},{25,17},{2,10},{10... | collective-permute-start | bytes 1572872 | tf_op jit(solution)/shard_map/ppermute | solution.py:91
  560.0 10.1 %collective-permute-start.59 = (bf16[512,256]{1,0:T(8,128)(2,1)}, bf16[512,256]{1,0:T(8,128)(2,1)S(1)}, u32[]{:S(2)}, u32[]{:S(2)}) collective-permute-start(bf16[512,256]{1,0:T(8,128)(2,1)} %bitcast.113), channel_id=1, source_target_pairs={{0,16},{8,24},{16,0},{24,8},{1,17},{9,25},{17,1},{25,9},{2,18},{10... | collective-permute-start | bytes 786440 | tf_op jit(solution)/shard_map/ppermute | solution.py:91
  565.3 126.9 %all-to-all-start.5 = ((bf16[8,576,512]{2,1,0:T(8,128)(2,1)}), bf16[8,576,512]{2,1,0:T(8,128)(2,1)}, u32[]{:S(2)}, u32[]{:S(2)}) async-start(bf16[8,576,512]{2,1,0:T(8,128)(2,1)} %maximum_add_fusion), calls=%async_computation.5 | async-start | bytes 9437184 | tf_op jit(solution)/shard_map/all_to_all | solution.py:95
  569.9 145.2 %all-gather.15.cloned.1.call-start = ((), (), s32[]{:S(2)}) async-start(), calls=%async_computation.11 | async-start | bytes 2359296 | tf_op jit(solution)/shard_map/all_gather | solution.py:602
  572.2 48.0 %collective-permute-start.60 = (bf16[2,512,256]{2,1,0:T(8,128)(2,1)}, bf16[2,512,256]{2,1,0:T(8,128)(2,1)}, u32[]{:S(2)}, u32[]{:S(2)}) collective-permute-start(bf16[2,512,256]{2,1,0:T(8,128)(2,1)} %maximum_select_fusion.12), channel_id=1, source_target_pairs={{0,8},{8,0},{16,24},{24,16},{1,9},{9,1},{17,25},{25,17},{2,10},{10... | collective-permute-start | bytes 1572872 | tf_op jit(solution)/shard_map/ppermute | solution.py:91
  598.8 27.9 %collective-permute-start.37 = (bf16[1024,512]{1,0:T(8,128)(2,1)}, bf16[1024,512]{1,0:T(8,128)(2,1)}, u32[]{:S(2)}, u32[]{:S(2)}) collective-permute-start(bf16[1024,512]{1,0:T(8,128)(2,1)} %fusion.11), channel_id=1, source_target_pairs={{0,8},{8,0},{16,24},{24,16},{1,9},{9,1},{17,25},{25,17},{2,10},{10... | collective-permute-start | bytes 3145736 | tf_op jit(solution)/shard_map/ppermute | solution.py:91
  606.1 57.5 %collective-permute-start.44 = (bf16[256,2048]{1,0:T(8,128)(2,1)}, bf16[256,2048]{1,0:T(8,128)(2,1)}, u32[]{:S(2)}, u32[]{:S(2)}) collective-permute-start(bf16[256,2048]{1,0:T(8,128)(2,1)} %get-tuple-element.74), channel_id=1, source_target_pairs={{0,16},{8,24},{16,0},{24,8},{1,17},{9,25},{17,1},{25,9},{2,18},{10... | collective-permute-start | bytes 3145736 | tf_op jit(solution)/shard_map/ppermute | solution.py:91
  607.1 56.5 %collective-permute-start.46 = (bf16[256,2048]{1,0:T(8,128)(2,1)}, bf16[256,2048]{1,0:T(8,128)(2,1)}, u32[]{:S(2)}, u32[]{:S(2)}) collective-permute-start(bf16[256,2048]{1,0:T(8,128)(2,1)} %get-tuple-element.75), channel_id=1, source_target_pairs={{0,1},{1,0},{2,3},{3,2},{4,5},{5,4},{6,7},{7,6},{8,9},{9,8},{10,11... | collective-permute-start | bytes 3145736 | tf_op jit(solution)/shard_map/ppermute | solution.py:91
  614.6 15.4 %collective-permute-start.35 = (bf16[2,64,2048]{2,1,0:T(8,128)(2,1)}, bf16[2,64,2048]{2,1,0:T(8,128)(2,1)}, u32[]{:S(2)}, u32[]{:S(2)}) collective-permute-start(bf16[2,64,2048]{2,1,0:T(8,128)(2,1)} %fusion.57), channel_id=1, source_target_pairs={{0,8},{8,0},{16,24},{24,16},{1,9},{9,1},{17,25},{25,17},{2,10},{10... | collective-permute-start | bytes 1572872 | tf_op jit(solution)/shard_map/ppermute | solution.py:91
  614.7 176.6 %all-gather.17.cloned.1.call-start = ((), (), s32[]{:S(2)}) async-start(), calls=%async_computation.12 | async-start | bytes 2162688 | tf_op jit(solution)/shard_map/all_gather | solution.py:632
  628.7 9.2 %collective-permute-start.38 = (bf16[256,512]{1,0:T(8,128)(2,1)S(1)}, bf16[256,512]{1,0:T(8,128)(2,1)S(1)}, u32[]{:S(2)}, u32[]{:S(2)}) collective-permute-start(bf16[256,512]{1,0:T(8,128)(2,1)S(1)} %get-tuple-element.85), channel_id=1, source_target_pairs={{0,16},{8,24},{16,0},{24,8},{1,17},{9,25},{17,1},{25,9},{2,18},{10... | collective-permute-start | bytes 786440 | tf_op jit(solution)/shard_map/ppermute | solution.py:91
  629.8 33.5 %collective-permute-start.40 = (bf16[256,512]{1,0:T(8,128)(2,1)S(1)}, bf16[256,512]{1,0:T(8,128)(2,1)S(1)}, u32[]{:S(2)}, u32[]{:S(2)}) collective-permute-start(bf16[256,512]{1,0:T(8,128)(2,1)S(1)} %get-tuple-element.86), channel_id=1, source_target_pairs={{0,1},{1,0},{2,3},{3,2},{4,5},{5,4},{6,7},{7,6},{8,9},{9,8},{10,11... | collective-permute-start | bytes 786440 | tf_op jit(solution)/shard_map/ppermute | solution.py:91
  632.0 103.5 %collective-permute-start.36 = (bf16[64,2048]{1,0:T(8,128)(2,1)}, bf16[64,2048]{1,0:T(8,128)(2,1)}, u32[]{:S(2)}, u32[]{:S(2)}) collective-permute-start(bf16[64,2048]{1,0:T(8,128)(2,1)} %fusion.66), channel_id=1, source_target_pairs={{0,16},{8,24},{16,0},{24,8},{1,17},{9,25},{17,1},{25,9},{2,18},{10... | collective-permute-start | bytes 786440 | tf_op jit(solution)/shard_map/ppermute | solution.py:91
  663.5 9.6 %collective-permute-start.39 = (bf16[128,512]{1,0:T(8,128)(2,1)S(1)}, bf16[128,512]{1,0:T(8,128)(2,1)S(1)}, u32[]{:S(2)}, u32[]{:S(2)}) collective-permute-start(bf16[128,512]{1,0:T(8,128)(2,1)S(1)} %slice.796), channel_id=1, source_target_pairs={{0,1},{1,0},{2,3},{3,2},{4,5},{5,4},{6,7},{7,6},{8,9},{9,8},{10,11... | collective-permute-start | bytes 393224 | tf_op jit(solution)/shard_map/ppermute | solution.py:91
  668.1 27.2 %collective-permute-start.45 = (bf16[128,2048]{1,0:T(8,128)(2,1)}, bf16[128,2048]{1,0:T(8,128)(2,1)}, u32[]{:S(2)}, u32[]{:S(2)}) collective-permute-start(bf16[128,2048]{1,0:T(8,128)(2,1)} %slice.788), channel_id=1, source_target_pairs={{0,1},{1,0},{2,3},{3,2},{4,5},{5,4},{6,7},{7,6},{8,9},{9,8},{10,11... | collective-permute-start | bytes 1572872 | tf_op jit(solution)/shard_map/ppermute | solution.py:91
  671.0 34.0 %collective-permute-start.47 = (bf16[128,2048]{1,0:T(8,128)(2,1)}, bf16[128,2048]{1,0:T(8,128)(2,1)}, u32[]{:S(2)}, u32[]{:S(2)}) collective-permute-start(bf16[128,2048]{1,0:T(8,128)(2,1)} %slice.787), channel_id=1, source_target_pairs={{0,16},{8,24},{16,0},{24,8},{1,17},{9,25},{17,1},{25,9},{2,18},{10... | collective-permute-start | bytes 1572872 | tf_op jit(solution)/shard_map/ppermute | solution.py:91
  672.0 15.1 %collective-permute-start.41 = (bf16[128,512]{1,0:T(8,128)(2,1)S(1)}, bf16[128,512]{1,0:T(8,128)(2,1)S(1)}, u32[]{:S(2)}, u32[]{:S(2)}) collective-permute-start(bf16[128,512]{1,0:T(8,128)(2,1)S(1)} %slice.795), channel_id=1, source_target_pairs={{0,16},{8,24},{16,0},{24,8},{1,17},{9,25},{17,1},{25,9},{2,18},{10... | collective-permute-start | bytes 393224 | tf_op jit(solution)/shard_map/ppermute | solution.py:91
  711.9 27.0 %collective-permute-start.48 = (bf16[128,2048]{1,0:T(8,128)(2,1)}, bf16[128,2048]{1,0:T(8,128)(2,1)}, u32[]{:S(2)}, u32[]{:S(2)}) collective-permute-start(bf16[128,2048]{1,0:T(8,128)(2,1)} %slice.786), channel_id=1, source_target_pairs={{0,2},{1,3},{2,0},{3,1},{4,6},{5,7},{6,4},{7,5},{8,10},{9,11},{10,... | collective-permute-start | bytes 1572872 | tf_op jit(solution)/shard_map/ppermute | solution.py:91
  719.3 22.7 %collective-permute-start.61 = (f32[256,512]{0,1:T(8,128)S(1)}, f32[256,512]{0,1:T(8,128)S(1)}, u32[]{:S(2)}, u32[]{:S(2)}) collective-permute-start(f32[256,512]{0,1:T(8,128)S(1)} %pad_maximum_fusion.10), channel_id=1, source_target_pairs={{0,8},{8,0},{16,24},{24,16},{1,9},{9,1},{17,25},{25,17},{2,10},{10... | collective-permute-start | bytes 1572872 | tf_op jit(solution)/shard_map/ppermute | solution.py:91
  733.2 29.0 %collective-permute-start.63 = (f32[256,768]{1,0:T(8,128)}, f32[256,768]{1,0:T(8,128)}, u32[]{:S(2)}, u32[]{:S(2)}) collective-permute-start(f32[256,768]{1,0:T(8,128)} %constant_dynamic-update-slice_fusion.43), channel_id=1, source_target_pairs={{0,8},{8,0},{16,24},{24,16},{1,9},{9,1},{17,25},{25,17},{2,10},{10... | collective-permute-start | bytes 2359304 | tf_op jit(solution)/shard_map/ppermute | solution.py:91
  737.8 16.6 %collective-permute-start.57 = (f32[64,2048]{1,0:T(8,128)S(1)}, f32[64,2048]{1,0:T(8,128)S(1)}, u32[]{:S(2)}, u32[]{:S(2)}) collective-permute-start(f32[64,2048]{1,0:T(8,128)S(1)} %fusion.51), channel_id=1, source_target_pairs={{0,16},{8,24},{16,0},{24,8},{1,17},{9,25},{17,1},{25,9},{2,18},{10... | collective-permute-start | bytes 1572872 | tf_op jit(solution)/shard_map/ppermute | solution.py:91
  740.1 16.7 %collective-permute-start.49 = (bf16[64,2048]{1,0:T(8,128)(2,1)S(1)}, bf16[64,2048]{1,0:T(8,128)(2,1)S(1)}, u32[]{:S(2)}, u32[]{:S(2)}) collective-permute-start(bf16[64,2048]{1,0:T(8,128)(2,1)S(1)} %slice.792), channel_id=1, source_target_pairs={{0,4},{1,5},{2,6},{3,7},{4,0},{5,1},{6,2},{7,3},{8,12},{9,13},{10,... | collective-permute-start | bytes 786440 | tf_op jit(solution)/shard_map/ppermute | solution.py:91
  742.0 25.1 %collective-permute-start.62 = (bf16[256,512]{0,1:T(8,128)(2,1)S(1)}, bf16[256,512]{0,1:T(8,128)(2,1)}, u32[]{:S(2)}, u32[]{:S(2)}) collective-permute-start(bf16[256,512]{0,1:T(8,128)(2,1)S(1)} %add_convert_fusion.3), channel_id=1, source_target_pairs={{0,16},{8,24},{16,0},{24,8},{1,17},{9,25},{17,1},{25,9},{2,18},{10... | collective-permute-start | bytes 786440 | tf_op jit(solution)/shard_map/ppermute | solution.py:91
  755.6 44.6 %collective-permute-start.58 = (f32[2,64,2048]{2,1,0:T(8,128)}, f32[2,64,2048]{2,1,0:T(8,128)}, u32[]{:S(2)}, u32[]{:S(2)}) collective-permute-start(f32[2,64,2048]{2,1,0:T(8,128)} %maximum_select_fusion.4), channel_id=1, source_target_pairs={{0,8},{8,0},{16,24},{24,16},{1,9},{9,1},{17,25},{25,17},{2,10},{10... | collective-permute-start | bytes 3145736 | tf_op jit(solution)/shard_map/ppermute | solution.py:91
  771.6 16.7 %collective-permute-start.64 = (bf16[256,768]{1,0:T(8,128)(2,1)S(1)}, bf16[256,768]{1,0:T(8,128)(2,1)S(1)}, u32[]{:S(2)}, u32[]{:S(2)}) collective-permute-start(bf16[256,768]{1,0:T(8,128)(2,1)S(1)} %add_convert_fusion.2), channel_id=1, source_target_pairs={{0,16},{8,24},{16,0},{24,8},{1,17},{9,25},{17,1},{25,9},{2,18},{10... | collective-permute-start | bytes 1179656 | tf_op jit(solution)/shard_map/ppermute | solution.py:91
  776.0 11.3 %collective-permute-start.55 = (bf16[64,2048]{1,0:T(8,128)(2,1)S(1)}, bf16[64,2048]{1,0:T(8,128)(2,1)S(1)}, u32[]{:S(2)}, u32[]{:S(2)}) collective-permute-start(bf16[64,2048]{1,0:T(8,128)(2,1)S(1)} %fusion.118), channel_id=1, source_target_pairs={{0,16},{8,24},{16,0},{24,8},{1,17},{9,25},{17,1},{25,9},{2,18},{10... | collective-permute-start | bytes 786440 | tf_op jit(solution)/shard_map/ppermute | solution.py:91
  788.2 15.2 %collective-permute-start.56 = (bf16[2,64,2048]{2,1,0:T(8,128)(2,1)}, bf16[2,64,2048]{2,1,0:T(8,128)(2,1)}, u32[]{:S(2)}, u32[]{:S(2)}) collective-permute-start(bf16[2,64,2048]{2,1,0:T(8,128)(2,1)} %maximum_select_fusion.10), channel_id=1, source_target_pairs={{0,8},{8,0},{16,24},{24,16},{1,9},{9,1},{17,25},{25,17},{2,10},{10... | collective-permute-start | bytes 1572872 | tf_op jit(solution)/shard_map/ppermute | solution.py:91
  795.9 25.1 %all-to-all-start.6 = ((bf16[8,32,1536]{2,1,0:T(8,128)(2,1)}), bf16[8,32,1536]{2,1,0:T(8,128)(2,1)S(1)}, u32[]{:S(2)}, u32[]{:S(2)}) async-start(bf16[8,32,1536]{2,1,0:T(8,128)(2,1)} %bitcast.125), calls=%async_computation.6 | async-start | bytes 1572864 | tf_op jit(solution)/shard_map/all_to_all | solution.py:95
  (142 other events, 1652.8 us)
Sparse Core Ops, SparseCore 0:
  12.0 64.6 all-gather.6
  79.4 86.0 all-gather.8
  270.5 87.4 all-gather.10
  375.8 53.0 all-gather.12
  614.8 87.8 all-gather.14
  715.2 60.0 all-gather.16

commit v5 on v4

--- a/solution.py
+++ b/solution.py
@@ -520,7 +520,8 @@
     middle = tokens_own + scatter_mp(dot_cols(attended_b, o_full))
     normed2_b = rms_norm(middle, feedforward_norm_gain).astype(bf16)
 
-    normed2_far = gather_far(after(normed2_b, gate_down))
+    cotangent_rows = lax.optimization_barrier(cotangent_rows)
+    normed2_far = gather_far(after(normed2_b, gate_down, cotangent_rows))
     up_own = exchange(
         merge_blocks(
             after(current_loop, normed2_far),

time: 838 us -> 838 us (level)
  waiting for transfers between devices: 345 us -> 359 us
  starting transfers between devices: 106 us -> 97.2 us
    ppermute x65, waiting for transfers between devices: 272 us -> 281 us  [swap(): lax.ppermute(value, axis, [(place, place ^ bit) for place in range(count)])]
    slice x17 -> x18, local copies, waits for them, and re-layouts: 16.2 us -> 16.8 us  [after(): last = other[tuple((size - 1 for size in other.shape))]]
    unnamed x291 -> x287, local copies, waits for them, and re-layouts: 51.9 us -> 51.6 us
  transfers between devices with their start and end apart: 78 -> 78, of which waited for: 41 -> 39; matrix products, arithmetic and copies ran while one was open for 30% -> 29% of each run, Pallas kernels for 8% -> 8%
where the time goes in v5:
time: 838 us; the launch traced here: 830 us
  waiting for transfers between devices  359 us (43%)
  local copies, waits for them, and re-layouts  106 us (13%)
  starting transfers between devices  97.2 us (12%)
  other arithmetic  92.3 us (11%)
  matrix products  78.1 us (9%)
  Pallas kernels  65.6 us (8%)
  between operations  32.1 us (4%)
    ppermute x65, waiting for transfers between devices, swap(): lax.ppermute(value, axis, [(place, place ^ bit) for place in range(count)])  281 us
    all_to_all x7, waiting for transfers between devices, exchange(): return lax.all_to_all(blocks, 'dp', 0, 0, tiled=True)  64.6 us
    ppermute x65, starting transfers between devices, swap(): lax.ppermute(value, axis, [(place, place ^ bit) for place in range(count)])  63.7 us
    unnamed x287, local copies, waits for them, and re-layouts  51.6 us
    dot_general x14, matrix products, dot_rows(): lax.dot_general(left, right, (((0,), (0,)), ((), ())), preferred_element_...  39.7 us
    pallas_call x1, Pallas kernels, feed_forward(): pl.pallas_call(feed_kernel, out_shape=(jax.ShapeDtypeStruct((rows, pairs...  34.8 us
    all_to_all x7, starting transfers between devices, exchange(): return lax.all_to_all(blocks, 'dp', 0, 0, tiled=True)  32.7 us
    pallas_call x3, Pallas kernels, receive_grad(): pl.pallas_call(receive_kernel, out_shape=(jax.ShapeDtypeStruct((rows, pla...  16.8 us
  transfers between devices with their start and end apart: 78, of which 39 were waited for; matrix products, arithmetic and copies ran while one was open for 29% of the time, Pallas kernels for 8%

profile of v5, /device:TPU:0, one launch (start us, length us, event | category | flops | bytes accessed | tf_op | source)
XLA Modules:
  0.0 830.1 jit_solution(2335990183077819389)
XLA Ops:
  13.7 4.0 collective-permute-start.2
  21.4 8.9 %collective-permute-done.2 = bf16[64,2048]{1,0:T(8,128)(2,1)S(1)} collective-permute-done((bf16[64,2048]{1,0:T(8,128)(2,1)S(1)}, bf16[64,2048]{1,0:T(8,128)(2,1)S(1)}, u32[]{:S(2)}, u32[]{:S(2)}) %collective-permute-start.2) | collective-permute-done | bytes 262176 | tf_op jit(solution)/shard_map/ppermute | solution.py:91
  34.2 11.1 %collective-permute-done.5 = bf16[128,2048]{1,0:T(8,128)(2,1)} collective-permute-done((bf16[128,2048]{1,0:T(8,128)(2,1)}, bf16[128,2048]{1,0:T(8,128)(2,1)}, u32[]{:S(2)}, u32[]{:S(2)}) %collective-permute-start.5) | collective-permute-done | bytes 524320 | tf_op jit(solution)/shard_map/ppermute | solution.py:91
  49.6 10.7 %collective-permute-done.6 = bf16[128,2048]{1,0:T(8,128)(2,1)S(1)} collective-permute-done((bf16[128,2048]{1,0:T(8,128)(2,1)}, bf16[128,2048]{1,0:T(8,128)(2,1)S(1)}, u32[]{:S(2)}, u32[]{:S(2)}) %collective-permute-start.6) | collective-permute-done | bytes 524320 | tf_op jit(solution)/shard_map/ppermute | solution.py:91
  63.7 13.2 %all-gather.7.cloned.1.call-done = bf16[2048,512]{1,0:T(8,128)(2,1)} async-done(((bf16[64,512]{1,0:T(8,128)(2,1)}), bf16[2048,512]{1,0:T(8,128)(2,1)}) %all-gather.7.cloned.1.call-update) | async-done | bytes 2097168 | tf_op jit(solution)/shard_map/all_gather | solution.py:445
  80.8 5.4 collective-permute-done
  91.4 9.1 %collective-permute-done.1 = bf16[144,512]{1,0:T(8,128)(2,1)S(1)} collective-permute-done((bf16[144,512]{1,0:T(8,128)(2,1)S(1)}, bf16[144,512]{1,0:T(8,128)(2,1)S(1)}, u32[]{:S(2)}, u32[]{:S(2)}) %collective-permute-start.1) | collective-permute-done | bytes 147488 | tf_op jit(solution)/shard_map/ppermute | solution.py:91
  104.3 3.0 collective-permute-done.8
  111.8 3.7 collective-permute-done.9
  120.1 3.4 all-to-all-start
  131.7 8.5 %collective-permute-done.11 = bf16[288,512]{1,0:T(8,128)(2,1)S(1)} collective-permute-done((bf16[288,512]{1,0:T(8,128)(2,1)S(1)}, bf16[288,512]{1,0:T(8,128)(2,1)S(1)}, u32[]{:S(2)}, u32[]{:S(2)}) %collective-permute-start.11) | collective-permute-done | bytes 294944 | tf_op jit(solution)/shard_map/ppermute | solution.py:91
  144.1 7.5 shard_map.442
  151.7 4.9 all-to-all-start.1
  161.9 7.0 collective-permute-done.13
  174.9 3.2 fusion.170
  184.0 4.5 fusion.177
  188.5 3.3 convolution_convert_fusion.7
  203.3 3.9 collective-permute-done.16
  209.8 42.2 %all-to-all-done.1 = bf16[8,256,1024]{2,1,0:T(8,128)(2,1)} async-done(((bf16[8,256,1024]{2,1,0:T(8,128)(2,1)}), bf16[8,256,1024]{2,1,0:T(8,128)(2,1)}, u32[]{:S(2)}, u32[]{:S(2)}) %all-to-all-start.1) | async-done | bytes 4194336 | tf_op jit(solution)/shard_map/all_to_all | solution.py:95
  256.8 11.4 %collective-permute-done.17 = bf16[64,2048]{1,0:T(8,128)(2,1)S(1)} collective-permute-done((bf16[64,2048]{1,0:T(8,128)(2,1)S(1)}, bf16[64,2048]{1,0:T(8,128)(2,1)S(1)}, u32[]{:S(2)}, u32[]{:S(2)}) %collective-permute-start.17) | collective-permute-done | bytes 262176 | tf_op jit(solution)/shard_map/ppermute | solution.py:91
  270.5 14.2 %collective-permute-done.20 = bf16[128,2048]{1,0:T(8,128)(2,1)} collective-permute-done((bf16[128,2048]{1,0:T(8,128)(2,1)}, bf16[128,2048]{1,0:T(8,128)(2,1)}, u32[]{:S(2)}, u32[]{:S(2)}) %collective-permute-start.20) | collective-permute-done | bytes 524320 | tf_op jit(solution)/shard_map/ppermute | solution.py:91
  286.6 6.5 shard_map.443
  293.0 3.8 all-to-all-start.2
  300.3 27.9 %collective-permute-done.18 = bf16[128,2048]{1,0:T(8,128)(2,1)S(1)} collective-permute-done((bf16[128,2048]{1,0:T(8,128)(2,1)}, bf16[128,2048]{1,0:T(8,128)(2,1)S(1)}, u32[]{:S(2)}, u32[]{:S(2)}) %collective-permute-start.18) | collective-permute-done | bytes 524320 | tf_op jit(solution)/shard_map/ppermute | solution.py:91
  331.4 24.0 %collective-permute-done.19 = bf16[256,2048]{1,0:T(8,128)(2,1)S(1)} collective-permute-done((bf16[256,2048]{1,0:T(8,128)(2,1)S(1)}, bf16[256,2048]{1,0:T(8,128)(2,1)S(1)}, u32[]{:S(2)}, u32[]{:S(2)}) %collective-permute-start.19) | collective-permute-done | bytes 1048608 | tf_op jit(solution)/shard_map/ppermute | solution.py:91
  356.7 3.8 collective-permute-done.22
  375.6 34.8 %shard_map.444 = (bf16[1024,1024]{1,0:T(8,128)(2,1)}, bf16[1024,2048]{1,0:T(8,128)(2,1)}, f32[1024,2048]{1,0:T(8,128)}, bf16[1024,2048]{1,0:T(8,128)(2,1)}) custom-call(bf16[1024,2048]{1,0:T(8,128)(2,1)} %constant_dynamic-update-slice_fusion.28.normed_ref, bf16[1024,2048]{1,0:T(8,128)(2,1)} %copy-done.24, bf16[2048,1024]{1,0:T(8,128)(2,1)} %bitcast.46.refs_0_, ...), custom_call_target="tpu_custom_call" | custom-call | tf_op jit(solution)/shard_map/pallas_call | solution.py:351
  410.4 3.8 convolution_convert_fusion.1
  414.8 6.5 convolution_convert_fusion
  425.9 4.0 add_convert_fusion.1
  435.4 7.7 all-to-all-start.3
  443.2 6.1 collective-permute-done.25
  449.3 13.0 %collective-permute-done.27 = bf16[256,2048]{1,0:T(8,128)(2,1)} collective-permute-done((bf16[256,2048]{1,0:T(8,128)(2,1)}, bf16[256,2048]{1,0:T(8,128)(2,1)}, u32[]{:S(2)}, u32[]{:S(2)}) %collective-permute-start.27) | collective-permute-done | bytes 1048608 | tf_op jit(solution)/shard_map/ppermute | solution.py:91
  462.3 3.6 convert_add_fusion.1
  472.4 16.5 %collective-permute-done.26 = bf16[128,2048]{1,0:T(8,128)(2,1)S(1)} collective-permute-done((bf16[128,2048]{1,0:T(8,128)(2,1)S(1)}, bf16[128,2048]{1,0:T(8,128)(2,1)S(1)}, u32[]{:S(2)}, u32[]{:S(2)}) %collective-permute-start.26) | collective-permute-done | bytes 524320 | tf_op jit(solution)/shard_map/ppermute | solution.py:91
  491.2 6.6 add_convert_fusion
  497.8 2.8 convolution_convert_fusion.5
  505.2 6.4 collective-permute-start.31
  513.9 9.6 %collective-permute-done.31 = bf16[128,2048]{1,0:T(8,128)(2,1)S(1)} collective-permute-done((bf16[128,2048]{1,0:T(8,128)(2,1)S(1)}, bf16[128,2048]{1,0:T(8,128)(2,1)S(1)}, u32[]{:S(2)}, u32[]{:S(2)}) %collective-permute-start.31) | collective-permute-done | bytes 524320 | tf_op jit(solution)/shard_map/ppermute | solution.py:91
  523.8 2.7 convolution_convert_fusion.4
  526.5 11.3 %collective-permute-done.32 = bf16[64,2048]{1,0:T(8,128)(2,1)S(1)} collective-permute-done((bf16[64,2048]{1,0:T(8,128)(2,1)S(1)}, bf16[64,2048]{1,0:T(8,128)(2,1)S(1)}, u32[]{:S(2)}, u32[]{:S(2)}) %collective-permute-start.32) | collective-permute-done | bytes 262176 | tf_op jit(solution)/shard_map/ppermute | solution.py:91
  544.5 4.0 all-to-all-start.4
  552.4 4.7 all-to-all-done.4
  560.9 4.3 maximum_add_fusion
  565.3 4.6 all-to-all-start.5
  580.5 3.4 fusion.1
  589.4 5.3 convolution_bitcast_fusion
  600.5 4.1 fusion.161
  614.1 5.2 shard_map.447
  632.9 4.9 collective-permute-done.38
  637.8 25.0 %collective-permute-done.40 = bf16[256,512]{1,0:T(8,128)(2,1)S(1)} collective-permute-done((bf16[256,512]{1,0:T(8,128)(2,1)S(1)}, bf16[256,512]{1,0:T(8,128)(2,1)S(1)}, u32[]{:S(2)}, u32[]{:S(2)}) %collective-permute-start.40) | collective-permute-done | bytes 262176 | tf_op jit(solution)/shard_map/ppermute | solution.py:91
  673.3 13.4 %collective-permute-done.41 = bf16[128,512]{1,0:T(8,128)(2,1)S(1)} collective-permute-done((bf16[128,512]{1,0:T(8,128)(2,1)S(1)}, bf16[128,512]{1,0:T(8,128)(2,1)S(1)}, u32[]{:S(2)}, u32[]{:S(2)}) %collective-permute-start.41) | collective-permute-done | bytes 131104 | tf_op jit(solution)/shard_map/ppermute | solution.py:91
  687.4 4.7 all-to-all-done.5.arrived_ref
  697.7 4.1 collective-permute-done.42
  701.8 3.0 collective-permute-start.43
  715.0 2.7 fusion.43
  719.2 5.8 shard_map.445
  725.8 5.9 shard_map.446
  739.4 2.8 collective-permute-start.49
  742.8 11.5 %collective-permute-done.57 = f32[64,2048]{1,0:T(8,128)S(1)} collective-permute-done((f32[64,2048]{1,0:T(8,128)S(1)}, f32[64,2048]{1,0:T(8,128)S(1)}, u32[]{:S(2)}, u32[]{:S(2)}) %collective-permute-start.57) | collective-permute-done | bytes 524320 | tf_op jit(solution)/shard_map/ppermute | solution.py:91
  782.0 5.1 collective-permute-done.55
  791.1 3.2 fusion.178
  795.7 4.2 all-to-all-start.6
  807.7 13.0 %all-to-all-done.6 = bf16[8,32,1536]{2,1,0:T(8,128)(2,1)S(1)} async-done(((bf16[8,32,1536]{2,1,0:T(8,128)(2,1)}), bf16[8,32,1536]{2,1,0:T(8,128)(2,1)S(1)}, u32[]{:S(2)}, u32[]{:S(2)}) %all-to-all-start.6) | async-done | bytes 786464 | tf_op jit(solution)/shard_map/all_to_all | solution.py:95
  (613 shorter events, 268.7 us)
Async XLA Ops:
  7.2 69.6 %all-gather.7.cloned.1.call-start = ((), (), s32[]{:S(2)}) async-start(), calls=%async_computation.7 | async-start | bytes 2162688 | tf_op jit(solution)/shard_map/all_gather | solution.py:445
  11.9 168.5 %all-gather.9.cloned.1.call-start = ((), (), s32[]{:S(2)}) async-start(), calls=%async_computation.8 | async-start | bytes 4718592 | tf_op jit(solution)/shard_map/all_gather | solution.py:451
  13.7 16.6 %collective-permute-start.2 = (bf16[64,2048]{1,0:T(8,128)(2,1)S(1)}, bf16[64,2048]{1,0:T(8,128)(2,1)S(1)}, u32[]{:S(2)}, u32[]{:S(2)}) collective-permute-start(bf16[64,2048]{1,0:T(8,128)(2,1)S(1)} %get-tuple-element.65), channel_id=1, source_target_pairs={{0,4},{1,5},{2,6},{3,7},{4,0},{5,1},{6,2},{7,3},{8,12},{9,13},{10,... | collective-permute-start | bytes 786440 | tf_op jit(solution)/shard_map/ppermute | solution.py:91
  31.1 14.1 %collective-permute-start.5 = (bf16[128,2048]{1,0:T(8,128)(2,1)}, bf16[128,2048]{1,0:T(8,128)(2,1)}, u32[]{:S(2)}, u32[]{:S(2)}) collective-permute-start(bf16[128,2048]{1,0:T(8,128)(2,1)} %pad_maximum_fusion.7), channel_id=1, source_target_pairs={{0,2},{1,3},{2,0},{3,1},{4,6},{5,7},{6,4},{7,5},{8,10},{9,11},{10,... | collective-permute-start | bytes 1572872 | tf_op jit(solution)/shard_map/ppermute | solution.py:91
  32.6 14.5 %collective-permute-start.3 = (bf16[128,2048]{1,0:T(8,128)(2,1)}, bf16[128,2048]{1,0:T(8,128)(2,1)S(1)}, u32[]{:S(2)}, u32[]{:S(2)}) collective-permute-start(bf16[128,2048]{1,0:T(8,128)(2,1)} %pad_maximum_fusion.7), channel_id=1, source_target_pairs={{0,1},{1,0},{2,3},{3,2},{4,5},{5,4},{6,7},{7,6},{8,9},{9,8},{10,11... | collective-permute-start | bytes 1572872 | tf_op jit(solution)/shard_map/ppermute | solution.py:91
  45.3 15.1 %collective-permute-start.6 = (bf16[128,2048]{1,0:T(8,128)(2,1)}, bf16[128,2048]{1,0:T(8,128)(2,1)S(1)}, u32[]{:S(2)}, u32[]{:S(2)}) collective-permute-start(bf16[128,2048]{1,0:T(8,128)(2,1)} %collective-permute-done.5), channel_id=1, source_target_pairs={{0,16},{8,24},{16,0},{24,8},{1,17},{9,25},{17,1},{25,9},{2,18},{10... | collective-permute-start | bytes 1572872 | tf_op jit(solution)/shard_map/ppermute | solution.py:91
  48.2 39.3 %collective-permute-start.4 = (bf16[256,2048]{1,0:T(8,128)(2,1)}, bf16[256,2048]{1,0:T(8,128)(2,1)}, u32[]{:S(2)}, u32[]{:S(2)}) collective-permute-start(bf16[256,2048]{1,0:T(8,128)(2,1)} %pad_maximum_fusion.2), channel_id=1, source_target_pairs={{0,16},{8,24},{16,0},{24,8},{1,17},{9,25},{17,1},{25,9},{2,18},{10... | collective-permute-start | bytes 3145736 | tf_op jit(solution)/shard_map/ppermute | solution.py:91
  62.6 26.8 %collective-permute-start.7 = (bf16[256,2048]{1,0:T(8,128)(2,1)}, bf16[256,2048]{1,0:T(8,128)(2,1)}, u32[]{:S(2)}, u32[]{:S(2)}) collective-permute-start(bf16[256,2048]{1,0:T(8,128)(2,1)} %pad_maximum_fusion.3), channel_id=1, source_target_pairs={{0,1},{1,0},{2,3},{3,2},{4,5},{5,4},{6,7},{7,6},{8,9},{9,8},{10,11... | collective-permute-start | bytes 3145736 | tf_op jit(solution)/shard_map/ppermute | solution.py:91
  86.2 14.3 %collective-permute-start.1 = (bf16[144,512]{1,0:T(8,128)(2,1)S(1)}, bf16[144,512]{1,0:T(8,128)(2,1)S(1)}, u32[]{:S(2)}, u32[]{:S(2)}) collective-permute-start(bf16[144,512]{1,0:T(8,128)(2,1)S(1)} %pad_maximum_fusion.14), channel_id=1, source_target_pairs={{0,2},{1,3},{2,0},{3,1},{4,6},{5,7},{6,4},{7,5},{8,10},{9,11},{10,... | collective-permute-start | bytes 442376 | tf_op jit(solution)/shard_map/ppermute | solution.py:91
  120.1 31.5 %all-to-all-start = ((bf16[8,64,256]{2,1,0:T(8,128)(2,1)}), bf16[8,64,256]{2,1,0:T(8,128)(2,1)S(1)}, u32[]{:S(2)}, u32[]{:S(2)}) async-start(bf16[8,64,256]{2,1,0:T(8,128)(2,1)} %constant_dynamic-update-slice_fusion.13), calls=%async_computation | async-start | bytes 524288 | tf_op jit(solution)/shard_map/all_to_all | solution.py:95
  125.2 15.0 %collective-permute-start.11 = (bf16[288,512]{1,0:T(8,128)(2,1)S(1)}, bf16[288,512]{1,0:T(8,128)(2,1)S(1)}, u32[]{:S(2)}, u32[]{:S(2)}) collective-permute-start(bf16[288,512]{1,0:T(8,128)(2,1)S(1)} %pad_maximum_fusion.13), channel_id=1, source_target_pairs={{0,1},{1,0},{2,3},{3,2},{4,5},{5,4},{6,7},{7,6},{8,9},{9,8},{10,11... | collective-permute-start | bytes 884744 | tf_op jit(solution)/shard_map/ppermute | solution.py:91
  151.7 100.3 %all-to-all-start.1 = ((bf16[8,256,1024]{2,1,0:T(8,128)(2,1)}), bf16[8,256,1024]{2,1,0:T(8,128)(2,1)}, u32[]{:S(2)}, u32[]{:S(2)}) async-start(bf16[8,256,1024]{2,1,0:T(8,128)(2,1)} %shard_map.442), calls=%async_computation.1 | async-start | bytes 8388608 | tf_op jit(solution)/shard_map/all_to_all | solution.py:95
  156.6 214.4 %all-gather.11.cloned.1.call-start = ((), (), s32[]{:S(2)}) async-start(), calls=%async_computation.9 | async-start | bytes 3244032 | tf_op jit(solution)/shard_map/all_gather | solution.py:534
  160.0 12.8 %collective-permute-start.12 = (bf16[1152,512]{1,0:T(8,128)(2,1)}, bf16[1152,512]{1,0:T(8,128)(2,1)S(1)}, u32[]{:S(2)}, u32[]{:S(2)}) collective-permute-start(bf16[1152,512]{1,0:T(8,128)(2,1)} %get-tuple-element.98), channel_id=1, source_target_pairs={{0,8},{8,0},{16,24},{24,16},{1,9},{9,1},{17,25},{25,17},{2,10},{10... | collective-permute-start | bytes 3538952 | tf_op jit(solution)/shard_map/ppermute | solution.py:91
  160.0 8.8 %collective-permute-start.13 = (bf16[512,256]{1,0:T(8,128)(2,1)S(1)}, bf16[512,256]{1,0:T(8,128)(2,1)S(1)}, u32[]{:S(2)}, u32[]{:S(2)}) collective-permute-start(bf16[512,256]{1,0:T(8,128)(2,1)S(1)} %bitcast.322), channel_id=1, source_target_pairs={{0,16},{8,24},{16,0},{24,8},{1,17},{9,25},{17,1},{25,9},{2,18},{10... | collective-permute-start | bytes 786440 | tf_op jit(solution)/shard_map/ppermute | solution.py:91
  198.7 8.6 %collective-permute-start.16 = (bf16[64,2048]{1,0:T(8,128)(2,1)S(1)}, bf16[64,2048]{1,0:T(8,128)(2,1)S(1)}, u32[]{:S(2)}, u32[]{:S(2)}) collective-permute-start(bf16[64,2048]{1,0:T(8,128)(2,1)S(1)} %fusion.64), channel_id=1, source_target_pairs={{0,16},{8,24},{16,0},{24,8},{1,17},{9,25},{17,1},{25,9},{2,18},{10... | collective-permute-start | bytes 786440 | tf_op jit(solution)/shard_map/ppermute | solution.py:91
  255.8 12.5 %collective-permute-start.17 = (bf16[64,2048]{1,0:T(8,128)(2,1)S(1)}, bf16[64,2048]{1,0:T(8,128)(2,1)S(1)}, u32[]{:S(2)}, u32[]{:S(2)}) collective-permute-start(bf16[64,2048]{1,0:T(8,128)(2,1)S(1)} %get-tuple-element.63), channel_id=1, source_target_pairs={{0,4},{1,5},{2,6},{3,7},{4,0},{5,1},{6,2},{7,3},{8,12},{9,13},{10,... | collective-permute-start | bytes 786440 | tf_op jit(solution)/shard_map/ppermute | solution.py:91
  269.8 14.9 %collective-permute-start.20 = (bf16[128,2048]{1,0:T(8,128)(2,1)}, bf16[128,2048]{1,0:T(8,128)(2,1)}, u32[]{:S(2)}, u32[]{:S(2)}) collective-permute-start(bf16[128,2048]{1,0:T(8,128)(2,1)} %pad_maximum_fusion.9), channel_id=1, source_target_pairs={{0,2},{1,3},{2,0},{3,1},{4,6},{5,7},{6,4},{7,5},{8,10},{9,11},{10,... | collective-permute-start | bytes 1572872 | tf_op jit(solution)/shard_map/ppermute | solution.py:91
  293.0 68.9 %all-to-all-start.2 = ((bf16[8,256,512]{2,1,0:T(8,128)(2,1)}), bf16[8,256,512]{2,1,0:T(8,128)(2,1)S(1)}, u32[]{:S(2)}, u32[]{:S(2)}) async-start(bf16[8,256,512]{2,1,0:T(8,128)(2,1)} %shard_map.443), calls=%async_computation.2 | async-start | bytes 4194304 | tf_op jit(solution)/shard_map/all_to_all | solution.py:95
  296.8 133.1 %all-gather.13.cloned.1.call-start = ((), (), s32[]{:S(2)}) async-start(), calls=%async_computation.10 | async-start | bytes 2359296 | tf_op jit(solution)/shard_map/all_gather | solution.py:538
  296.9 31.4 %collective-permute-start.18 = (bf16[128,2048]{1,0:T(8,128)(2,1)}, bf16[128,2048]{1,0:T(8,128)(2,1)S(1)}, u32[]{:S(2)}, u32[]{:S(2)}) collective-permute-start(bf16[128,2048]{1,0:T(8,128)(2,1)} %pad_maximum_fusion.9), channel_id=1, source_target_pairs={{0,1},{1,0},{2,3},{3,2},{4,5},{5,4},{6,7},{7,6},{8,9},{9,8},{10,11... | collective-permute-start | bytes 1572872 | tf_op jit(solution)/shard_map/ppermute | solution.py:91
  298.9 30.9 %collective-permute-start.21 = (bf16[128,2048]{1,0:T(8,128)(2,1)}, bf16[128,2048]{1,0:T(8,128)(2,1)S(1)}, u32[]{:S(2)}, u32[]{:S(2)}) collective-permute-start(bf16[128,2048]{1,0:T(8,128)(2,1)} %collective-permute-done.20), channel_id=1, source_target_pairs={{0,16},{8,24},{16,0},{24,8},{1,17},{9,25},{17,1},{25,9},{2,18},{10... | collective-permute-start | bytes 1572872 | tf_op jit(solution)/shard_map/ppermute | solution.py:91
  300.3 75.2 %collective-permute-start.23 = (bf16[2048,1024]{1,0:T(8,128)(2,1)}, bf16[2048,1024]{1,0:T(8,128)(2,1)}, u32[]{:S(2)}, u32[]{:S(2)}) collective-permute-start(bf16[2048,1024]{1,0:T(8,128)(2,1)} %bitcast.46.refs_0_), channel_id=1, source_target_pairs={{0,8},{8,0},{16,24},{24,16},{1,9},{9,1},{17,25},{25,17},{2,10},{10... | collective-permute-start | bytes 12582920 | tf_op jit(solution)/shard_map/ppermute | solution.py:91
  328.4 27.0 %collective-permute-start.19 = (bf16[256,2048]{1,0:T(8,128)(2,1)S(1)}, bf16[256,2048]{1,0:T(8,128)(2,1)S(1)}, u32[]{:S(2)}, u32[]{:S(2)}) collective-permute-start(bf16[256,2048]{1,0:T(8,128)(2,1)S(1)} %pad_maximum_fusion.4), channel_id=1, source_target_pairs={{0,16},{8,24},{16,0},{24,8},{1,17},{9,25},{17,1},{25,9},{2,18},{10... | collective-permute-start | bytes 3145736 | tf_op jit(solution)/shard_map/ppermute | solution.py:91
  331.1 29.4 %collective-permute-start.22 = (bf16[256,2048]{1,0:T(8,128)(2,1)S(1)}, bf16[256,2048]{1,0:T(8,128)(2,1)S(1)}, u32[]{:S(2)}, u32[]{:S(2)}) collective-permute-start(bf16[256,2048]{1,0:T(8,128)(2,1)S(1)} %pad_maximum_fusion.5), channel_id=1, source_target_pairs={{0,1},{1,0},{2,3},{3,2},{4,5},{5,4},{6,7},{7,6},{8,9},{9,8},{10,11... | collective-permute-start | bytes 3145736 | tf_op jit(solution)/shard_map/ppermute | solution.py:91
  363.9 11.6 %collective-permute-start.24 = (bf16[2048,512]{1,0:T(8,128)(2,1)}, bf16[2048,512]{1,0:T(8,128)(2,1)}, u32[]{:S(2)}, u32[]{:S(2)}) collective-permute-start(bf16[2048,512]{1,0:T(8,128)(2,1)} %broadcast_add_fusion.1), channel_id=1, source_target_pairs={{0,8},{8,0},{16,24},{24,16},{1,9},{9,1},{17,25},{25,17},{2,10},{10... | collective-permute-start | bytes 6291464 | tf_op jit(solution)/shard_map/ppermute | solution.py:91
  414.1 11.7 %collective-permute-start.29 = (bf16[2048,512]{1,0:T(8,128)(2,1)S(1)}, bf16[2048,512]{1,0:T(8,128)(2,1)}, u32[]{:S(2)}, u32[]{:S(2)}) collective-permute-start(bf16[2048,512]{1,0:T(8,128)(2,1)S(1)} %convolution_convert_fusion.1), channel_id=1, source_target_pairs={{0,8},{8,0},{16,24},{24,16},{1,9},{9,1},{17,25},{25,17},{2,10},{10... | collective-permute-start | bytes 6291464 | tf_op jit(solution)/shard_map/ppermute | solution.py:91
  421.2 70.0 %collective-permute-start.30 = (bf16[2048,1024]{1,0:T(8,128)(2,1)}, bf16[2048,1024]{1,0:T(8,128)(2,1)}, u32[]{:S(2)}, u32[]{:S(2)}) collective-permute-start(bf16[2048,1024]{1,0:T(8,128)(2,1)} %convolution_convert_fusion), channel_id=1, source_target_pairs={{0,8},{8,0},{16,24},{24,16},{1,9},{9,1},{17,25},{25,17},{2,10},{10... | collective-permute-start | bytes 12582920 | tf_op jit(solution)/shard_map/ppermute | solution.py:91
  423.5 25.9 %collective-permute-start.25 = (bf16[256,2048]{1,0:T(8,128)(2,1)}, bf16[256,2048]{1,0:T(8,128)(2,1)}, u32[]{:S(2)}, u32[]{:S(2)}) collective-permute-start(bf16[256,2048]{1,0:T(8,128)(2,1)} %get-tuple-element.78), channel_id=1, source_target_pairs={{0,16},{8,24},{16,0},{24,8},{1,17},{9,25},{17,1},{25,9},{2,18},{10... | collective-permute-start | bytes 3145736 | tf_op jit(solution)/shard_map/ppermute | solution.py:91
  425.0 37.4 %collective-permute-start.27 = (bf16[256,2048]{1,0:T(8,128)(2,1)}, bf16[256,2048]{1,0:T(8,128)(2,1)}, u32[]{:S(2)}, u32[]{:S(2)}) collective-permute-start(bf16[256,2048]{1,0:T(8,128)(2,1)} %get-tuple-element.79), channel_id=1, source_target_pairs={{0,1},{1,0},{2,3},{3,2},{4,5},{5,4},{6,7},{7,6},{8,9},{9,8},{10,11... | collective-permute-start | bytes 3145736 | tf_op jit(solution)/shard_map/ppermute | solution.py:91
  435.4 66.5 %all-to-all-start.3 = ((bf16[8,288,512]{2,1,0:T(8,128)(2,1)}), bf16[8,288,512]{2,1,0:T(8,128)(2,1)S(1)}, u32[]{:S(2)}, u32[]{:S(2)}) async-start(bf16[8,288,512]{2,1,0:T(8,128)(2,1)} %pad_maximum_fusion), calls=%async_computation.3 | async-start | bytes 4718592 | tf_op jit(solution)/shard_map/all_to_all | solution.py:95
  466.0 23.0 %collective-permute-start.26 = (bf16[128,2048]{1,0:T(8,128)(2,1)S(1)}, bf16[128,2048]{1,0:T(8,128)(2,1)S(1)}, u32[]{:S(2)}, u32[]{:S(2)}) collective-permute-start(bf16[128,2048]{1,0:T(8,128)(2,1)S(1)} %slice.796), channel_id=1, source_target_pairs={{0,1},{1,0},{2,3},{3,2},{4,5},{5,4},{6,7},{7,6},{8,9},{9,8},{10,11... | collective-permute-start | bytes 1572872 | tf_op jit(solution)/shard_map/ppermute | solution.py:91
  471.5 18.6 %collective-permute-start.28 = (bf16[128,2048]{1,0:T(8,128)(2,1)S(1)}, bf16[128,2048]{1,0:T(8,128)(2,1)S(1)}, u32[]{:S(2)}, u32[]{:S(2)}) collective-permute-start(bf16[128,2048]{1,0:T(8,128)(2,1)S(1)} %slice.795), channel_id=1, source_target_pairs={{0,16},{8,24},{16,0},{24,8},{1,17},{9,25},{17,1},{25,9},{2,18},{10... | collective-permute-start | bytes 1572872 | tf_op jit(solution)/shard_map/ppermute | solution.py:91
  505.2 18.3 %collective-permute-start.31 = (bf16[128,2048]{1,0:T(8,128)(2,1)S(1)}, bf16[128,2048]{1,0:T(8,128)(2,1)S(1)}, u32[]{:S(2)}, u32[]{:S(2)}) collective-permute-start(bf16[128,2048]{1,0:T(8,128)(2,1)S(1)} %slice.794), channel_id=1, source_target_pairs={{0,2},{1,3},{2,0},{3,1},{4,6},{5,7},{6,4},{7,5},{8,10},{9,11},{10,... | collective-permute-start | bytes 1572872 | tf_op jit(solution)/shard_map/ppermute | solution.py:91
  523.7 14.1 %collective-permute-start.32 = (bf16[64,2048]{1,0:T(8,128)(2,1)S(1)}, bf16[64,2048]{1,0:T(8,128)(2,1)S(1)}, u32[]{:S(2)}, u32[]{:S(2)}) collective-permute-start(bf16[64,2048]{1,0:T(8,128)(2,1)S(1)} %slice.798), channel_id=1, source_target_pairs={{0,4},{1,5},{2,6},{3,7},{4,0},{5,1},{6,2},{7,3},{8,12},{9,13},{10,... | collective-permute-start | bytes 786440 | tf_op jit(solution)/shard_map/ppermute | solution.py:91
  544.5 12.6 %all-to-all-start.4 = ((bf16[8,64,256]{2,1,0:T(8,128)(2,1)}), bf16[8,64,256]{2,1,0:T(8,128)(2,1)}, u32[]{:S(2)}, u32[]{:S(2)}) async-start(bf16[8,64,256]{2,1,0:T(8,128)(2,1)} %constant_dynamic-update-slice_fusion.35), calls=%async_computation.4 | async-start | bytes 524288 | tf_op jit(solution)/shard_map/all_to_all | solution.py:95
  550.5 23.5 %collective-permute-start.34 = (bf16[2,64,2048]{2,1,0:T(8,128)(2,1)}, bf16[2,64,2048]{2,1,0:T(8,128)(2,1)}, u32[]{:S(2)}, u32[]{:S(2)}) collective-permute-start(bf16[2,64,2048]{2,1,0:T(8,128)(2,1)} %maximum_select_fusion.8), channel_id=1, source_target_pairs={{0,8},{8,0},{16,24},{24,16},{1,9},{9,1},{17,25},{25,17},{2,10},{10... | collective-permute-start | bytes 1572872 | tf_op jit(solution)/shard_map/ppermute | solution.py:91
  559.0 11.1 %collective-permute-start.59 = (bf16[512,256]{1,0:T(8,128)(2,1)}, bf16[512,256]{1,0:T(8,128)(2,1)S(1)}, u32[]{:S(2)}, u32[]{:S(2)}) collective-permute-start(bf16[512,256]{1,0:T(8,128)(2,1)} %bitcast.114), channel_id=1, source_target_pairs={{0,16},{8,24},{16,0},{24,8},{1,17},{9,25},{17,1},{25,9},{2,18},{10... | collective-permute-start | bytes 786440 | tf_op jit(solution)/shard_map/ppermute | solution.py:91
  565.3 126.8 %all-to-all-start.5 = ((bf16[8,576,512]{2,1,0:T(8,128)(2,1)}), bf16[8,576,512]{2,1,0:T(8,128)(2,1)}, u32[]{:S(2)}, u32[]{:S(2)}) async-start(bf16[8,576,512]{2,1,0:T(8,128)(2,1)} %maximum_add_fusion), calls=%async_computation.5 | async-start | bytes 9437184 | tf_op jit(solution)/shard_map/all_to_all | solution.py:95
  569.9 145.1 %all-gather.15.cloned.1.call-start = ((), (), s32[]{:S(2)}) async-start(), calls=%async_computation.11 | async-start | bytes 2359296 | tf_op jit(solution)/shard_map/all_gather | solution.py:603
  572.1 47.1 %collective-permute-start.60 = (bf16[2,512,256]{2,1,0:T(8,128)(2,1)}, bf16[2,512,256]{2,1,0:T(8,128)(2,1)}, u32[]{:S(2)}, u32[]{:S(2)}) collective-permute-start(bf16[2,512,256]{2,1,0:T(8,128)(2,1)} %maximum_select_fusion.12), channel_id=1, source_target_pairs={{0,8},{8,0},{16,24},{24,16},{1,9},{9,1},{17,25},{25,17},{2,10},{10... | collective-permute-start | bytes 1572872 | tf_op jit(solution)/shard_map/ppermute | solution.py:91
  598.8 27.1 %collective-permute-start.37 = (bf16[1024,512]{1,0:T(8,128)(2,1)}, bf16[1024,512]{1,0:T(8,128)(2,1)}, u32[]{:S(2)}, u32[]{:S(2)}) collective-permute-start(bf16[1024,512]{1,0:T(8,128)(2,1)} %fusion.11), channel_id=1, source_target_pairs={{0,8},{8,0},{16,24},{24,16},{1,9},{9,1},{17,25},{25,17},{2,10},{10... | collective-permute-start | bytes 3145736 | tf_op jit(solution)/shard_map/ppermute | solution.py:91
  606.0 57.1 %collective-permute-start.44 = (bf16[256,2048]{1,0:T(8,128)(2,1)}, bf16[256,2048]{1,0:T(8,128)(2,1)}, u32[]{:S(2)}, u32[]{:S(2)}) collective-permute-start(bf16[256,2048]{1,0:T(8,128)(2,1)} %get-tuple-element.74), channel_id=1, source_target_pairs={{0,16},{8,24},{16,0},{24,8},{1,17},{9,25},{17,1},{25,9},{2,18},{10... | collective-permute-start | bytes 3145736 | tf_op jit(solution)/shard_map/ppermute | solution.py:91
  606.2 56.9 %collective-permute-start.46 = (bf16[256,2048]{1,0:T(8,128)(2,1)}, bf16[256,2048]{1,0:T(8,128)(2,1)}, u32[]{:S(2)}, u32[]{:S(2)}) collective-permute-start(bf16[256,2048]{1,0:T(8,128)(2,1)} %get-tuple-element.75), channel_id=1, source_target_pairs={{0,1},{1,0},{2,3},{3,2},{4,5},{5,4},{6,7},{7,6},{8,9},{9,8},{10,11... | collective-permute-start | bytes 3145736 | tf_op jit(solution)/shard_map/ppermute | solution.py:91
  613.7 16.3 %collective-permute-start.35 = (bf16[2,64,2048]{2,1,0:T(8,128)(2,1)}, bf16[2,64,2048]{2,1,0:T(8,128)(2,1)}, u32[]{:S(2)}, u32[]{:S(2)}) collective-permute-start(bf16[2,64,2048]{2,1,0:T(8,128)(2,1)} %fusion.57), channel_id=1, source_target_pairs={{0,8},{8,0},{16,24},{24,16},{1,9},{9,1},{17,25},{25,17},{2,10},{10... | collective-permute-start | bytes 1572872 | tf_op jit(solution)/shard_map/ppermute | solution.py:91
  613.7 177.3 %all-gather.17.cloned.1.call-start = ((), (), s32[]{:S(2)}) async-start(), calls=%async_computation.12 | async-start | bytes 2162688 | tf_op jit(solution)/shard_map/all_gather | solution.py:633
  627.9 9.9 %collective-permute-start.38 = (bf16[256,512]{1,0:T(8,128)(2,1)S(1)}, bf16[256,512]{1,0:T(8,128)(2,1)S(1)}, u32[]{:S(2)}, u32[]{:S(2)}) collective-permute-start(bf16[256,512]{1,0:T(8,128)(2,1)S(1)} %get-tuple-element.85), channel_id=1, source_target_pairs={{0,16},{8,24},{16,0},{24,8},{1,17},{9,25},{17,1},{25,9},{2,18},{10... | collective-permute-start | bytes 786440 | tf_op jit(solution)/shard_map/ppermute | solution.py:91
  629.8 33.0 %collective-permute-start.40 = (bf16[256,512]{1,0:T(8,128)(2,1)S(1)}, bf16[256,512]{1,0:T(8,128)(2,1)S(1)}, u32[]{:S(2)}, u32[]{:S(2)}) collective-permute-start(bf16[256,512]{1,0:T(8,128)(2,1)S(1)} %get-tuple-element.86), channel_id=1, source_target_pairs={{0,1},{1,0},{2,3},{3,2},{4,5},{5,4},{6,7},{7,6},{8,9},{9,8},{10,11... | collective-permute-start | bytes 786440 | tf_op jit(solution)/shard_map/ppermute | solution.py:91
  631.9 103.5 %collective-permute-start.36 = (bf16[64,2048]{1,0:T(8,128)(2,1)}, bf16[64,2048]{1,0:T(8,128)(2,1)}, u32[]{:S(2)}, u32[]{:S(2)}) collective-permute-start(bf16[64,2048]{1,0:T(8,128)(2,1)} %fusion.66), channel_id=1, source_target_pairs={{0,16},{8,24},{16,0},{24,8},{1,17},{9,25},{17,1},{25,9},{2,18},{10... | collective-permute-start | bytes 786440 | tf_op jit(solution)/shard_map/ppermute | solution.py:91
  663.0 9.6 %collective-permute-start.39 = (bf16[128,512]{1,0:T(8,128)(2,1)S(1)}, bf16[128,512]{1,0:T(8,128)(2,1)S(1)}, u32[]{:S(2)}, u32[]{:S(2)}) collective-permute-start(bf16[128,512]{1,0:T(8,128)(2,1)S(1)} %slice.801), channel_id=1, source_target_pairs={{0,1},{1,0},{2,3},{3,2},{4,5},{5,4},{6,7},{7,6},{8,9},{9,8},{10,11... | collective-permute-start | bytes 393224 | tf_op jit(solution)/shard_map/ppermute | solution.py:91
  667.6 27.6 %collective-permute-start.45 = (bf16[128,2048]{1,0:T(8,128)(2,1)}, bf16[128,2048]{1,0:T(8,128)(2,1)}, u32[]{:S(2)}, u32[]{:S(2)}) collective-permute-start(bf16[128,2048]{1,0:T(8,128)(2,1)} %slice.793), channel_id=1, source_target_pairs={{0,1},{1,0},{2,3},{3,2},{4,5},{5,4},{6,7},{7,6},{8,9},{9,8},{10,11... | collective-permute-start | bytes 1572872 | tf_op jit(solution)/shard_map/ppermute | solution.py:91
  670.4 34.4 %collective-permute-start.47 = (bf16[128,2048]{1,0:T(8,128)(2,1)}, bf16[128,2048]{1,0:T(8,128)(2,1)}, u32[]{:S(2)}, u32[]{:S(2)}) collective-permute-start(bf16[128,2048]{1,0:T(8,128)(2,1)} %slice.792), channel_id=1, source_target_pairs={{0,16},{8,24},{16,0},{24,8},{1,17},{9,25},{17,1},{25,9},{2,18},{10... | collective-permute-start | bytes 1572872 | tf_op jit(solution)/shard_map/ppermute | solution.py:91
  671.6 15.1 %collective-permute-start.41 = (bf16[128,512]{1,0:T(8,128)(2,1)S(1)}, bf16[128,512]{1,0:T(8,128)(2,1)S(1)}, u32[]{:S(2)}, u32[]{:S(2)}) collective-permute-start(bf16[128,512]{1,0:T(8,128)(2,1)S(1)} %slice.800), channel_id=1, source_target_pairs={{0,16},{8,24},{16,0},{24,8},{1,17},{9,25},{17,1},{25,9},{2,18},{10... | collective-permute-start | bytes 393224 | tf_op jit(solution)/shard_map/ppermute | solution.py:91
  711.7 26.4 %collective-permute-start.48 = (bf16[128,2048]{1,0:T(8,128)(2,1)}, bf16[128,2048]{1,0:T(8,128)(2,1)}, u32[]{:S(2)}, u32[]{:S(2)}) collective-permute-start(bf16[128,2048]{1,0:T(8,128)(2,1)} %slice.791), channel_id=1, source_target_pairs={{0,2},{1,3},{2,0},{3,1},{4,6},{5,7},{6,4},{7,5},{8,10},{9,11},{10,... | collective-permute-start | bytes 1572872 | tf_op jit(solution)/shard_map/ppermute | solution.py:91
  719.2 23.0 %collective-permute-start.61 = (f32[256,512]{0,1:T(8,128)S(1)}, f32[256,512]{0,1:T(8,128)S(1)}, u32[]{:S(2)}, u32[]{:S(2)}) collective-permute-start(f32[256,512]{0,1:T(8,128)S(1)} %pad_maximum_fusion.10), channel_id=1, source_target_pairs={{0,8},{8,0},{16,24},{24,16},{1,9},{9,1},{17,25},{25,17},{2,10},{10... | collective-permute-start | bytes 1572872 | tf_op jit(solution)/shard_map/ppermute | solution.py:91
  733.1 29.0 %collective-permute-start.63 = (f32[256,768]{1,0:T(8,128)}, f32[256,768]{1,0:T(8,128)}, u32[]{:S(2)}, u32[]{:S(2)}) collective-permute-start(f32[256,768]{1,0:T(8,128)} %constant_dynamic-update-slice_fusion.43), channel_id=1, source_target_pairs={{0,8},{8,0},{16,24},{24,16},{1,9},{9,1},{17,25},{25,17},{2,10},{10... | collective-permute-start | bytes 2359304 | tf_op jit(solution)/shard_map/ppermute | solution.py:91
  737.7 16.6 %collective-permute-start.57 = (f32[64,2048]{1,0:T(8,128)S(1)}, f32[64,2048]{1,0:T(8,128)S(1)}, u32[]{:S(2)}, u32[]{:S(2)}) collective-permute-start(f32[64,2048]{1,0:T(8,128)S(1)} %fusion.51), channel_id=1, source_target_pairs={{0,16},{8,24},{16,0},{24,8},{1,17},{9,25},{17,1},{25,9},{2,18},{10... | collective-permute-start | bytes 1572872 | tf_op jit(solution)/shard_map/ppermute | solution.py:91
  739.4 16.9 %collective-permute-start.49 = (bf16[64,2048]{1,0:T(8,128)(2,1)S(1)}, bf16[64,2048]{1,0:T(8,128)(2,1)S(1)}, u32[]{:S(2)}, u32[]{:S(2)}) collective-permute-start(bf16[64,2048]{1,0:T(8,128)(2,1)S(1)} %slice.797), channel_id=1, source_target_pairs={{0,4},{1,5},{2,6},{3,7},{4,0},{5,1},{6,2},{7,3},{8,12},{9,13},{10,... | collective-permute-start | bytes 786440 | tf_op jit(solution)/shard_map/ppermute | solution.py:91
  742.2 24.7 %collective-permute-start.62 = (bf16[256,512]{0,1:T(8,128)(2,1)S(1)}, bf16[256,512]{0,1:T(8,128)(2,1)}, u32[]{:S(2)}, u32[]{:S(2)}) collective-permute-start(bf16[256,512]{0,1:T(8,128)(2,1)S(1)} %add_convert_fusion.3), channel_id=1, source_target_pairs={{0,16},{8,24},{16,0},{24,8},{1,17},{9,25},{17,1},{25,9},{2,18},{10... | collective-permute-start | bytes 786440 | tf_op jit(solution)/shard_map/ppermute | solution.py:91
  755.4 44.5 %collective-permute-start.58 = (f32[2,64,2048]{2,1,0:T(8,128)}, f32[2,64,2048]{2,1,0:T(8,128)}, u32[]{:S(2)}, u32[]{:S(2)}) collective-permute-start(f32[2,64,2048]{2,1,0:T(8,128)} %maximum_select_fusion.4), channel_id=1, source_target_pairs={{0,8},{8,0},{16,24},{24,16},{1,9},{9,1},{17,25},{25,17},{2,10},{10... | collective-permute-start | bytes 3145736 | tf_op jit(solution)/shard_map/ppermute | solution.py:91
  771.1 17.0 %collective-permute-start.64 = (bf16[256,768]{1,0:T(8,128)(2,1)S(1)}, bf16[256,768]{1,0:T(8,128)(2,1)S(1)}, u32[]{:S(2)}, u32[]{:S(2)}) collective-permute-start(bf16[256,768]{1,0:T(8,128)(2,1)S(1)} %add_convert_fusion.2), channel_id=1, source_target_pairs={{0,16},{8,24},{16,0},{24,8},{1,17},{9,25},{17,1},{25,9},{2,18},{10... | collective-permute-start | bytes 1179656 | tf_op jit(solution)/shard_map/ppermute | solution.py:91
  775.9 11.2 %collective-permute-start.55 = (bf16[64,2048]{1,0:T(8,128)(2,1)S(1)}, bf16[64,2048]{1,0:T(8,128)(2,1)S(1)}, u32[]{:S(2)}, u32[]{:S(2)}) collective-permute-start(bf16[64,2048]{1,0:T(8,128)(2,1)S(1)} %fusion.118), channel_id=1, source_target_pairs={{0,16},{8,24},{16,0},{24,8},{1,17},{9,25},{17,1},{25,9},{2,18},{10... | collective-permute-start | bytes 786440 | tf_op jit(solution)/shard_map/ppermute | solution.py:91
  788.0 15.2 %collective-permute-start.56 = (bf16[2,64,2048]{2,1,0:T(8,128)(2,1)}, bf16[2,64,2048]{2,1,0:T(8,128)(2,1)}, u32[]{:S(2)}, u32[]{:S(2)}) collective-permute-start(bf16[2,64,2048]{2,1,0:T(8,128)(2,1)} %maximum_select_fusion.10), channel_id=1, source_target_pairs={{0,8},{8,0},{16,24},{24,16},{1,9},{9,1},{17,25},{25,17},{2,10},{10... | collective-permute-start | bytes 1572872 | tf_op jit(solution)/shard_map/ppermute | solution.py:91
  795.7 25.0 %all-to-all-start.6 = ((bf16[8,32,1536]{2,1,0:T(8,128)(2,1)}), bf16[8,32,1536]{2,1,0:T(8,128)(2,1)S(1)}, u32[]{:S(2)}, u32[]{:S(2)}) async-start(bf16[8,32,1536]{2,1,0:T(8,128)(2,1)} %bitcast.126), calls=%async_computation.6 | async-start | bytes 1572864 | tf_op jit(solution)/shard_map/all_to_all | solution.py:95
  (140 other events, 1670.4 us)
Sparse Core Ops, SparseCore 0:
  12.0 64.8 all-gather.6
  79.5 86.0 all-gather.8
  270.6 87.6 all-gather.10
  373.8 51.8 all-gather.12
  613.9 88.3 all-gather.14
  715.1 59.9 all-gather.16
